TPU v7x, 32 devices: a whole 2x2x4 slice. The times are simulated.
32 devices in a mesh: grp: 8 (over z, core), seq: 4 (over y, x).
Axes of the slice: x: 2, y: 2, z: 4, core: 2. Of those that a mesh axis runs over, the one named last changes fastest.
Arguments:
- prompt_len: int32 [8], replicated, may hold values from 128 to 256, as said below
- resp_len: int32 [8, 4], replicated, may hold values from 1 to 128, as said below
- resp_host: int32 [8, 4], replicated, may hold values from 0 to 7, as said below
- q_prompt: bfloat16 [8, 256, 4096], P('grp', 'seq'), may hold values from -5 to 5
- k_prompt: bfloat16 [8, 256, 512], P('grp', 'seq'), may hold values from -5 to 5
- v_prompt: bfloat16 [8, 256, 512], P('grp', 'seq'), may hold values from -6 to 6
- g_prompt: bfloat16 [8, 256, 4096], P('grp', 'seq'), may hold values from -6 to 6
- q_resp: bfloat16 [8, 512, 4096], P('grp', 'seq'), may hold values from -5 to 5
- k_resp: bfloat16 [8, 512, 512], P('grp', 'seq'), may hold values from -5 to 5
- v_resp: bfloat16 [8, 512, 512], P('grp', 'seq'), may hold values from -6 to 6
- g_resp: bfloat16 [8, 512, 4096], P('grp', 'seq'), may hold values from -6 to 6
Outputs:
- out_prompt: bfloat16 [8, 256, 4096], P('grp', 'seq')
- out_resp: bfloat16 [8, 512, 4096], P('grp', 'seq')
- dq_prompt: bfloat16 [8, 256, 4096], P('grp', 'seq')
- dq_resp: bfloat16 [8, 512, 4096], P('grp', 'seq')
- dk_prompt: bfloat16 [8, 256, 512], P('grp', 'seq')
- dv_prompt: bfloat16 [8, 256, 512], P('grp', 'seq')
- dk_resp: bfloat16 [8, 512, 512], P('grp', 'seq')
- dv_resp: bfloat16 [8, 512, 512], P('grp', 'seq')
Inputs may be any that keep to these rules, and one draw needn't show every extreme that they name: `prompt_len`: one prompt in every draw has all 256 rows live. `resp_len`: every prompt has a response of 128 rows. `resp_host`: response r of prompt p runs on group 2 * (p // 2) + h // 4 at seq index h % 4, h its entry; every device hosts exactly one response, and in each pair of groups some response of each prompt runs on the other group of the pair.
All inputs are finite; a program needn't handle non-finite values.
Results may differ from a plain program's by a relative error of at most 0.012.
The roundings to bfloat16 on the way count: a program that leaves them out, or rounds other values in their place, can miss the bound.
Values may be sent and summed in bfloat16 or wider, within the bound.
No kernel may reach another device: no remote copies, remote signals or barrier semaphores. Data moves between devices by JAX's collectives and lax.ppermute only.
A program may use at most 128 MiB of HBM per device.

v0:
```python
import jax
import jax.numpy as jnp
from jax import lax
from jax.sharding import PartitionSpec as P

HQ = 32
KVH = 4
DH = 128


def swapped(block, axis, bit):
    count = lax.axis_size(axis)
    route = []
    for low in range(count):
        high = low | 1 << bit
        if high != low and high < count:
            route += [(low, high), (high, low)]
    return lax.ppermute(block, axis, route)


def attend(queries, keys_in, values_in, cotangent, allowed, live_rows):
    score_scale = DH ** (-0.5)
    row_count = queries.shape[0]
    key_count = keys_in.shape[0]
    heads_per = HQ // KVH
    masked_cot = jnp.where(live_rows[:, None], cotangent, jnp.zeros_like(cotangent))
    query_heads = queries.reshape(row_count, KVH, heads_per, DH).transpose(1, 0, 2, 3)
    cotan_heads = masked_cot.reshape(row_count, KVH, heads_per, DH).transpose(1, 0, 2, 3)
    key_heads = keys_in.reshape(key_count, KVH, DH).transpose(1, 0, 2)
    value_heads = values_in.reshape(key_count, KVH, DH).transpose(1, 0, 2)
    key_mask = allowed[None]
    live_cube = live_rows[:, None, None]

    def per_head(inputs):
        query_one, key_one, value_one, cotan_one = inputs
        scores = (
            jnp.einsum("rgd,nd->grn", query_one, key_one, preferred_element_type=jnp.float32)
            * score_scale
        )
        row_top = jnp.max(jnp.where(key_mask, scores, -jnp.inf), axis=-1, keepdims=True)
        raised = jnp.where(key_mask, jnp.exp(scores - row_top), 0.0)
        softmax = raised / jnp.sum(raised, axis=-1, keepdims=True)
        soft_half = softmax.astype(jnp.bfloat16)
        mixed = jnp.einsum("grn,nd->rgd", soft_half, value_one, preferred_element_type=jnp.float32)
        result = jnp.where(live_cube, mixed, 0.0).astype(jnp.bfloat16)
        row_delta = jnp.einsum("rgd,rgd->gr", cotan_one, result, preferred_element_type=jnp.float32)
        dprob = jnp.einsum("rgd,nd->grn", cotan_one, value_one, preferred_element_type=jnp.float32)
        dscore = (softmax * (dprob - row_delta[:, :, None]) * score_scale).astype(jnp.bfloat16)
        grad_query = jnp.einsum(
            "grn,nd->rgd", dscore, key_one, preferred_element_type=jnp.float32
        ).astype(jnp.bfloat16)
        grad_key = jnp.einsum("grn,rgd->nd", dscore, query_one, preferred_element_type=jnp.float32)
        grad_value = jnp.einsum(
            "grn,rgd->nd", soft_half, cotan_one, preferred_element_type=jnp.float32
        )
        return (result, grad_query, grad_key, grad_value)

    mixed_all, grad_q, grad_k, grad_v = lax.map(
        per_head, (query_heads, key_heads, value_heads, cotan_heads)
    )
    return (
        mixed_all.transpose(1, 0, 2, 3).reshape(row_count, HQ * DH),
        grad_q.transpose(1, 0, 2, 3).reshape(row_count, HQ * DH),
        grad_k.transpose(1, 0, 2).reshape(key_count, KVH * DH),
        grad_v.transpose(1, 0, 2).reshape(key_count, KVH * DH),
    )


def shards(
    prompt_len,
    resp_len,
    resp_host,
    q_prompt,
    k_prompt,
    v_prompt,
    g_prompt,
    q_resp,
    k_resp,
    v_resp,
    g_resp,
):
    group_id = lax.axis_index("grp")
    shard_id = lax.axis_index("seq")
    seq_count = lax.axis_size("seq")
    group_count = prompt_len.shape[0]
    prompt_rows = q_prompt.shape[1]
    slot_count = q_resp.shape[1]
    own_keys = k_prompt[0]
    own_values = v_prompt[0]
    whole_keys, whole_values = (
        lax.all_gather(own_keys, "seq", axis=0, tiled=True),
        lax.all_gather(own_values, "seq", axis=0, tiled=True),
    )
    paired = swapped(jnp.stack([whole_keys, whole_values]), "grp", 0)
    other_keys = paired[0]
    other_values = paired[1]
    prompt_total = whole_keys.shape[0]
    group_ids = jnp.arange(group_count, dtype=jnp.int32)
    own_length = jnp.sum(jnp.where(group_ids == group_id, prompt_len, 0))
    positions = shard_id * prompt_rows + jnp.arange(prompt_rows, dtype=jnp.int32)
    key_index = jnp.arange(prompt_total, dtype=jnp.int32)
    prompt_allowed = (key_index[None, :] == positions[:, None]) | (
        key_index[None, :] < positions[:, None]
    ) & (positions[:, None] < own_length)
    prompt_mixed, prompt_gq, prompt_gk, prompt_gv = attend(
        q_prompt[0], whole_keys, whole_values, g_prompt[0], prompt_allowed, positions < own_length
    )
    pair_slot = group_id % 2 * seq_count + shard_id
    match_table = (group_ids[:, None] // 2 == group_id // 2) & (resp_host == pair_slot)
    owner_id = jnp.sum(jnp.where(match_table, group_ids[:, None], 0))
    resp_length = jnp.sum(jnp.where(match_table, resp_len, 0))
    owner_length = jnp.sum(jnp.where(group_ids == owner_id, prompt_len, 0))
    is_own = owner_id == group_id
    chosen_keys = jnp.where(is_own, whole_keys, other_keys)
    chosen_values = jnp.where(is_own, whole_values, other_values)
    slot_index = jnp.arange(slot_count, dtype=jnp.int32)
    live_slots = slot_index < resp_length
    reach_prompt = live_slots[:, None] & (key_index[None, :] < owner_length)
    reach_resp = (slot_index[None, :] == slot_index[:, None]) | (
        slot_index[None, :] < slot_index[:, None]
    ) & live_slots[:, None]
    resp_allowed = jnp.concatenate([reach_prompt, reach_resp], axis=1)
    keys_all = jnp.concatenate([chosen_keys, k_resp[0]], axis=0)
    values_all = jnp.concatenate([chosen_values, v_resp[0]], axis=0)
    resp_mixed, resp_gq, resp_gk, resp_gv = attend(
        q_resp[0], keys_all, values_all, g_resp[0], resp_allowed, live_slots
    )
    chosen_gk = resp_gk[:prompt_total]
    chosen_gv = resp_gv[:prompt_total]
    own_gk = prompt_gk + jnp.where(is_own, chosen_gk, 0.0)
    own_gv = prompt_gv + jnp.where(is_own, chosen_gv, 0.0)
    other_gk = jnp.where(is_own, 0.0, chosen_gk)
    other_gv = jnp.where(is_own, 0.0, chosen_gv)
    returned = swapped(jnp.stack([other_gk, other_gv]), "grp", 0)
    total_gk, total_gv = (
        lax.psum_scatter(own_gk + returned[0], "seq", scatter_dimension=0, tiled=True),
        lax.psum_scatter(own_gv + returned[1], "seq", scatter_dimension=0, tiled=True),
    )
    return (
        prompt_mixed[None],
        resp_mixed[None],
        prompt_gq[None],
        resp_gq[None],
        total_gk.astype(jnp.bfloat16)[None],
        total_gv.astype(jnp.bfloat16)[None],
        resp_gk[prompt_total:].astype(jnp.bfloat16)[None],
        resp_gv[prompt_total:].astype(jnp.bfloat16)[None],
    )


def solution(mesh):
    placed = (
        P(),
        P(),
        P(),
        P("grp", "seq", None),
        P("grp", "seq", None),
        P("grp", "seq", None),
        P("grp", "seq", None),
        P("grp", "seq", None),
        P("grp", "seq", None),
        P("grp", "seq", None),
        P("grp", "seq", None),
    )
    return jax.shard_map(
        shards,
        mesh=mesh,
        in_specs=placed,
        out_specs=(
            P("grp", "seq", None),
            P("grp", "seq", None),
            P("grp", "seq", None),
            P("grp", "seq", None),
            P("grp", "seq", None),
            P("grp", "seq", None),
            P("grp", "seq", None),
            P("grp", "seq", None),
        ),
        check_vma=False,
    )
```

profile of v0, /device:TPU:0, one launch (start us, length us, event | category | flops | bytes accessed | tf_op | source)
XLA Modules:
  0.0 205.3 jit_solution(9247765093787074689)
XLA Ops:
  7.3 10.9 %all-gather = bf16[1,256,512]{2,1,0:T(8,128)(2,1)S(1)} all-gather(bf16[1,64,512]{2,1,0:T(8,128)(2,1)} %param.20), channel_id=2, replica_groups=mesh['grp'=8,'seq'=4] {'seq'}, dimensions={1}, use_global_device_ids=true | all-gather | bytes 327680 | tf_op jit(solution)/shard_map/all_gather | solution.py:92
  18.9 8.7 %all-gather.1 = bf16[1,256,512]{2,1,0:T(8,128)(2,1)S(1)} all-gather(bf16[1,64,512]{2,1,0:T(8,128)(2,1)} %param.19), channel_id=3, replica_groups=mesh['grp'=8,'seq'=4] {'seq'}, dimensions={1}, use_global_device_ids=true | all-gather | bytes 327680 | tf_op jit(solution)/shard_map/all_gather | solution.py:91
  27.8 1.8 pad_maximum_fusion.1
  31.9 1.2 iota_compare_fusion.5
  33.8 1.3 fusion.98
  35.1 1.2 iota_compare_fusion.4
  36.3 2.3 %copy.79 = bf16[1,128,4096]{1,2,0:T(8,128)(2,1)} copy(bf16[1,128,4096]{2,1,0:T(8,128)(2,1)} %param.22) | data formatting | bytes 2097152 | tf_op args[7]
  40.5 1.5 select_bitcast_fusion.1
  42.0 42.7 %while.34 = (s32[]{:T(128)}, bf16[4,64,8,128]{3,1,2,0:T(8,128)(2,1)}, bf16[4,64,8,128]{3,1,2,0:T(8,128)(2,1)}, f32[4,256,128]{2,1,0:T(8,128)}, f32[4,256,128]{2,...) while((s32[]{:T(128)}, ...), condition=%wide.region_4.5_spmd.clone, body=%wide.region_1.4_spmd.clone.sunk | while | flops 204473728 | bytes 7339605 | solution.py:58
  44.7 2.5 %bitcast_dynamic-update-slice_fusion.4 = (bf16[4,64,8,128]{3,1,2,0:T(8,128)(2,1)}, bf16[128,8,64]{0,2,1:T(8,128)(2,1)S(1)}) fusion(bf16[4,64,8,128]{3,1,2,0:T(8,128)(2,1)} %get-tuple-element.495, s32[]{:T(128)} %get-tuple-element.494, f32[8,64]{1,0:T(8,128)S(1)} %get-tuple-element.460, f32[8,64,256]{2,1,0:T(8,128)S(1)} %fusion.150, ...), kind=kOutput, calls=%fused_computation.32.clone.1 | convolution fusion | flops 34341632 | bytes 1414656 | tf_op jit(solution)/shard_map/while/body/eval_jaxpr/grn,nd->rgd/dot_general | solution.py:44
  49.4 2.4 %fusion.157 = f32[4,256,128]{2,1,0:T(8,128)} fusion(f32[4,256,128]{2,1,0:T(8,128)} %get-tuple-element.498, s32[]{:T(128)} %get-tuple-element.494, bf16[1,64,8,128]{3,2,0,1:T(8,128)(2,1)S(1)} %get-tuple-element.463, f32[8,64]{1,0:T(8,128)} %copy-done.11, f32[8,64,256]{2,1,0:T(8,128)S(1)} %fusion.150, pred[64,256]{1,0:T(8,128)(4,1)S(1)} %fusion.151), kind=kOutput, calls=%fused_computation.18.clone.1 | convolution fusion | flops 34210560 | bytes 1348096 | tf_op jit(solution)/shard_map/while/body/eval_jaxpr/grn,rgd->nd/dot_general | solution.py:53
  55.4 2.5 %bitcast_dynamic-update-slice_fusion.4 = (bf16[4,64,8,128]{3,1,2,0:T(8,128)(2,1)}, bf16[128,8,64]{0,2,1:T(8,128)(2,1)S(1)}) fusion(bf16[4,64,8,128]{3,1,2,0:T(8,128)(2,1)} %get-tuple-element.495, s32[]{:T(128)} %get-tuple-element.494, f32[8,64]{1,0:T(8,128)S(1)} %get-tuple-element.460, f32[8,64,256]{2,1,0:T(8,128)S(1)} %fusion.150, ...), kind=kOutput, calls=%fused_computation.32.clone.1 | convolution fusion | flops 34341632 | bytes 1414656 | tf_op jit(solution)/shard_map/while/body/eval_jaxpr/grn,nd->rgd/dot_general | solution.py:44
  60.1 2.4 %fusion.157 = f32[4,256,128]{2,1,0:T(8,128)} fusion(f32[4,256,128]{2,1,0:T(8,128)} %get-tuple-element.498, s32[]{:T(128)} %get-tuple-element.494, bf16[1,64,8,128]{3,2,0,1:T(8,128)(2,1)S(1)} %get-tuple-element.463, f32[8,64]{1,0:T(8,128)} %copy-done.11, f32[8,64,256]{2,1,0:T(8,128)S(1)} %fusion.150, pred[64,256]{1,0:T(8,128)(4,1)S(1)} %fusion.151), kind=kOutput, calls=%fused_computation.18.clone.1 | convolution fusion | flops 34210560 | bytes 1348096 | tf_op jit(solution)/shard_map/while/body/eval_jaxpr/grn,rgd->nd/dot_general | solution.py:53
  66.0 2.5 %bitcast_dynamic-update-slice_fusion.4 = (bf16[4,64,8,128]{3,1,2,0:T(8,128)(2,1)}, bf16[128,8,64]{0,2,1:T(8,128)(2,1)S(1)}) fusion(bf16[4,64,8,128]{3,1,2,0:T(8,128)(2,1)} %get-tuple-element.495, s32[]{:T(128)} %get-tuple-element.494, f32[8,64]{1,0:T(8,128)S(1)} %get-tuple-element.460, f32[8,64,256]{2,1,0:T(8,128)S(1)} %fusion.150, ...), kind=kOutput, calls=%fused_computation.32.clone.1 | convolution fusion | flops 34341632 | bytes 1414656 | tf_op jit(solution)/shard_map/while/body/eval_jaxpr/grn,nd->rgd/dot_general | solution.py:44
  70.7 2.4 %fusion.157 = f32[4,256,128]{2,1,0:T(8,128)} fusion(f32[4,256,128]{2,1,0:T(8,128)} %get-tuple-element.498, s32[]{:T(128)} %get-tuple-element.494, bf16[1,64,8,128]{3,2,0,1:T(8,128)(2,1)S(1)} %get-tuple-element.463, f32[8,64]{1,0:T(8,128)} %copy-done.11, f32[8,64,256]{2,1,0:T(8,128)S(1)} %fusion.150, pred[64,256]{1,0:T(8,128)(4,1)S(1)} %fusion.151), kind=kOutput, calls=%fused_computation.18.clone.1 | convolution fusion | flops 34210560 | bytes 1348096 | tf_op jit(solution)/shard_map/while/body/eval_jaxpr/grn,rgd->nd/dot_general | solution.py:53
  76.7 2.5 %bitcast_dynamic-update-slice_fusion.4 = (bf16[4,64,8,128]{3,1,2,0:T(8,128)(2,1)}, bf16[128,8,64]{0,2,1:T(8,128)(2,1)S(1)}) fusion(bf16[4,64,8,128]{3,1,2,0:T(8,128)(2,1)} %get-tuple-element.495, s32[]{:T(128)} %get-tuple-element.494, f32[8,64]{1,0:T(8,128)S(1)} %get-tuple-element.460, f32[8,64,256]{2,1,0:T(8,128)S(1)} %fusion.150, ...), kind=kOutput, calls=%fused_computation.32.clone.1 | convolution fusion | flops 34341632 | bytes 1414656 | tf_op jit(solution)/shard_map/while/body/eval_jaxpr/grn,nd->rgd/dot_general | solution.py:44
  81.4 2.4 %fusion.157 = f32[4,256,128]{2,1,0:T(8,128)} fusion(f32[4,256,128]{2,1,0:T(8,128)} %get-tuple-element.498, s32[]{:T(128)} %get-tuple-element.494, bf16[1,64,8,128]{3,2,0,1:T(8,128)(2,1)S(1)} %get-tuple-element.463, f32[8,64]{1,0:T(8,128)} %copy-done.11, f32[8,64,256]{2,1,0:T(8,128)S(1)} %fusion.150, pred[64,256]{1,0:T(8,128)(4,1)S(1)} %fusion.151), kind=kOutput, calls=%fused_computation.18.clone.1 | convolution fusion | flops 34210560 | bytes 1348096 | tf_op jit(solution)/shard_map/while/body/eval_jaxpr/grn,rgd->nd/dot_general | solution.py:53
  86.9 1.1 slice_select_fusion.2
  89.6 47.3 %while.35 = (s32[]{:T(128)}, bf16[4,128,8,128]{1,3,2,0:T(8,128)(2,1)}, bf16[4,128,8,128]{1,3,2,0:T(8,128)(2,1)}, f32[4,384,128]{2,1,0:T(8,128)}, f32[4,384,128]{...) while((s32[]{:T(128)}, ...), condition=%wide.region_11.12_spmd.clone, body=%wide.region_8.11_spmd.clone.sunk | while | flops 610401792 | bytes 26556852 | solution.py:58
  89.6 1.7 convolution_multiply_fusion.3
  92.5 1.9 bitcast_dynamic-update-slice_fusion.5
  94.9 1.4 fusion.169
  96.4 2.0 fusion.170
  98.4 2.0 fusion.171
  101.4 1.7 convolution_multiply_fusion.3
  104.3 1.9 bitcast_dynamic-update-slice_fusion.5
  106.8 1.4 fusion.169
  108.2 2.0 fusion.170
  110.2 2.0 fusion.171
  113.2 1.7 convolution_multiply_fusion.3
  116.1 1.9 bitcast_dynamic-update-slice_fusion.5
  118.6 1.4 fusion.169
  120.0 2.0 fusion.170
  122.0 2.0 fusion.171
  125.1 1.7 convolution_multiply_fusion.3
  127.9 1.9 bitcast_dynamic-update-slice_fusion.5
  130.4 1.4 fusion.169
  131.9 2.0 fusion.170
  133.9 2.0 fusion.171
  136.9 1.7 fusion.92
  140.3 2.3 %collective-permute-done.1 = f32[2,256,512]{2,1,0:T(8,128)S(1)} collective-permute-done((f32[2,256,512]{2,1,0:T(8,128)S(1)}, f32[2,256,512]{2,1,0:T(8,128)S(1)}, u32[]{:S(2)}, u32[]{:S(2)}) %collective-permute-start.1) | collective-permute-done | bytes 1048608 | tf_op jit(solution)/shard_map/ppermute | solution.py:18
  142.6 1.1 bitcast_add_fusion
  149.3 2.3 %copy.109 = bf16[1,128,4096]{2,1,0:T(8,128)(2,1)} copy(bf16[1,128,4096]{1,2,0:T(8,128)(2,1)} %bitcast.23) | data formatting | bytes 2097152 | tf_op jit(solution)/shard_map/broadcast_in_dim;reshape | solution.py:141
  151.5 1.3 copy.110
  154.5 14.6 %reduce-scatter.5.cloned.1.call-done = f32[64,512]{1,0:T(8,128)} async-done(((f32[256,512]{1,0:T(8,128)}), f32[64,512]{1,0:T(8,128)}) %reduce-scatter.5.cloned.1.call-update) | async-done | bytes 131088 | tf_op jit(solution)/shard_map/reduce_scatter | solution.py:137
  169.1 1.5 convert_bitcast_fusion
  170.6 26.3 %reduce-scatter.3.cloned.1.call-done = f32[64,512]{1,0:T(8,128)} async-done(((f32[256,512]{1,0:T(8,128)}), f32[64,512]{1,0:T(8,128)}) %reduce-scatter.3.cloned.1.call-update) | async-done | bytes 131088 | tf_op jit(solution)/shard_map/reduce_scatter | solution.py:136
  196.9 1.5 convert_bitcast_fusion.1
  (173 shorter events, 51.5 us)
Async XLA Ops:
  7.2 22.5 %copy-start.14 = (s32[8,4]{0,1:T(4,128)S(1)}, s32[8,4]{0,1:T(4,128)}, u32[]{:S(2)}) copy-start(s32[8,4]{0,1:T(4,128)} %param.16) | copy-start | bytes 388
  7.2 22.5 %copy-start.15 = (s32[8,4]{0,1:T(4,128)S(1)}, s32[8,4]{0,1:T(4,128)}, u32[]{:S(2)}) copy-start(s32[8,4]{0,1:T(4,128)} %param.17) | copy-start | bytes 388
  7.2 23.8 %copy-start.9 = (bf16[1,128,512]{2,1,0:T(8,128)(2,1)S(1)}, bf16[1,128,512]{2,1,0:T(8,128)(2,1)}, u32[]{:S(2)}) copy-start(bf16[1,128,512]{2,1,0:T(8,128)(2,1)} %param.24) | copy-start | bytes 393220
  7.2 24.6 %copy-start.10 = (bf16[1,128,512]{2,1,0:T(8,128)(2,1)S(1)}, bf16[1,128,512]{2,1,0:T(8,128)(2,1)}, u32[]{:S(2)}) copy-start(bf16[1,128,512]{2,1,0:T(8,128)(2,1)} %param.23) | copy-start | bytes 393220
  7.2 161.9 %reduce-scatter.5.cloned.1.call-start = ((), (), s32[]{:S(2)}) async-start(), calls=%async_computation.3 | async-start | bytes 655360 | tf_op jit(solution)/shard_map/reduce_scatter | solution.py:137
  18.1 15.0 %copy-start.2 = (bf16[1,128,4096]{2,1,0:T(8,128)(2,1)S(1)}, bf16[1,128,4096]{2,1,0:T(8,128)(2,1)}, u32[]{:S(2)}) copy-start(bf16[1,128,4096]{2,1,0:T(8,128)(2,1)} %param.25) | copy-start | bytes 3145732
  29.6 4.2 %copy-start.16 = (s32[8]{0:T(128)S(1)}, s32[8]{0:T(128)}, u32[]{:S(2)}) copy-start(s32[8]{0:T(128)} %param.15) | copy-start | bytes 100
  29.6 57.4 %collective-permute-start = (bf16[2,256,512]{1,2,0:T(8,128)(2,1)}, bf16[2,256,512]{1,2,0:T(8,128)(2,1)}, u32[]{:S(2)}, u32[]{:S(2)}) collective-permute-start(bf16[2,256,512]{1,2,0:T(8,128)(2,1)} %pad_maximum_fusion.1), channel_id=1, source_target_pairs={{0,4},{4,0},{8,12},{12,8},{16,20},{20,16},{24,28},{28,24},{1,5},{5... | collective-permute-start | bytes 1572872 | tf_op jit(solution)/shard_map/ppermute | solution.py:18
  33.8 6.5 %copy-start.4 = (bf16[1,64,4096]{2,1,0:T(8,128)(2,1)S(1)}, bf16[1,64,4096]{2,1,0:T(8,128)(2,1)}, u32[]{:S(2)}) copy-start(bf16[1,64,4096]{2,1,0:T(8,128)(2,1)} %param.21) | copy-start | bytes 1572868
  36.3 4.1 %copy-start.5 = (bf16[1,64,4096]{2,1,0:T(8,128)(2,1)S(1)}, bf16[1,64,4096]{2,1,0:T(8,128)(2,1)}, u32[]{:S(2)}) copy-start(bf16[1,64,4096]{2,1,0:T(8,128)(2,1)} %param.18) | copy-start | bytes 1572868
  40.4 1.7 copy-start.12
  44.1 3.3 %copy-start.11 = (f32[8,64]{1,0:T(8,128)}, f32[8,64]{1,0:T(8,128)S(1)}, u32[]{:S(2)}) copy-start(f32[8,64]{1,0:T(8,128)S(1)} %get-tuple-element.460) | copy-start | bytes 6148 | tf_op jit(solution)/shard_map/while
  49.4 3.2 %copy-start.13 = (s32[64]{0:T(128)S(1)}, s32[64]{0:T(128)}, u32[]{:S(2)}) copy-start(s32[64]{0:T(128)} %get-tuple-element.583) | copy-start | bytes 772 | tf_op jit(solution)/shard_map/while
  54.8 3.3 %copy-start.11 = (f32[8,64]{1,0:T(8,128)}, f32[8,64]{1,0:T(8,128)S(1)}, u32[]{:S(2)}) copy-start(f32[8,64]{1,0:T(8,128)S(1)} %get-tuple-element.460) | copy-start | bytes 6148 | tf_op jit(solution)/shard_map/while
  60.1 3.2 %copy-start.13 = (s32[64]{0:T(128)S(1)}, s32[64]{0:T(128)}, u32[]{:S(2)}) copy-start(s32[64]{0:T(128)} %get-tuple-element.583) | copy-start | bytes 772 | tf_op jit(solution)/shard_map/while
  65.4 3.3 %copy-start.11 = (f32[8,64]{1,0:T(8,128)}, f32[8,64]{1,0:T(8,128)S(1)}, u32[]{:S(2)}) copy-start(f32[8,64]{1,0:T(8,128)S(1)} %get-tuple-element.460) | copy-start | bytes 6148 | tf_op jit(solution)/shard_map/while
  70.7 3.3 %copy-start.13 = (s32[64]{0:T(128)S(1)}, s32[64]{0:T(128)}, u32[]{:S(2)}) copy-start(s32[64]{0:T(128)} %get-tuple-element.583) | copy-start | bytes 772 | tf_op jit(solution)/shard_map/while
  76.1 3.3 %copy-start.11 = (f32[8,64]{1,0:T(8,128)}, f32[8,64]{1,0:T(8,128)S(1)}, u32[]{:S(2)}) copy-start(f32[8,64]{1,0:T(8,128)S(1)} %get-tuple-element.460) | copy-start | bytes 6148 | tf_op jit(solution)/shard_map/while
  81.4 3.3 %copy-start.13 = (s32[64]{0:T(128)S(1)}, s32[64]{0:T(128)}, u32[]{:S(2)}) copy-start(s32[64]{0:T(128)} %get-tuple-element.583) | copy-start | bytes 772 | tf_op jit(solution)/shard_map/while
  86.2 1.9 copy-start.8
  89.6 4.8 %copy-start = (bf16[4,128,8,128]{1,3,2,0:T(8,128)(2,1)}, bf16[4,128,8,128]{1,3,2,0:T(8,128)(2,1)S(1)}, u32[]{:S(2)}) copy-start(bf16[4,128,8,128]{1,3,2,0:T(8,128)(2,1)S(1)} %get-tuple-element.555) | copy-start | bytes 3145732 | tf_op jit(solution)/shard_map/while
  96.4 4.0 %copy-start.1 = (bf16[4,128,8,128]{1,3,2,0:T(8,128)(2,1)S(1)}, bf16[4,128,8,128]{1,3,2,0:T(8,128)(2,1)}, u32[]{:S(2)}) copy-start(bf16[4,128,8,128]{1,3,2,0:T(8,128)(2,1)} %copy-done) | copy-start | bytes 3145732 | tf_op jit(solution)/shard_map/while
  101.4 4.8 %copy-start = (bf16[4,128,8,128]{1,3,2,0:T(8,128)(2,1)}, bf16[4,128,8,128]{1,3,2,0:T(8,128)(2,1)S(1)}, u32[]{:S(2)}) copy-start(bf16[4,128,8,128]{1,3,2,0:T(8,128)(2,1)S(1)} %get-tuple-element.555) | copy-start | bytes 3145732 | tf_op jit(solution)/shard_map/while
  108.2 4.0 %copy-start.1 = (bf16[4,128,8,128]{1,3,2,0:T(8,128)(2,1)S(1)}, bf16[4,128,8,128]{1,3,2,0:T(8,128)(2,1)}, u32[]{:S(2)}) copy-start(bf16[4,128,8,128]{1,3,2,0:T(8,128)(2,1)} %copy-done) | copy-start | bytes 3145732 | tf_op jit(solution)/shard_map/while
  113.2 4.8 %copy-start = (bf16[4,128,8,128]{1,3,2,0:T(8,128)(2,1)}, bf16[4,128,8,128]{1,3,2,0:T(8,128)(2,1)S(1)}, u32[]{:S(2)}) copy-start(bf16[4,128,8,128]{1,3,2,0:T(8,128)(2,1)S(1)} %get-tuple-element.555) | copy-start | bytes 3145732 | tf_op jit(solution)/shard_map/while
  120.0 4.0 %copy-start.1 = (bf16[4,128,8,128]{1,3,2,0:T(8,128)(2,1)S(1)}, bf16[4,128,8,128]{1,3,2,0:T(8,128)(2,1)}, u32[]{:S(2)}) copy-start(bf16[4,128,8,128]{1,3,2,0:T(8,128)(2,1)} %copy-done) | copy-start | bytes 3145732 | tf_op jit(solution)/shard_map/while
  125.1 4.8 %copy-start = (bf16[4,128,8,128]{1,3,2,0:T(8,128)(2,1)}, bf16[4,128,8,128]{1,3,2,0:T(8,128)(2,1)S(1)}, u32[]{:S(2)}) copy-start(bf16[4,128,8,128]{1,3,2,0:T(8,128)(2,1)S(1)} %get-tuple-element.555) | copy-start | bytes 3145732 | tf_op jit(solution)/shard_map/while
  131.8 4.0 %copy-start.1 = (bf16[4,128,8,128]{1,3,2,0:T(8,128)(2,1)S(1)}, bf16[4,128,8,128]{1,3,2,0:T(8,128)(2,1)}, u32[]{:S(2)}) copy-start(bf16[4,128,8,128]{1,3,2,0:T(8,128)(2,1)} %copy-done) | copy-start | bytes 3145732 | tf_op jit(solution)/shard_map/while
  139.8 2.8 %collective-permute-start.1 = (f32[2,256,512]{2,1,0:T(8,128)S(1)}, f32[2,256,512]{2,1,0:T(8,128)S(1)}, u32[]{:S(2)}, u32[]{:S(2)}) collective-permute-start(f32[2,256,512]{2,1,0:T(8,128)S(1)} %pad_maximum_fusion), channel_id=1, source_target_pairs={{0,4},{4,0},{8,12},{12,8},{16,20},{20,16},{24,28},{28,24},{1,5},{5... | collective-permute-start | bytes 3145736 | tf_op jit(solution)/shard_map/ppermute | solution.py:18
  142.6 1.9 copy-start.6
  143.7 2.2 %copy-start.7 = (bf16[4,64,8,128]{3,1,2,0:T(8,128)(2,1)S(1)}, bf16[4,64,8,128]{3,1,2,0:T(8,128)(2,1)}, u32[]{:S(2)}) copy-start(bf16[4,64,8,128]{3,1,2,0:T(8,128)(2,1)} %get-tuple-element.571) | copy-start | bytes 1572868
  143.7 53.2 %reduce-scatter.3.cloned.1.call-start = ((), (), s32[]{:S(2)}) async-start(), calls=%async_computation.2 | async-start | bytes 655360 | tf_op jit(solution)/shard_map/reduce_scatter | solution.py:136
  147.2 4.3 %copy-start.3 = (bf16[4,128,8,128]{1,3,2,0:T(8,128)(2,1)S(1)}, bf16[4,128,8,128]{1,3,2,0:T(8,128)(2,1)}, u32[]{:S(2)}) copy-start(bf16[4,128,8,128]{1,3,2,0:T(8,128)(2,1)} %get-tuple-element.131) | copy-start | bytes 3145732
Sparse Core Ops, SparseCore 0:
  143.9 25.1 reduce-scatter.4
  172.1 24.7 reduce-scatter.2
where the time goes:
time: 207 us; the launch traced here: 205 us
  matrix products  72.3 us (35%)
  waiting for transfers between devices  43.9 us (21%)
  other arithmetic  31.9 us (15%)
  local copies, waits for them, and re-layouts  21.5 us (10%)
  blocking collectives  19.5 us (9%)
  between operations  15 us (7%)
    reduce_scatter x1, waiting for transfers between devices, shards(): lax.psum_scatter(own_gk + returned[0], 'seq', scatter_dimension=0, tiled=...  26.3 us
    dot_general x8, matrix products, per_head(): jnp.einsum('grn,nd->rgd', soft_half, value_one, preferred_element_type=jn...  17.8 us
    reduce_scatter x1, waiting for transfers between devices, shards(): lax.psum_scatter(own_gv + returned[1], 'seq', scatter_dimension=0, tiled=...  14.6 us
    dot_general x8, matrix products, per_head(): jnp.einsum('grn,rgd->nd', soft_half, cotan_one, preferred_element_type=jn...  13.7 us
    dot_general x8, matrix products, per_head(): jnp.einsum('grn,rgd->nd', dscore, query_one, preferred_element_type=jnp.f...  11.7 us
    dot_general x8, matrix products, per_head(): jnp.einsum('grn,nd->rgd', dscore, key_one, preferred_element_type=jnp.flo...  11.5 us
    all_gather x1, blocking collectives, shards(): lax.all_gather(own_values, 'seq', axis=0, tiled=True)  10.9 us
    dot_general x8, matrix products, per_head(): jnp.einsum('rgd,nd->grn', cotan_one, value_one, preferred_element_type=jn...  10.1 us
  transfers between devices with their start and end apart: 4, of which 3 were waited for; matrix products, arithmetic and copies ran while one was open for 33% of the time, Pallas kernels for 0%

commit v1 on v0

v1 whole, which is shorter than its diff:
```python
import jax
import jax.numpy as jnp
from jax import lax
from jax.experimental import pallas as pl
from jax.experimental.pallas import tpu as pltpu
from jax.sharding import PartitionSpec as P

HQ = 32
KVH = 4
DH = 128
PER = HQ // KVH
SCALE = DH ** (-0.5)
LOG2E = 1.4426950408889634
BLOCKED = -1e30
NN = (((1,), (0,)), ((), ()))
NT = (((1,), (1,)), ((), ()))
TN = (((0,), (0,)), ((), ()))


def dot(a, b, dims=NN):
    return lax.dot_general(a, b, dims, preferred_element_type=jnp.float32)


def swapped(block, axis, distance):
    count = lax.axis_size(axis)
    return lax.ppermute(block, axis, [(i, i ^ distance) for i in range(count)])


def tall(block):
    return jnp.concatenate([block[:, h * DH : (h + 1) * DH] for h in range(PER)], axis=0)


def wide(block):
    rows = block.shape[0] // PER
    return jnp.concatenate([block[h * rows : (h + 1) * rows] for h in range(PER)], axis=1)


def attend(queries, cotangent, keys, values, bias, live):
    rows, count = bias.shape
    scores = (dot(queries, keys, NT) * (SCALE * LOG2E)).reshape(PER, rows, count) + bias[None]
    top = jnp.max(scores, axis=-1, keepdims=True)
    raised = jnp.exp2(scores - top)
    total = jnp.sum(raised, axis=-1, keepdims=True)
    probs = (raised * (1.0 / total)).reshape(PER * rows, count)
    half = probs.astype(jnp.bfloat16)
    mixed = dot(half, values).reshape(PER, rows, DH)
    result = jnp.where(live[None], mixed, 0.0).astype(jnp.bfloat16).reshape(PER * rows, DH)
    delta = jnp.sum(
        cotangent.astype(jnp.float32) * result.astype(jnp.float32), axis=-1, keepdims=True
    )
    dprob = dot(cotangent, values, NT)
    dscore = (probs * (dprob - delta) * SCALE).astype(jnp.bfloat16)
    grad_q = dot(dscore, keys).astype(jnp.bfloat16)
    grad_k = dot(dscore, queries, TN)
    grad_v = dot(half, cotangent, TN)
    return result, grad_q, grad_k, grad_v


def kernel(count, *refs):
    facts, q_p, g_p, q_r, g_r, k_r, v_r = refs[:7]
    own_k = refs[7 : 7 + count]
    own_v = refs[7 + count : 7 + 2 * count]
    pair_k = refs[7 + 2 * count : 7 + 3 * count]
    pair_v = refs[7 + 3 * count : 7 + 4 * count]
    out_p, dq_p, out_r, dq_r, dk_r, dv_r, far, *near = refs[7 + 4 * count :]
    own_length, resp_length, owner_length, shard, is_own = [facts[i] for i in range(5)]
    is_own = is_own == 1
    piece = own_k[0].shape[0]
    rows = q_p.shape[0]
    slots = q_r.shape[0]
    span = count * piece
    column = lax.broadcasted_iota(jnp.int32, (1, span), 1)
    place = ((column // piece) ^ shard) * piece + column % piece
    position = lax.broadcasted_iota(jnp.int32, (rows, 1), 0) + shard * rows
    live = position < own_length
    allowed = (place == position) | ((place < position) & live)
    bias = jnp.where(allowed, 0.0, BLOCKED)
    keys = jnp.concatenate([ref[...] for ref in own_k], axis=0)
    values = jnp.concatenate([ref[...] for ref in own_v], axis=0)
    queries = tall(q_p[...])
    cotangent = tall(jnp.where(live, g_p[...], 0))
    result, grad_q, own_gk, own_gv = attend(queries, cotangent, keys, values, bias, live)
    out_p[...] = wide(result)
    dq_p[...] = wide(grad_q)

    slot = lax.broadcasted_iota(jnp.int32, (slots, 1), 0)
    live = slot < resp_length
    other = lax.broadcasted_iota(jnp.int32, (1, slots), 1)
    bias = jnp.concatenate(
        [
            jnp.where(live & (place < owner_length), 0.0, BLOCKED),
            jnp.where((other == slot) | ((other < slot) & live), 0.0, BLOCKED),
        ],
        axis=1,
    )
    keys = jnp.concatenate(
        [jnp.where(is_own, a[...], b[...]) for a, b in zip(own_k, pair_k)] + [k_r[...]], axis=0
    )
    values = jnp.concatenate(
        [jnp.where(is_own, a[...], b[...]) for a, b in zip(own_v, pair_v)] + [v_r[...]], axis=0
    )
    queries = tall(q_r[...])
    cotangent = tall(jnp.where(live, g_r[...], 0))
    result, grad_q, grad_k, grad_v = attend(queries, cotangent, keys, values, bias, live)
    out_r[...] = wide(result)
    dq_r[...] = wide(grad_q)
    dk_r[...] = grad_k[span:].astype(jnp.bfloat16)
    dv_r[...] = grad_v[span:].astype(jnp.bfloat16)
    for d in range(count):
        part = slice(d * piece, (d + 1) * piece)
        near[d][0] = own_gk[part] + jnp.where(is_own, grad_k[part], 0.0)
        near[d][1] = own_gv[part] + jnp.where(is_own, grad_v[part], 0.0)
        far[d, 0] = jnp.where(is_own, 0.0, grad_k[part]).astype(jnp.bfloat16)
        far[d, 1] = jnp.where(is_own, 0.0, grad_v[part]).astype(jnp.bfloat16)


def shards(
    prompt_len,
    resp_len,
    resp_host,
    q_prompt,
    k_prompt,
    v_prompt,
    g_prompt,
    q_resp,
    k_resp,
    v_resp,
    g_resp,
):
    group_id = lax.axis_index("grp")
    shard_id = lax.axis_index("seq")
    count = lax.axis_size("seq")
    rows = q_prompt.shape[1]
    slots = q_resp.shape[1]
    piece = k_prompt.shape[1]
    width = KVH * DH

    mine = jnp.concatenate([k_prompt[0], v_prompt[0]], axis=1)
    own = [mine] + [swapped(mine, "seq", d) for d in range(1, count)]
    pair = [swapped(part, "grp", 1) for part in own]

    group_ids = jnp.arange(prompt_len.shape[0], dtype=jnp.int32)
    own_length = jnp.sum(jnp.where(group_ids == group_id, prompt_len, 0))
    pair_slot = group_id % 2 * count + shard_id
    match = (group_ids[:, None] // 2 == group_id // 2) & (resp_host == pair_slot)
    owner = jnp.sum(jnp.where(match, group_ids[:, None], 0))
    resp_length = jnp.sum(jnp.where(match, resp_len, 0))
    owner_length = jnp.sum(jnp.where(group_ids == owner, prompt_len, 0))
    is_own = (owner == group_id).astype(jnp.int32)
    facts = jnp.stack([own_length, resp_length, owner_length, shard_id, is_own]).astype(jnp.int32)

    def block(height, lanes, offset=0):
        return pl.BlockSpec((height, lanes), lambda c: (0, c + offset))

    wide_p, wide_r = block(rows, PER * DH), block(slots, PER * DH)
    bf16 = jnp.bfloat16
    outs = pl.pallas_call(
        lambda *refs: kernel(count, *refs),
        grid=(KVH,),
        in_specs=[pl.BlockSpec(memory_space=pltpu.SMEM), wide_p, wide_p, wide_r, wide_r]
        + [block(slots, DH)] * 2
        + [block(piece, DH)] * count
        + [block(piece, DH, KVH)] * count
        + [block(piece, DH)] * count
        + [block(piece, DH, KVH)] * count,
        out_specs=[wide_p, wide_p, wide_r, wide_r]
        + [block(slots, DH)] * 2
        + [pl.BlockSpec((count, 2, piece, DH), lambda c: (0, 0, 0, c))]
        + [pl.BlockSpec((2, piece, DH), lambda c: (0, 0, c))] * count,
        out_shape=[jax.ShapeDtypeStruct((rows, HQ * DH), bf16)] * 2
        + [jax.ShapeDtypeStruct((slots, HQ * DH), bf16)] * 2
        + [jax.ShapeDtypeStruct((slots, width), bf16)] * 2
        + [jax.ShapeDtypeStruct((count, 2, piece, width), bf16)]
        + [jax.ShapeDtypeStruct((2, piece, width), jnp.float32)] * count,
        compiler_params=pltpu.CompilerParams(vmem_limit_bytes=56 * 2**20),
        name="tree_attention",
    )(facts, q_prompt[0], g_prompt[0], q_resp[0], g_resp[0], k_resp[0], v_resp[0], *own, *own, *pair, *pair)
    out_p, dq_p, out_r, dq_r, dk_r, dv_r, far, *near = outs
    back = swapped(far, "grp", 1)
    total = near[0] + back[0].astype(jnp.float32)
    for d in range(1, count):
        part = (near[d] + back[d].astype(jnp.float32)).astype(bf16)
        total = total + swapped(part, "seq", d).astype(jnp.float32)
    total = total.astype(bf16)
    return (
        out_p[None],
        out_r[None],
        dq_p[None],
        dq_r[None],
        total[0][None],
        total[1][None],
        dk_r[None],
        dv_r[None],
    )


def solution(mesh):
    split = P("grp", "seq", None)
    return jax.shard_map(
        shards,
        mesh=mesh,
        in_specs=(P(), P(), P()) + (split,) * 8,
        out_specs=(split,) * 8,
        check_vma=False,
    )
```

time: 207 us -> 47.9 us (0.23)
  matrix products: 72.3 us -> 0 us
  waiting for transfers between devices: 43.9 us -> 15.2 us
  other arithmetic: 31.9 us -> 4.16 us
  blocking collectives: 19.5 us -> 0 us
  local copies, waits for them, and re-layouts: 21.5 us -> 4.6 us
  between operations: 15 us -> 1.41 us
  Pallas kernels: 0 us -> 13.5 us
  starting transfers between devices: 0.6 us -> 8.74 us
    dot_general x48 -> x0, matrix products: 72.3 us -> none  [the longest x8 17.8 us: per_head(): jnp.einsum('grn,nd->rgd', soft_half, value_one, preferred_element_type=jn...]
    reduce_scatter x2 -> x0, waiting for transfers between devices: 40.9 us -> none  [the longest x1 26.3 us: shards(): lax.psum_scatter(own_gk + returned[0], 'seq', scatter_dimension=0, tiled=...]
    all_gather x2 -> x0, blocking collectives: 19.5 us -> none  [the longest x1 10.9 us: shards(): lax.all_gather(own_values, 'seq', axis=0, tiled=True)]
    pallas_call x0 -> x1, Pallas kernels: none -> 13.5 us  [shards(): pl.pallas_call(lambda *refs: kernel(count, *refs), grid=(KVH,), in_specs=...]
    ppermute x2 -> x11, waiting for transfers between devices: 2.29 us -> 15.2 us  [swapped(): return lax.ppermute(block, axis, [(i, i ^ distance) for i in range(count)])]
    broadcast_in_dim x15 -> x0, other arithmetic: 10.7 us -> none  [the longest x8 4.88 us: per_head(): result = jnp.where(live_cube, mixed, 0.0).astype(jnp.bfloat16)]
    ppermute x2 -> x11, starting transfers between devices: 0.52 us -> 8.74 us  [swapped(): return lax.ppermute(block, axis, [(i, i ^ distance) for i in range(count)])]
    dynamic_slice x12 -> x0, local copies, waits for them, and re-layouts: 4.5 us -> none  [attend(): lax.map(per_head, (query_heads, key_heads, value_heads, cotan_heads))]
  transfers between devices with their start and end apart: 4 -> 11, of which waited for: 3 -> 7; matrix products, arithmetic and copies ran while one was open for 33% -> 9% of each run, Pallas kernels for 0% -> 0%
where the time goes in v1:
time: 47.9 us; the launch traced here: 47.6 us
  waiting for transfers between devices  15.2 us (32%)
  Pallas kernels  13.5 us (28%)
  starting transfers between devices  8.74 us (18%)
  local copies, waits for them, and re-layouts  4.6 us (10%)
  other arithmetic  4.16 us (9%)
  between operations  1.41 us (3%)
    ppermute x11, waiting for transfers between devices, swapped(): return lax.ppermute(block, axis, [(i, i ^ distance) for i in range(count)])  15.2 us
    pallas_call x1, Pallas kernels, shards(): pl.pallas_call(lambda *refs: kernel(count, *refs), grid=(KVH,), in_specs=...  13.5 us
    ppermute x11, starting transfers between devices, swapped(): return lax.ppermute(block, axis, [(i, i ^ distance) for i in range(count)])  8.74 us
    another operation x1, local copies, waits for them, and re-layouts, shards(): jnp.stack([own_length, resp_length, owner_length, shard_id, is_own])  2.54 us
    unnamed x24, local copies, waits for them, and re-layouts  1.4 us
    reduce_sum x1, other arithmetic, shards(): owner_length = jnp.sum(jnp.where(group_ids == owner, prompt_len, 0))  1.28 us
    convert_element_type x1, other arithmetic, shards(): part = (near[d] + back[d].astype(jnp.float32)).astype(bf16)  1.27 us
  transfers between devices with their start and end apart: 11, of which 7 were waited for; matrix products, arithmetic and copies ran while one was open for 9% of the time, Pallas kernels for 0%

profile of v1, /device:TPU:0, one launch (start us, length us, event | category | flops | bytes accessed | tf_op | source)
XLA Modules:
  0.0 47.6 jit_solution(2504116958045053237)
XLA Ops:
  0.6 0.9 %pad_maximum_fusion.refs_7_.refs_11_ = bf16[64,1024]{1,0:T(8,128)(2,1)S(1)} fusion(bf16[64,512]{1,0:T(8,128)(2,1)} %bitcast.45, bf16[64,512]{1,0:T(8,128)(2,1)} %bitcast.46), kind=kLoop, calls=%fused_computation.15 | loop fusion | flops 262144 | bytes 262144 | tf_op jit(solution)/shard_map/concatenate | solution.py:138
  1.5 0.0 copy-start
  1.5 4.0 %collective-permute-start.2 = (bf16[64,1024]{1,0:T(8,128)(2,1)S(1)}, bf16[64,1024]{1,0:T(8,128)(2,1)S(1)}, u32[]{:S(2)}, u32[]{:S(2)}) collective-permute-start(bf16[64,1024]{1,0:T(8,128)(2,1)S(1)} %pad_maximum_fusion.refs_7_.refs_11_), channel_id=1, source_target_pairs={{0,3},{1,2},{2,1},{3,0},{4,7},{5,6},{6,5},{7,4},{8,11},{9,10},{10,... | collective-permute-start | bytes 393224 | tf_op jit(solution)/shard_map/ppermute | solution.py:26
  5.5 0.5 %collective-permute-start.1 = (bf16[64,1024]{1,0:T(8,128)(2,1)S(1)}, bf16[64,1024]{1,0:T(8,128)(2,1)S(1)}, u32[]{:S(2)}, u32[]{:S(2)}) collective-permute-start(bf16[64,1024]{1,0:T(8,128)(2,1)S(1)} %pad_maximum_fusion.refs_7_.refs_11_), channel_id=1, source_target_pairs={{0,2},{1,3},{2,0},{3,1},{4,6},{5,7},{6,4},{7,5},{8,10},{9,11},{10,... | collective-permute-start | bytes 393224 | tf_op jit(solution)/shard_map/ppermute | solution.py:26
  6.0 0.1 collective-permute-start
  6.1 0.0 collective-permute-start.3
  6.1 0.0 copy-start.10
  6.1 3.2 %collective-permute-done.2.refs_10_.refs_14_ = bf16[64,1024]{1,0:T(8,128)(2,1)S(1)} collective-permute-done((bf16[64,1024]{1,0:T(8,128)(2,1)S(1)}, bf16[64,1024]{1,0:T(8,128)(2,1)S(1)}, u32[]{:S(2)}, u32[]{:S(2)}) %collective-permute-start.2) | collective-permute-done | bytes 131104 | tf_op jit(solution)/shard_map/ppermute | solution.py:26
  9.4 0.0 collective-permute-start.6
  9.4 2.4 %collective-permute-done.1.refs_9_.refs_13_ = bf16[64,1024]{1,0:T(8,128)(2,1)S(1)} collective-permute-done((bf16[64,1024]{1,0:T(8,128)(2,1)S(1)}, bf16[64,1024]{1,0:T(8,128)(2,1)S(1)}, u32[]{:S(2)}, u32[]{:S(2)}) %collective-permute-start.1) | collective-permute-done | bytes 131104 | tf_op jit(solution)/shard_map/ppermute | solution.py:26
  11.8 0.0 collective-permute-start.5
  11.8 0.2 collective-permute-done.refs_8_.refs_12_
  12.0 0.3 collective-permute-start.4
  12.3 0.0 copy-done.10
  12.3 0.0 copy-done.9
  12.3 0.6 %select_reduce_fusion = (s32[]{:T(128)}, s32[]{:T(128)}) fusion(s32[8,4]{0,1:T(4,128)S(1)} %copy-done.9, s32[8,4]{0,1:T(4,128)S(1)} %copy-done.10, s32[]{:T(128)S(6)} %add.36, pred[8]{0:T(512)(128)(4,1)S(1)} %fusion.7), kind=kLoop, calls=%fused_computation.16 | loop fusion | flops 190 | bytes 276 | tf_op jit(solution)/shard_map/reduce_sum | solution.py:146
  13.6 0.0 copy-start.11
  13.6 0.6 %copy-done.11 = s32[8]{0:T(128)S(1)} copy-done((s32[8]{0:T(128)S(1)}, s32[8]{0:T(128)}, u32[]{:S(2)}) %copy-start.11) | copy-done | bytes 56
  14.3 1.3 %fusion.9 = (s32[]{:T(128)}, s32[]{:T(128)}) fusion(s32[8]{0:T(128)S(1)} %copy-done.11, s32[]{:T(128)} %get-tuple-element.32, s32[]{:T(128)S(6)} %axis_index.23), kind=kLoop, calls=%fused_computation.27 | loop fusion | flops 46 | bytes 48 | tf_op jit(solution)/shard_map/reduce_sum | solution.py:148
  15.5 2.5 %stack.27.refs_0_ = s32[5]{0:T(128)} concatenate(s32[1]{0:T(128)} %bitcast, s32[1]{0:T(128)} %bitcast.1, s32[1]{0:T(128)} %bitcast.2, s32[1]{0:T(128)} %bitcast.3, s32[1]{0:T(128)} %bitcast.4), dimensions={0} | concatenate | bytes 40 | tf_op jit(solution)/shard_map/stack | solution.py:150
  18.1 0.0 collective-permute-done.3.refs_15_.refs_19_
  18.1 0.0 collective-permute-done.6.refs_18_.refs_22_
  18.1 0.0 copy-start.5
  18.1 0.0 collective-permute-done.5.refs_17_.refs_21_
  18.1 0.0 copy-start.6
  18.1 0.0 collective-permute-done.4.refs_16_.refs_20_
  18.1 0.0 copy-start.7
  18.1 0.0 copy-done
  18.2 0.0 copy-done.1
  18.2 0.0 copy-done.2
  18.2 0.0 copy-done.3
  18.2 0.6 %copy-done.4 = bf16[64,1024]{1,0:T(8,128)(2,1)} copy-done((bf16[64,1024]{1,0:T(8,128)(2,1)}, bf16[64,1024]{1,0:T(8,128)(2,1)S(1)}, u32[]{:S(2)}) %copy-start.4) | copy-done | bytes 131096
  18.7 0.1 copy-done.5
  18.8 0.1 copy-done.6
  18.9 0.0 copy-done.7
  18.9 13.5 %tree_attention.1 = (bf16[64,4096]{1,0:T(8,128)(2,1)}, bf16[64,4096]{1,0:T(8,128)(2,1)}, bf16[128,4096]{1,0:T(8,128)(2,1)}, bf16[128,4096]{1,0:T(8,128)(2,1)}, b...) custom-call(s32[5]{0:T(128)} %stack.27.refs_0_, ...), custom_call_target="tpu_custom_call" | custom-call | tf_op jit(solution)/shard_map/tree_attention/pallas_call | solution.py:157
  32.4 0.3 collective-permute-start.7
  32.7 1.9 %collective-permute-done.7 = bf16[4,2,64,512]{3,2,1,0:T(8,128)(2,1)S(1)} collective-permute-done((bf16[4,2,64,512]{3,2,1,0:T(8,128)(2,1)}, bf16[4,2,64,512]{3,2,1,0:T(8,128)(2,1)S(1)}, u32[]{:S(2)}, u32[]{:S(2)}) %collective-permute-start.7) | collective-permute-done | bytes 524320 | tf_op jit(solution)/shard_map/ppermute | solution.py:26
  34.6 1.3 %fusion.2 = (bf16[2,64,512]{2,1,0:T(8,128)(2,1)S(1)}, bf16[2,64,512]{2,1,0:T(8,128)(2,1)S(1)}, bf16[2,64,512]{2,1,0:T(8,128)(2,1)S(1)}) fusion(f32[2,64,512]{2,1,0:T(8,128)} %get-tuple-element.25, bf16[4,2,64,512]{3,2,1,0:T(8,128)(2,1)S(1)} %collective-permute-done.7, f32[2,64,512]{2,1,0:T(8,128)} %get-tuple-element.27, f32[2,64,512]{2,1,0:T(8,128)} %get-tuple-element.26), kind=kLoop, calls=%fused_computation.5 | loop fusion | flops 589824 | bytes 1572864 | tf_op jit(solution)/shard_map/convert_element_type | solution.py:182
  35.8 1.7 %collective-permute-start.8 = (bf16[2,64,512]{2,1,0:T(8,128)(2,1)S(1)}, bf16[2,64,512]{2,1,0:T(8,128)(2,1)S(1)}, u32[]{:S(2)}, u32[]{:S(2)}) collective-permute-start(bf16[2,64,512]{2,1,0:T(8,128)(2,1)S(1)} %get-tuple-element.34), channel_id=1, source_target_pairs={{0,1},{1,0},{2,3},{3,2},{4,5},{5,4},{6,7},{7,6},{8,9},{9,8},{10,11... | collective-permute-start | bytes 393224 | tf_op jit(solution)/shard_map/ppermute | solution.py:26
  37.6 1.5 %collective-permute-start.10 = (bf16[2,64,512]{2,1,0:T(8,128)(2,1)S(1)}, bf16[2,64,512]{2,1,0:T(8,128)(2,1)S(1)}, u32[]{:S(2)}, u32[]{:S(2)}) collective-permute-start(bf16[2,64,512]{2,1,0:T(8,128)(2,1)S(1)} %get-tuple-element.35), channel_id=1, source_target_pairs={{0,3},{1,2},{2,1},{3,0},{4,7},{5,6},{6,5},{7,4},{8,11},{9,10},{10,... | collective-permute-start | bytes 393224 | tf_op jit(solution)/shard_map/ppermute | solution.py:26
  39.1 0.3 collective-permute-start.9
  39.4 2.8 %collective-permute-done.8 = bf16[2,64,512]{2,1,0:T(8,128)(2,1)S(1)} collective-permute-done((bf16[2,64,512]{2,1,0:T(8,128)(2,1)S(1)}, bf16[2,64,512]{2,1,0:T(8,128)(2,1)S(1)}, u32[]{:S(2)}, u32[]{:S(2)}) %collective-permute-start.8) | collective-permute-done | bytes 131104 | tf_op jit(solution)/shard_map/ppermute | solution.py:26
  42.2 3.3 %collective-permute-done.10 = bf16[2,64,512]{2,1,0:T(8,128)(2,1)S(1)} collective-permute-done((bf16[2,64,512]{2,1,0:T(8,128)(2,1)S(1)}, bf16[2,64,512]{2,1,0:T(8,128)(2,1)S(1)}, u32[]{:S(2)}, u32[]{:S(2)}) %collective-permute-start.10) | collective-permute-done | bytes 131104 | tf_op jit(solution)/shard_map/ppermute | solution.py:26
  45.5 1.4 %collective-permute-done.9 = bf16[2,64,512]{2,1,0:T(8,128)(2,1)S(1)} collective-permute-done((bf16[2,64,512]{2,1,0:T(8,128)(2,1)S(1)}, bf16[2,64,512]{2,1,0:T(8,128)(2,1)S(1)}, u32[]{:S(2)}, u32[]{:S(2)}) %collective-permute-start.9) | collective-permute-done | bytes 131104 | tf_op jit(solution)/shard_map/ppermute | solution.py:26
  46.9 0.0 copy-done.8
  46.9 0.1 fusion.6
  47.0 0.7 %fusion.10 = (bf16[1,64,512]{2,1,0:T(8,128)(2,1)}, bf16[1,64,512]{2,1,0:T(8,128)(2,1)}) fusion(bf16[2,64,512]{2,1,0:T(8,128)(2,1)S(1)} %fusion.6), kind=kLoop, calls=%fused_computation.28 | loop fusion | bytes 262144 | tf_op jit(solution)/shard_map/slice | solution.py:191
  (7 shorter events, 0.0 us)
Async XLA Ops:
  1.5 16.6 %copy-start = (bf16[64,1024]{1,0:T(8,128)(2,1)}, bf16[64,1024]{1,0:T(8,128)(2,1)S(1)}, u32[]{:S(2)}) copy-start(bf16[64,1024]{1,0:T(8,128)(2,1)S(1)} %pad_maximum_fusion.refs_7_.refs_11_) | copy-start | bytes 393220
  1.5 7.9 %collective-permute-start.2 = (bf16[64,1024]{1,0:T(8,128)(2,1)S(1)}, bf16[64,1024]{1,0:T(8,128)(2,1)S(1)}, u32[]{:S(2)}, u32[]{:S(2)}) collective-permute-start(bf16[64,1024]{1,0:T(8,128)(2,1)S(1)} %pad_maximum_fusion.refs_7_.refs_11_), channel_id=1, source_target_pairs={{0,3},{1,2},{2,1},{3,0},{4,7},{5,6},{6,5},{7,4},{8,11},{9,10},{10,... | collective-permute-start | bytes 393224 | tf_op jit(solution)/shard_map/ppermute | solution.py:26
  5.5 6.3 %collective-permute-start.1 = (bf16[64,1024]{1,0:T(8,128)(2,1)S(1)}, bf16[64,1024]{1,0:T(8,128)(2,1)S(1)}, u32[]{:S(2)}, u32[]{:S(2)}) collective-permute-start(bf16[64,1024]{1,0:T(8,128)(2,1)S(1)} %pad_maximum_fusion.refs_7_.refs_11_), channel_id=1, source_target_pairs={{0,2},{1,3},{2,0},{3,1},{4,6},{5,7},{6,4},{7,5},{8,10},{9,11},{10,... | collective-permute-start | bytes 393224 | tf_op jit(solution)/shard_map/ppermute | solution.py:26
  6.0 6.0 %collective-permute-start = (bf16[64,1024]{1,0:T(8,128)(2,1)S(1)}, bf16[64,1024]{1,0:T(8,128)(2,1)S(1)}, u32[]{:S(2)}, u32[]{:S(2)}) collective-permute-start(bf16[64,1024]{1,0:T(8,128)(2,1)S(1)} %pad_maximum_fusion.refs_7_.refs_11_), channel_id=1, source_target_pairs={{0,1},{1,0},{2,3},{3,2},{4,5},{5,4},{6,7},{7,6},{8,9},{9,8},{10,11... | collective-permute-start | bytes 393224 | tf_op jit(solution)/shard_map/ppermute | solution.py:26
  6.1 12.0 %collective-permute-start.3 = (bf16[64,1024]{1,0:T(8,128)(2,1)S(1)}, bf16[64,1024]{1,0:T(8,128)(2,1)S(1)}, u32[]{:S(2)}, u32[]{:S(2)}) collective-permute-start(bf16[64,1024]{1,0:T(8,128)(2,1)S(1)} %pad_maximum_fusion.refs_7_.refs_11_), channel_id=1, source_target_pairs={{0,4},{4,0},{8,12},{12,8},{16,20},{20,16},{24,28},{28,24},{1,5},{5... | collective-permute-start | bytes 393224 | tf_op jit(solution)/shard_map/ppermute | solution.py:26
  6.1 6.2 %copy-start.10 = (s32[8,4]{0,1:T(4,128)S(1)}, s32[8,4]{0,1:T(4,128)}, u32[]{:S(2)}) copy-start(s32[8,4]{0,1:T(4,128)} %param.13) | copy-start | bytes 388
  6.1 6.2 %copy-start.9 = (s32[8,4]{0,1:T(4,128)S(1)}, s32[8,4]{0,1:T(4,128)}, u32[]{:S(2)}) copy-start(s32[8,4]{0,1:T(4,128)} %param.12) | copy-start | bytes 388
  9.4 8.8 %copy-start.1 = (bf16[64,1024]{1,0:T(8,128)(2,1)}, bf16[64,1024]{1,0:T(8,128)(2,1)S(1)}, u32[]{:S(2)}) copy-start(bf16[64,1024]{1,0:T(8,128)(2,1)S(1)} %collective-permute-done.2.refs_10_.refs_14_) | copy-start | bytes 393220
  9.4 8.7 %collective-permute-start.6 = (bf16[64,1024]{1,0:T(8,128)(2,1)S(1)}, bf16[64,1024]{1,0:T(8,128)(2,1)S(1)}, u32[]{:S(2)}, u32[]{:S(2)}) collective-permute-start(bf16[64,1024]{1,0:T(8,128)(2,1)S(1)} %collective-permute-done.2.refs_10_.refs_14_), channel_id=1, source_target_pairs={{0,4},{4,0},{8,12},{12,8},{16,20},{20,16},{24,28},{28,24},{1,5},{5... | collective-permute-start | bytes 393224 | tf_op jit(solution)/shard_map/ppermute | solution.py:26
  11.8 6.4 %copy-start.2 = (bf16[64,1024]{1,0:T(8,128)(2,1)}, bf16[64,1024]{1,0:T(8,128)(2,1)S(1)}, u32[]{:S(2)}) copy-start(bf16[64,1024]{1,0:T(8,128)(2,1)S(1)} %collective-permute-done.1.refs_9_.refs_13_) | copy-start | bytes 393220
  11.8 6.3 %collective-permute-start.5 = (bf16[64,1024]{1,0:T(8,128)(2,1)S(1)}, bf16[64,1024]{1,0:T(8,128)(2,1)S(1)}, u32[]{:S(2)}, u32[]{:S(2)}) collective-permute-start(bf16[64,1024]{1,0:T(8,128)(2,1)S(1)} %collective-permute-done.1.refs_9_.refs_13_), channel_id=1, source_target_pairs={{0,4},{4,0},{8,12},{12,8},{16,20},{20,16},{24,28},{28,24},{1,5},{5... | collective-permute-start | bytes 393224 | tf_op jit(solution)/shard_map/ppermute | solution.py:26
  12.0 6.1 %copy-start.3 = (bf16[64,1024]{1,0:T(8,128)(2,1)}, bf16[64,1024]{1,0:T(8,128)(2,1)S(1)}, u32[]{:S(2)}) copy-start(bf16[64,1024]{1,0:T(8,128)(2,1)S(1)} %collective-permute-done.refs_8_.refs_12_) | copy-start | bytes 393220
  12.0 6.1 %collective-permute-start.4 = (bf16[64,1024]{1,0:T(8,128)(2,1)S(1)}, bf16[64,1024]{1,0:T(8,128)(2,1)S(1)}, u32[]{:S(2)}, u32[]{:S(2)}) collective-permute-start(bf16[64,1024]{1,0:T(8,128)(2,1)S(1)} %collective-permute-done.refs_8_.refs_12_), channel_id=1, source_target_pairs={{0,4},{4,0},{8,12},{12,8},{16,20},{20,16},{24,28},{28,24},{1,5},{5... | collective-permute-start | bytes 393224 | tf_op jit(solution)/shard_map/ppermute | solution.py:26
  13.6 0.7 %copy-start.11 = (s32[8]{0:T(128)S(1)}, s32[8]{0:T(128)}, u32[]{:S(2)}) copy-start(s32[8]{0:T(128)} %param.11) | copy-start | bytes 100
  18.1 0.7 %copy-start.4 = (bf16[64,1024]{1,0:T(8,128)(2,1)}, bf16[64,1024]{1,0:T(8,128)(2,1)S(1)}, u32[]{:S(2)}) copy-start(bf16[64,1024]{1,0:T(8,128)(2,1)S(1)} %collective-permute-done.3.refs_15_.refs_19_) | copy-start | bytes 393220
  18.1 0.7 %copy-start.5 = (bf16[64,1024]{1,0:T(8,128)(2,1)}, bf16[64,1024]{1,0:T(8,128)(2,1)S(1)}, u32[]{:S(2)}) copy-start(bf16[64,1024]{1,0:T(8,128)(2,1)S(1)} %collective-permute-done.6.refs_18_.refs_22_) | copy-start | bytes 393220
  18.1 0.8 %copy-start.6 = (bf16[64,1024]{1,0:T(8,128)(2,1)}, bf16[64,1024]{1,0:T(8,128)(2,1)S(1)}, u32[]{:S(2)}) copy-start(bf16[64,1024]{1,0:T(8,128)(2,1)S(1)} %collective-permute-done.5.refs_17_.refs_21_) | copy-start | bytes 393220
  18.1 0.8 %copy-start.7 = (bf16[64,1024]{1,0:T(8,128)(2,1)}, bf16[64,1024]{1,0:T(8,128)(2,1)S(1)}, u32[]{:S(2)}) copy-start(bf16[64,1024]{1,0:T(8,128)(2,1)S(1)} %collective-permute-done.4.refs_16_.refs_20_) | copy-start | bytes 393220
  32.4 2.2 %collective-permute-start.7 = (bf16[4,2,64,512]{3,2,1,0:T(8,128)(2,1)}, bf16[4,2,64,512]{3,2,1,0:T(8,128)(2,1)S(1)}, u32[]{:S(2)}, u32[]{:S(2)}) collective-permute-start(bf16[4,2,64,512]{3,2,1,0:T(8,128)(2,1)} %get-tuple-element.24), channel_id=1, source_target_pairs={{0,4},{4,0},{8,12},{12,8},{16,20},{20,16},{24,28},{28,24},{1,5},{5... | collective-permute-start | bytes 1572872 | tf_op jit(solution)/shard_map/ppermute | solution.py:26
  34.6 12.3 %copy-start.8 = (f32[2,64,512]{2,1,0:T(8,128)S(1)}, f32[2,64,512]{2,1,0:T(8,128)}, u32[]{:S(2)}) copy-start(f32[2,64,512]{2,1,0:T(8,128)} %get-tuple-element.23) | copy-start | bytes 786436
  35.8 6.4 %collective-permute-start.8 = (bf16[2,64,512]{2,1,0:T(8,128)(2,1)S(1)}, bf16[2,64,512]{2,1,0:T(8,128)(2,1)S(1)}, u32[]{:S(2)}, u32[]{:S(2)}) collective-permute-start(bf16[2,64,512]{2,1,0:T(8,128)(2,1)S(1)} %get-tuple-element.34), channel_id=1, source_target_pairs={{0,1},{1,0},{2,3},{3,2},{4,5},{5,4},{6,7},{7,6},{8,9},{9,8},{10,11... | collective-permute-start | bytes 393224 | tf_op jit(solution)/shard_map/ppermute | solution.py:26
  37.6 7.9 %collective-permute-start.10 = (bf16[2,64,512]{2,1,0:T(8,128)(2,1)S(1)}, bf16[2,64,512]{2,1,0:T(8,128)(2,1)S(1)}, u32[]{:S(2)}, u32[]{:S(2)}) collective-permute-start(bf16[2,64,512]{2,1,0:T(8,128)(2,1)S(1)} %get-tuple-element.35), channel_id=1, source_target_pairs={{0,3},{1,2},{2,1},{3,0},{4,7},{5,6},{6,5},{7,4},{8,11},{9,10},{10,... | collective-permute-start | bytes 393224 | tf_op jit(solution)/shard_map/ppermute | solution.py:26
  39.1 7.8 %collective-permute-start.9 = (bf16[2,64,512]{2,1,0:T(8,128)(2,1)S(1)}, bf16[2,64,512]{2,1,0:T(8,128)(2,1)S(1)}, u32[]{:S(2)}, u32[]{:S(2)}) collective-permute-start(bf16[2,64,512]{2,1,0:T(8,128)(2,1)S(1)} %get-tuple-element.36), channel_id=1, source_target_pairs={{0,2},{1,3},{2,0},{3,1},{4,6},{5,7},{6,4},{7,5},{8,10},{9,11},{10,... | collective-permute-start | bytes 393224 | tf_op jit(solution)/shard_map/ppermute | solution.py:26

commit v2 on v1

v2 whole, which is shorter than its diff:
```python
import jax
import jax.numpy as jnp
from jax import lax
from jax.experimental import pallas as pl
from jax.experimental.pallas import tpu as pltpu
from jax.sharding import PartitionSpec as P

HQ = 32
KVH = 4
DH = 128
PER = HQ // KVH
SCALE = DH ** (-0.5)
LOG2E = 1.4426950408889634
BLOCKED = -1e30
LONG = 512
BF16 = jnp.bfloat16
F32 = jnp.float32
NN = (((1,), (0,)), ((), ()))
NT = (((1,), (1,)), ((), ()))
TN = (((0,), (0,)), ((), ()))


def dot(a, b, dims=NN):
    return lax.dot_general(a, b, dims, preferred_element_type=F32)


def swapped(block, axis, distance):
    count = lax.axis_size(axis)
    return lax.ppermute(block, axis, [(i, i ^ distance) for i in range(count)])


def tall(block):
    return jnp.concatenate([block[:, lanes(h)] for h in range(PER)], axis=0)


def wide(block):
    rows = block.shape[0] // PER
    return jnp.concatenate([block[h * rows : (h + 1) * rows] for h in range(PER)], axis=1)


def lanes(c, width=DH):
    return slice(c * width, (c + 1) * width)


def hosted(resp_len, resp_host, count):
    group = lax.axis_index("grp")
    first = group // 2 * 2
    slot = group % 2 * count + lax.axis_index("seq")
    owner, length = first, jnp.int32(0)
    for offset in range(2):
        for r in range(resp_host.shape[0]):
            match = resp_host[r, first + offset] == slot
            owner = jnp.where(match, first + offset, owner)
            length = jnp.where(match, resp_len[r, first + offset], length)
    return owner, length


def beside(a, b):
    blank = jnp.zeros_like(a)
    return jnp.concatenate(
        [jnp.concatenate([a, blank], axis=1), jnp.concatenate([jnp.zeros_like(b), b], axis=1)], axis=0
    )


def softmax(scores, dprob):
    top = jnp.max(scores, axis=-1, keepdims=True)
    raised = jnp.exp2(scores - top)
    probs = raised * (1.0 / jnp.sum(raised, axis=-1, keepdims=True))
    weighted = probs * dprob
    delta = jnp.sum(weighted, axis=-1, keepdims=True)
    return probs.astype(BF16), ((weighted - probs * delta) * SCALE).astype(BF16)


def masked(scores, bias):
    rows, columns = bias.shape
    scaled = (scores * (SCALE * LOG2E)).reshape(PER, rows, columns) + bias[None]
    return scaled.reshape(PER * rows, columns)


def prepare_kernel(
    count, prompt_table, len_table, host_table, q_p, g_p, q_r, g_r, k_r, v_r,
    qg_p, qg_r, bias_p, bias_r, own_r, keep_p, keep_r, chosen, buf_qp, buf_gp, buf_qr, buf_gr, buf_k, buf_v, prompt_len, resp_len, resp_host, sems,
):
    buffers = (buf_qr, buf_gr, buf_k, buf_v, buf_qp, buf_gp)
    copies = [
        pltpu.make_async_copy(src, dst, sems.at[i])
        for i, (src, dst) in enumerate(zip((q_r, g_r, k_r, v_r, q_p, g_p), buffers))
    ]
    tables = [
        pltpu.make_async_copy(src, dst, sems.at[6 + i])
        for i, (src, dst) in enumerate(
            ((prompt_table, prompt_len), (len_table, resp_len), (host_table, resp_host))
        )
    ]
    for copy in tables + copies:
        copy.start()
    for copy in tables:
        copy.wait()
    shard = lax.axis_index("seq")
    owner, resp_length = hosted(resp_len, resp_host, count)
    own_length = prompt_len[lax.axis_index("grp")]
    owner_length = prompt_len[owner]
    rows, slots = buf_qp.shape[0], buf_qr.shape[0]
    column = lax.broadcasted_iota(jnp.int32, (1, count * rows), 1)
    place = ((column // rows) ^ shard) * rows + column % rows
    position = lax.broadcasted_iota(jnp.int32, (rows, 1), 0) + shard * rows
    live_p = position < own_length
    bias_p[...] = jnp.where((place == position) | ((place < position) & live_p), 0.0, BLOCKED)
    slot = lax.broadcasted_iota(jnp.int32, (slots, 1), 0)
    live_r = slot < resp_length
    keep_p[...] = jnp.where(live_p, 1.0, 0.0) + jnp.zeros(keep_p.shape, F32)
    keep_r[...] = jnp.where(live_r, 1.0, 0.0) + jnp.zeros(keep_r.shape, F32)
    chosen[...] = jnp.zeros(chosen.shape, F32) + jnp.where(owner == lax.axis_index("grp"), 1.0, 0.0)
    bias_r[...] = jnp.where(live_r & (place < owner_length), 0.0, BLOCKED)
    other = lax.broadcasted_iota(jnp.int32, (1, slots), 1)
    bias_own = jnp.where((other == slot) | ((other < slot) & live_r), 0.0, BLOCKED)
    for copy in copies[:4]:
        copy.wait()
    for c in range(KVH):
        for h in range(PER):
            to, at = slice(h * slots, (h + 1) * slots), lanes(c * PER + h)
            qg_r[c, to, :DH] = buf_qr[:, at]
            qg_r[c, to, DH:] = jnp.where(live_r, buf_gr[:, at], 0)
        both = dot(qg_r[c], beside(buf_k[:, lanes(c)], buf_v[:, lanes(c)]), NT)
        for h in range(PER):
            to = slice(h * slots, (h + 1) * slots)
            own_r[c, to, :slots] = both[to, :slots] * (SCALE * LOG2E) + bias_own
            own_r[c, to, slots:] = both[to, slots:]
    for copy in copies[4:]:
        copy.wait()
    for c in range(KVH):
        for h in range(PER):
            to, at = slice(h * rows, (h + 1) * rows), lanes(c * PER + h)
            qg_p[c, to, :DH] = buf_qp[:, at]
            qg_p[c, to, DH:] = jnp.where(live_p, buf_gp[:, at], 0)


def response_kernel(count, *refs):
    qg, bias, own, chosen, k_r, v_r = refs[:6]
    own_kv, pair_kv = refs[6 : 6 + count], refs[6 + count : 6 + 2 * count]
    pds, mix, near, far, scores = refs[6 + 2 * count :]
    piece = own_kv[0].shape[0]
    span, slots = count * piece, k_r.shape[0]
    is_own = chosen[0:1, :]
    is_pair = 1.0 - is_own
    own_half, pair_half = is_own.astype(BF16), is_pair.astype(BF16)

    def first(c):
        for d in range(count):
            part = slice(d * piece, (d + 1) * piece)
            low = slice(span + 2 * slots + d * piece, span + 2 * slots + (d + 1) * piece)
            k = own_kv[d][:, lanes(c)] * own_half + pair_kv[d][:, lanes(c)] * pair_half
            v = own_kv[d][:, lanes(KVH + c)] * own_half + pair_kv[d][:, lanes(KVH + c)] * pair_half
            mix[c, part, :DH] = v
            mix[c, part, DH:] = jnp.zeros_like(v)
            mix[c, low, :DH] = jnp.zeros_like(k)
            mix[c, low, DH:] = k
        mix[c, span : span + 2 * slots] = beside(v_r[:, lanes(c)], k_r[:, lanes(c)])
        scores[c % 2, :, :span] = dot(qg[c, :, :DH], mix[c, span + 2 * slots :, DH:], NT)
        scores[c % 2, :, span:] = dot(qg[c, :, DH:], mix[c, :span, :DH], NT)

    def second(c):
        block = jnp.concatenate(
            [masked(scores[c % 2, :, :span], bias[...]), own[c, :, :slots]], axis=1
        )
        dprob = jnp.concatenate([scores[c % 2, :, span:], own[c, :, slots:]], axis=1)
        probs, dscore = softmax(block, dprob)
        pds[c, :, : span + slots] = probs
        pds[c, :, span + slots : span + 2 * slots] = dscore[:, span:]
        pds[c, :, span + 2 * slots :] = dscore[:, :span]

    def third(c):
        grad_k = dot(pds[c, :, span + 2 * slots :], qg[c, :, :DH], TN)
        grad_v = dot(pds[c, :, :span], qg[c, :, DH:], TN)
        for d in range(count):
            part = slice(d * piece, (d + 1) * piece)
            for i, grad in enumerate((grad_k[part], grad_v[part])):
                near[d, i, :, lanes(c)] = grad * is_own
                far[d, i, :, lanes(c)] = (grad * is_pair).astype(BF16)

    first(0)
    for c in range(KVH):
        if c + 1 < KVH:
            first(c + 1)
        second(c)
        third(c)


def prompt_kernel(count, qg, bias, near_r, *refs):
    own_kv = refs[:count]
    pds, mix, *near, scores = refs[count:]
    rows = piece = own_kv[0].shape[0]
    span = count * piece

    def first(c):
        for d in range(count):
            part, low = slice(d * piece, (d + 1) * piece), slice(span + d * piece, span + (d + 1) * piece)
            k, v = own_kv[d][:, lanes(c)], own_kv[d][:, lanes(KVH + c)]
            mix[c, part, :DH] = v
            mix[c, part, DH:] = jnp.zeros_like(v)
            mix[c, low, :DH] = jnp.zeros_like(k)
            mix[c, low, DH:] = k
        scores[c % 2, :, :span] = dot(qg[c, :, :DH], mix[c, span:, DH:], NT)
        scores[c % 2, :, span:] = dot(qg[c, :, DH:], mix[c, :span, :DH], NT)

    def second(c):
        probs, dscore = softmax(masked(scores[c % 2, :, :span], bias[...]), scores[c % 2, :, span:])
        pds[c, :, :span] = probs
        pds[c, :, span:] = dscore

    def third(c):
        grad_k = dot(pds[c, :, span:], qg[c, :, :DH], TN)
        grad_v = dot(pds[c, :, :span], qg[c, :, DH:], TN)
        for d in range(count):
            part = slice(d * piece, (d + 1) * piece)
            for i, grad in enumerate((grad_k[part], grad_v[part])):
                near[d][i, :, lanes(c)] = near_r[d, i, :, lanes(c)] + grad

    first(0)
    for c in range(KVH):
        if c + 1 < KVH:
            first(c + 1)
        second(c)
        third(c)


def kept(block, keep):
    rows = keep.shape[0]
    return (block.reshape(PER, rows, DH) * keep[None]).reshape(PER * rows, DH).astype(BF16)


def finish_kernel(span, keep_p, keep_r, pds_p, mix_p, pds_r, mix_r, qg_r, out_p, dq_p, out_r, dq_r, dk_r, dv_r):
    c = pl.program_id(0)
    slots = dk_r.shape[0]
    both = dot(pds_r[c], mix_r[c])
    out_r[...] = wide(kept(both[:, :DH], keep_r[...]))
    dq_r[...] = wide(both[:, DH:].astype(BF16))
    dv_r[...] = dot(pds_r[c, :, span : span + slots], qg_r[c, :, DH:], TN).astype(BF16)
    dk_r[...] = dot(pds_r[c, :, span + slots : span + 2 * slots], qg_r[c, :, :DH], TN).astype(BF16)
    both = dot(pds_p[c], mix_p[c])
    out_p[...] = wide(kept(both[:, :DH], keep_p[...]))
    dq_p[...] = wide(both[:, DH:].astype(BF16))


def attend(queries, cotangent, keys, values, bias, live):
    rows, count = bias.shape
    scores = (dot(queries, keys, NT) * (SCALE * LOG2E)).reshape(PER, rows, count) + bias[None]
    top = jnp.max(scores, axis=-1, keepdims=True)
    raised = jnp.exp2(scores - top)
    total = jnp.sum(raised, axis=-1, keepdims=True)
    probs = (raised * (1.0 / total)).reshape(PER * rows, count)
    half = probs.astype(BF16)
    mixed = dot(half, values).reshape(PER, rows, DH)
    result = jnp.where(live[None], mixed, 0.0).astype(BF16).reshape(PER * rows, DH)
    delta = jnp.sum(
        cotangent.astype(F32) * result.astype(F32), axis=-1, keepdims=True
    )
    dprob = dot(cotangent, values, NT)
    dscore = (probs * (dprob - delta) * SCALE).astype(BF16)
    grad_q = dot(dscore, keys).astype(BF16)
    grad_k = dot(dscore, queries, TN)
    grad_v = dot(half, cotangent, TN)
    return result, grad_q, grad_k, grad_v


def long_kernel(count, *refs):
    prompt_len, resp_len, resp_host, q_p, g_p, q_r, g_r, k_r, v_r = refs[:9]
    own_k, own_v, pair_k, pair_v = [refs[9 + i * count : 9 + (i + 1) * count] for i in range(4)]
    out_p, dq_p, out_r, dq_r, dk_r, dv_r, far, *near = refs[9 + 4 * count :]
    group = lax.axis_index("grp")
    shard = lax.axis_index("seq")
    own_length = prompt_len[group]
    owner, resp_length = hosted(resp_len, resp_host, count)
    owner_length = prompt_len[owner]
    is_own = owner == group
    piece = own_k[0].shape[0]
    rows = q_p.shape[0]
    slots = q_r.shape[0]
    span = count * piece
    column = lax.broadcasted_iota(jnp.int32, (1, span), 1)
    place = ((column // piece) ^ shard) * piece + column % piece
    position = lax.broadcasted_iota(jnp.int32, (rows, 1), 0) + shard * rows
    live = position < own_length
    allowed = (place == position) | ((place < position) & live)
    bias = jnp.where(allowed, 0.0, BLOCKED)
    keys = jnp.concatenate([ref[...] for ref in own_k], axis=0)
    values = jnp.concatenate([ref[...] for ref in own_v], axis=0)
    queries = tall(q_p[...])
    cotangent = tall(jnp.where(live, g_p[...], 0))
    result, grad_q, own_gk, own_gv = attend(queries, cotangent, keys, values, bias, live)
    out_p[...] = wide(result)
    dq_p[...] = wide(grad_q)

    slot = lax.broadcasted_iota(jnp.int32, (slots, 1), 0)
    live = slot < resp_length
    other = lax.broadcasted_iota(jnp.int32, (1, slots), 1)
    bias = jnp.concatenate(
        [
            jnp.where(live & (place < owner_length), 0.0, BLOCKED),
            jnp.where((other == slot) | ((other < slot) & live), 0.0, BLOCKED),
        ],
        axis=1,
    )
    keys = jnp.concatenate(
        [jnp.where(is_own, a[...], b[...]) for a, b in zip(own_k, pair_k)] + [k_r[...]], axis=0
    )
    values = jnp.concatenate(
        [jnp.where(is_own, a[...], b[...]) for a, b in zip(own_v, pair_v)] + [v_r[...]], axis=0
    )
    queries = tall(q_r[...])
    cotangent = tall(jnp.where(live, g_r[...], 0))
    result, grad_q, grad_k, grad_v = attend(queries, cotangent, keys, values, bias, live)
    out_r[...] = wide(result)
    dq_r[...] = wide(grad_q)
    dk_r[...] = grad_k[span:].astype(BF16)
    dv_r[...] = grad_v[span:].astype(BF16)
    for d in range(count):
        part = slice(d * piece, (d + 1) * piece)
        near[d][0] = own_gk[part] + jnp.where(is_own, grad_k[part], 0.0)
        near[d][1] = own_gv[part] + jnp.where(is_own, grad_v[part], 0.0)
        far[d, 0] = jnp.where(is_own, 0.0, grad_k[part]).astype(BF16)
        far[d, 1] = jnp.where(is_own, 0.0, grad_v[part]).astype(BF16)


def long_prompts(prompt_len, resp_len, resp_host, q_p, g_p, q_r, g_r, k_r, v_r, own, pair):
    count, rows, slots = len(own), q_p.shape[0], q_r.shape[0]
    piece, width = rows, KVH * DH

    def block(height, lanes, offset=0):
        return pl.BlockSpec((height, lanes), lambda c: (0, c + offset))

    wide_p, wide_r = block(rows, PER * DH), block(slots, PER * DH)
    return pl.pallas_call(
        lambda *refs: long_kernel(count, *refs),
        grid=(KVH,),
        in_specs=[pl.BlockSpec(memory_space=pltpu.SMEM)] * 3
        + [wide_p, wide_p, wide_r, wide_r]
        + [block(slots, DH)] * 2
        + [block(piece, DH)] * count
        + [block(piece, DH, KVH)] * count
        + [block(piece, DH)] * count
        + [block(piece, DH, KVH)] * count,
        out_specs=[wide_p, wide_p, wide_r, wide_r]
        + [block(slots, DH)] * 2
        + [pl.BlockSpec((count, 2, piece, DH), lambda c: (0, 0, 0, c))]
        + [pl.BlockSpec((2, piece, DH), lambda c: (0, 0, c))] * count,
        out_shape=[jax.ShapeDtypeStruct((rows, HQ * DH), BF16)] * 2
        + [jax.ShapeDtypeStruct((slots, HQ * DH), BF16)] * 2
        + [jax.ShapeDtypeStruct((slots, width), BF16)] * 2
        + [jax.ShapeDtypeStruct((count, 2, piece, width), BF16)]
        + [jax.ShapeDtypeStruct((2, piece, width), F32)] * count,
        compiler_params=pltpu.CompilerParams(vmem_limit_bytes=56 * 2**20),
        name="long_prompts",
    )(prompt_len, resp_len, resp_host, q_p, g_p, q_r, g_r, k_r, v_r, *own, *own, *pair, *pair)


def summed(near, back):
    total = near[0] + back[0].astype(F32)
    for d in range(1, len(near)):
        part = (near[d] + back[d].astype(F32)).astype(BF16)
        total = total + swapped(part, "seq", d).astype(F32)
    return total.astype(BF16)


def collected(out_p, dq_p, out_r, dq_r, dk_r, dv_r, total):
    return tuple(
        array[None] for array in (out_p, out_r, dq_p, dq_r, total[0], total[1], dk_r, dv_r)
    )


def shards(
    prompt_len,
    resp_len,
    resp_host,
    q_prompt,
    k_prompt,
    v_prompt,
    g_prompt,
    q_resp,
    k_resp,
    v_resp,
    g_resp,
):
    count = lax.axis_size("seq")
    rows = q_prompt.shape[1]
    slots = q_resp.shape[1]
    width = KVH * DH
    span = count * rows
    vmem, hbm = [pl.BlockSpec(memory_space=space) for space in (pltpu.VMEM, pltpu.HBM)]
    resp_len, resp_host = resp_len.T, resp_host.T

    def inside(*shape, dtype=BF16):
        return pltpu.VMEM(shape, dtype)

    def held(array):
        return pltpu.with_memory_space_constraint(array, pltpu.HBM)

    def options(megabytes):
        return pltpu.CompilerParams(vmem_limit_bytes=megabytes * 2**20)

    def cost(flops):
        return pl.CostEstimate(flops=flops, bytes_accessed=2**20, transcendentals=0)

    mine = jnp.concatenate([k_prompt[0], v_prompt[0]], axis=1)
    own = [mine] + [swapped(mine, "seq", d) for d in range(1, count)]
    if span > LONG:
        pair = [swapped(part, "grp", 1) for part in own]
        out_p, dq_p, out_r, dq_r, dk_r, dv_r, far, *near = long_prompts(
            prompt_len, resp_len, resp_host, q_prompt[0], g_prompt[0], q_resp[0], g_resp[0],
            k_resp[0], v_resp[0], own, pair,
        )
        total = summed(near, swapped(far, "grp", 1))
        return collected(out_p, dq_p, out_r, dq_r, dk_r, dv_r, total)

    qg_p, qg_r, bias_p, bias_r, own_r, keep_p, keep_r, chosen = pl.pallas_call(
        lambda *refs: prepare_kernel(count, *refs),
        in_specs=[hbm] * 9,
        out_specs=[vmem] * 8,
        out_shape=[
            inside(KVH, PER * rows, 2 * DH),
            inside(KVH, PER * slots, 2 * DH),
            inside(rows, span, dtype=F32),
            inside(slots, span, dtype=F32),
            inside(KVH, PER * slots, 2 * slots, dtype=F32),
            inside(rows, DH, dtype=F32),
            inside(slots, DH, dtype=F32),
            inside(8, DH, dtype=F32),
        ],
        scratch_shapes=[pltpu.VMEM((rows, HQ * DH), BF16)] * 2
        + [pltpu.VMEM((slots, HQ * DH), BF16)] * 2
        + [pltpu.VMEM((slots, width), BF16)] * 2
        + [pltpu.SMEM(t.shape, jnp.int32) for t in (prompt_len, resp_len, resp_host)]
        + [pltpu.SemaphoreType.DMA((9,))],
        compiler_params=options(20),
        cost_estimate=cost(4 * 10**9),
        name="prepare",
    )(
        held(prompt_len), held(resp_len), held(resp_host),
        held(q_prompt[0]), held(g_prompt[0]), held(q_resp[0]), held(g_resp[0]),
        held(k_resp[0]), held(v_resp[0]),
    )

    own[1:] = [lax.optimization_barrier((part, chosen))[0] for part in own[1:]]
    pair = [swapped(part, "grp", 1) for part in own]
    pds_r, mix_r, near_r, far = pl.pallas_call(
        lambda *refs: response_kernel(count, *refs),
        in_specs=[vmem] * (6 + 2 * count),
        out_specs=[vmem] * 4,
        out_shape=[
            inside(KVH, PER * slots, 2 * (span + slots)),
            inside(KVH, 2 * (span + slots), 2 * DH),
            inside(count, 2, rows, width, dtype=F32),
            inside(count, 2, rows, width),
        ],
        scratch_shapes=[pltpu.VMEM((2, PER * slots, 2 * span), F32)],
        compiler_params=options(20),
        cost_estimate=cost(3 * 10**9),
        name="responses",
    )(qg_r, bias_r, own_r, chosen, k_resp[0], v_resp[0], *own, *pair)
    back = swapped(far, "grp", 1)

    pds_p, mix_p, *near = pl.pallas_call(
        lambda *refs: prompt_kernel(count, *refs),
        in_specs=[vmem] * (3 + count),
        out_specs=[vmem] * (2 + count),
        out_shape=[inside(KVH, PER * rows, 2 * span), inside(KVH, 2 * span, 2 * DH)]
        + [inside(2, rows, width, dtype=F32)] * count,
        scratch_shapes=[pltpu.VMEM((2, PER * rows, 2 * span), F32)],
        compiler_params=options(20),
        cost_estimate=cost(2 * 10**9),
        name="prompts",
    )(qg_p, bias_p, near_r, *own)

    def block(height, extent):
        return pl.BlockSpec((height, extent), lambda c: (0, c))

    wide_p, wide_r = block(rows, PER * DH), block(slots, PER * DH)
    out_p, dq_p, out_r, dq_r, dk_r, dv_r = pl.pallas_call(
        lambda *refs: finish_kernel(span, *refs),
        grid=(KVH,),
        in_specs=[vmem] * 7,
        out_specs=[wide_p, wide_p, wide_r, wide_r] + [block(slots, DH)] * 2,
        out_shape=[jax.ShapeDtypeStruct((rows, HQ * DH), BF16)] * 2
        + [jax.ShapeDtypeStruct((slots, HQ * DH), BF16)] * 2
        + [jax.ShapeDtypeStruct((slots, width), BF16)] * 2,
        compiler_params=options(20),
        cost_estimate=cost(8 * 10**9),
        name="finish",
    )(keep_p, keep_r, pds_p, mix_p, pds_r, mix_r, qg_r)
    return collected(out_p, dq_p, out_r, dq_r, dk_r, dv_r, summed(near, back))


def solution(mesh):
    split = P("grp", "seq", None)
    return jax.shard_map(
        shards,
        mesh=mesh,
        in_specs=(P(), P(), P()) + (split,) * 8,
        out_specs=(split,) * 8,
        check_vma=False,
    )
```

time: 47.9 us -> 33 us (0.69)
  waiting for transfers between devices: 15.2 us -> 5.18 us
  local copies, waits for them, and re-layouts: 4.6 us -> 0.67 us
  other arithmetic: 4.16 us -> 1.09 us
  Pallas kernels: 13.5 us -> 15.7 us
  starting transfers between devices: 8.74 us -> 9.57 us
  between operations: 1.41 us -> 0.7 us
    ppermute x11, waiting for transfers between devices: 15.2 us -> 5.18 us  [swapped(): return lax.ppermute(block, axis, [(i, i ^ distance) for i in range(count)])]
    another operation x1 -> x0, local copies, waits for them, and re-layouts: 2.54 us -> none  [shards(): jnp.stack([own_length, resp_length, owner_length, shard_id, is_own])]
    pallas_call x1 -> x4, Pallas kernels: 13.5 us -> 15.7 us  [the longest x1 5.67 us: shards(): pl.pallas_call(lambda *refs: response_kernel(count, *refs), in_specs=[vme...]
    reduce_sum x2 -> x0, other arithmetic: 1.92 us -> none  [the longest x1 1.28 us: shards(): owner_length = jnp.sum(jnp.where(group_ids == owner, prompt_len, 0))]
    unnamed x24 -> x4, local copies, waits for them, and re-layouts: 1.4 us -> 0.01 us
    convert_element_type x2, other arithmetic: 1.36 us -> 0.21 us  [the longest x1 0.12 us: summed(): part = (near[d] + back[d].astype(F32)).astype(BF16)]
    ppermute x11, starting transfers between devices: 8.74 us -> 9.57 us  [swapped(): return lax.ppermute(block, axis, [(i, i ^ distance) for i in range(count)])]
  transfers between devices with their start and end apart: 11 -> 11, of which waited for: 7 -> 4; matrix products, arithmetic and copies ran while one was open for 9% -> 0% of each run, Pallas kernels for 0% -> 30%
where the time goes in v2:
time: 33 us; the launch traced here: 32.9 us
  Pallas kernels  15.7 us (48%)
  starting transfers between devices  9.57 us (29%)
  waiting for transfers between devices  5.18 us (16%)
  other arithmetic  1.09 us (3%)
  between operations  0.7 us (2%)
  local copies, waits for them, and re-layouts  0.67 us (2%)
    ppermute x11, starting transfers between devices, swapped(): return lax.ppermute(block, axis, [(i, i ^ distance) for i in range(count)])  9.57 us
    pallas_call x1, Pallas kernels, shards(): pl.pallas_call(lambda *refs: response_kernel(count, *refs), in_specs=[vme...  5.67 us
    ppermute x11, waiting for transfers between devices, swapped(): return lax.ppermute(block, axis, [(i, i ^ distance) for i in range(count)])  5.18 us
    pallas_call x1, Pallas kernels, shards(): pl.pallas_call(lambda *refs: finish_kernel(span, *refs), grid=(KVH,), in_...  4.4 us
    pallas_call x1, Pallas kernels, shards(): pl.pallas_call(lambda *refs: prepare_kernel(count, *refs), in_specs=[hbm]...  2.95 us
    pallas_call x1, Pallas kernels, shards(): pl.pallas_call(lambda *refs: prompt_kernel(count, *refs), in_specs=[vmem]...  2.64 us
    concatenate x1, other arithmetic, shards(): mine = jnp.concatenate([k_prompt[0], v_prompt[0]], axis=1)  0.88 us
    slice x1, local copies, waits for them, and re-layouts, collected(): total[1]  0.66 us
  transfers between devices with their start and end apart: 11, of which 4 were waited for; matrix products, arithmetic and copies ran while one was open for 0% of the time, Pallas kernels for 30%

profile of v2, /device:TPU:0, one launch (start us, length us, event | category | flops | bytes accessed | tf_op | source)
XLA Modules:
  0.0 32.9 jit_solution(99980944405858889)
XLA Ops:
  0.6 0.9 %pad_maximum_fusion.refs_6_.refs_3_ = bf16[64,1024]{1,0:T(8,128)(2,1)S(1)} fusion(bf16[64,512]{1,0:T(8,128)(2,1)} %bitcast.40, bf16[64,512]{1,0:T(8,128)(2,1)} %bitcast.41), kind=kLoop, calls=%fused_computation.15 | loop fusion | flops 262144 | bytes 262144 | tf_op jit(solution)/shard_map/concatenate | solution.py:404
  1.5 3.0 %collective-permute-start = (bf16[64,1024]{1,0:T(8,128)(2,1)S(1)}, bf16[64,1024]{1,0:T(8,128)(2,1)S(1)}, u32[]{:S(2)}, u32[]{:S(2)}) collective-permute-start(bf16[64,1024]{1,0:T(8,128)(2,1)S(1)} %pad_maximum_fusion.refs_6_.refs_3_), channel_id=1, source_target_pairs={{0,1},{1,0},{2,3},{3,2},{4,5},{5,4},{6,7},{7,6},{8,9},{9,8},{10,11... | collective-permute-start | bytes 393224 | tf_op jit(solution)/shard_map/ppermute | solution.py:29
  4.5 1.5 %collective-permute-start.1 = (bf16[64,1024]{1,0:T(8,128)(2,1)S(1)}, bf16[64,1024]{1,0:T(8,128)(2,1)S(1)}, u32[]{:S(2)}, u32[]{:S(2)}) collective-permute-start(bf16[64,1024]{1,0:T(8,128)(2,1)S(1)} %pad_maximum_fusion.refs_6_.refs_3_), channel_id=1, source_target_pairs={{0,2},{1,3},{2,0},{3,1},{4,6},{5,7},{6,4},{7,5},{8,10},{9,11},{10,... | collective-permute-start | bytes 393224 | tf_op jit(solution)/shard_map/ppermute | solution.py:29
  6.0 0.0 collective-permute-start.2
  6.1 0.0 collective-permute-start.3
  6.1 0.0 copy-start
  6.1 0.0 copy-start.1
  6.1 2.9 %prepare.1 = (bf16[4,512,256]{2,1,0:T(8,128)(2,1)S(1)}, bf16[4,1024,256]{2,1,0:T(8,128)(2,1)S(1)}, f32[64,256]{1,0:T(8,128)S(1)}, f32[128,256]{1,0:T(8,128)S(1)}...) custom-call(s32[8]{0:T(128)} %refs_0_.1, ...), custom_call_target="tpu_custom_call" | custom-call | flops 4000000000 | bytes 1048576 | tf_op jit(solution)/shard_map/prepare/pallas_call | solution.py:415
  9.0 0.0 collective-permute-done.refs_7_.refs_4_
  9.0 0.6 %collective-permute-start.4 = (bf16[64,1024]{1,0:T(8,128)(2,1)S(1)}, bf16[64,1024]{1,0:T(8,128)(2,1)S(1)}, u32[]{:S(2)}, u32[]{:S(2)}) collective-permute-start(bf16[64,1024]{1,0:T(8,128)(2,1)S(1)} %collective-permute-done.refs_7_.refs_4_), channel_id=1, source_target_pairs={{0,4},{4,0},{8,12},{12,8},{16,20},{20,16},{24,28},{28,24},{1,5},{5... | collective-permute-start | bytes 393224 | tf_op jit(solution)/shard_map/ppermute | solution.py:29
  9.6 2.7 %collective-permute-done.1.refs_8_.refs_5_ = bf16[64,1024]{1,0:T(8,128)(2,1)S(1)} collective-permute-done((bf16[64,1024]{1,0:T(8,128)(2,1)S(1)}, bf16[64,1024]{1,0:T(8,128)(2,1)S(1)}, u32[]{:S(2)}, u32[]{:S(2)}) %collective-permute-start.1) | collective-permute-done | bytes 131104 | tf_op jit(solution)/shard_map/ppermute | solution.py:29
  12.3 0.0 collective-permute-start.5
  12.3 0.0 collective-permute-done.2.refs_9_.refs_6_
  12.3 0.5 %collective-permute-start.6 = (bf16[64,1024]{1,0:T(8,128)(2,1)S(1)}, bf16[64,1024]{1,0:T(8,128)(2,1)S(1)}, u32[]{:S(2)}, u32[]{:S(2)}) collective-permute-start(bf16[64,1024]{1,0:T(8,128)(2,1)S(1)} %collective-permute-done.2.refs_9_.refs_6_), channel_id=1, source_target_pairs={{0,4},{4,0},{8,12},{12,8},{16,20},{20,16},{24,28},{28,24},{1,5},{5... | collective-permute-start | bytes 393224 | tf_op jit(solution)/shard_map/ppermute | solution.py:29
  12.8 0.0 collective-permute-done.3.refs_10_
  12.8 0.0 collective-permute-done.4.refs_11_
  12.8 0.8 %collective-permute-done.5.refs_12_ = bf16[64,1024]{1,0:T(8,128)(2,1)S(1)} collective-permute-done((bf16[64,1024]{1,0:T(8,128)(2,1)S(1)}, bf16[64,1024]{1,0:T(8,128)(2,1)S(1)}, u32[]{:S(2)}, u32[]{:S(2)}) %collective-permute-start.5) | collective-permute-done | bytes 131104 | tf_op jit(solution)/shard_map/ppermute | solution.py:29
  13.6 0.2 collective-permute-done.6.refs_13_
  13.8 0.0 copy-done
  13.8 0.0 copy-done.1
  13.8 5.7 %responses.1 = (bf16[4,1024,768]{2,1,0:T(8,128)(2,1)S(1)}, bf16[4,768,256]{2,1,0:T(8,128)(2,1)S(1)}, f32[4,2,64,512]{3,2,1,0:T(8,128)S(1)}, bf16[4,2,64,512]{3,2,1,0:T(8,128)(2,1)S(1)}) custom-call(bf16[4,1024,256]{2,1,0:T(8,128)(2,1)S(1)} %get-tuple-element.39.refs_0_.refs_6_, f32[128,256]{1,0:T(8,128)S(1)} %get-tuple-element.40.refs_1_, ...), custom_call_target="tpu_custom_call" | custom-call | flops 3000000000 | bytes 1048576 | tf_op jit(solution)/shard_map/responses/pallas_call | solution.py:445
  19.5 0.4 %collective-permute-start.7 = (bf16[4,2,64,512]{3,2,1,0:T(8,128)(2,1)S(1)}, bf16[4,2,64,512]{3,2,1,0:T(8,128)(2,1)S(1)}, u32[]{:S(2)}, u32[]{:S(2)}) collective-permute-start(bf16[4,2,64,512]{3,2,1,0:T(8,128)(2,1)S(1)} %get-tuple-element.56), channel_id=1, source_target_pairs={{0,4},{4,0},{8,12},{12,8},{16,20},{20,16},{24,28},{28,24},{1,5},{5... | collective-permute-start | bytes 1572872 | tf_op jit(solution)/shard_map/ppermute | solution.py:29
  19.9 2.6 %prompts.1 = (bf16[4,512,512]{2,1,0:T(8,128)(2,1)S(1)}, bf16[4,512,256]{2,1,0:T(8,128)(2,1)S(1)}, f32[2,64,512]{2,1,0:T(8,128)S(1)}, f32[2,64,512]{2,1,0:T(8,128...) custom-call(bf16[4,512,256]{2,1,0:T(8,128)(2,1)S(1)} %get-tuple-element.37.refs_0_, ...), custom_call_target="tpu_custom_call" | custom-call | flops 2000000000 | bytes 1048576 | tf_op jit(solution)/shard_map/prompts/pallas_call | solution.py:462
  22.6 0.0 collective-permute-done.7
  22.6 0.1 fusion.2
  22.7 1.5 %collective-permute-start.10 = (bf16[2,64,512]{2,1,0:T(8,128)(2,1)S(1)}, bf16[2,64,512]{2,1,0:T(8,128)(2,1)S(1)}, u32[]{:S(2)}, u32[]{:S(2)}) collective-permute-start(bf16[2,64,512]{2,1,0:T(8,128)(2,1)S(1)} %get-tuple-element.63), channel_id=1, source_target_pairs={{0,3},{1,2},{2,1},{3,0},{4,7},{5,6},{6,5},{7,4},{8,11},{9,10},{10,... | collective-permute-start | bytes 393224 | tf_op jit(solution)/shard_map/ppermute | solution.py:29
  24.2 1.5 %collective-permute-start.8 = (bf16[2,64,512]{2,1,0:T(8,128)(2,1)S(1)}, bf16[2,64,512]{2,1,0:T(8,128)(2,1)S(1)}, u32[]{:S(2)}, u32[]{:S(2)}) collective-permute-start(bf16[2,64,512]{2,1,0:T(8,128)(2,1)S(1)} %get-tuple-element.62), channel_id=1, source_target_pairs={{0,1},{1,0},{2,3},{3,2},{4,5},{5,4},{6,7},{7,6},{8,9},{9,8},{10,11... | collective-permute-start | bytes 393224 | tf_op jit(solution)/shard_map/ppermute | solution.py:29
  25.7 0.5 %collective-permute-start.9 = (bf16[2,64,512]{2,1,0:T(8,128)(2,1)S(1)}, bf16[2,64,512]{2,1,0:T(8,128)(2,1)S(1)}, u32[]{:S(2)}, u32[]{:S(2)}) collective-permute-start(bf16[2,64,512]{2,1,0:T(8,128)(2,1)S(1)} %get-tuple-element.64), channel_id=1, source_target_pairs={{0,2},{1,3},{2,0},{3,1},{4,6},{5,7},{6,4},{7,5},{8,10},{9,11},{10,... | collective-permute-start | bytes 393224 | tf_op jit(solution)/shard_map/ppermute | solution.py:29
  26.3 4.4 %finish.1 = (bf16[64,4096]{1,0:T(8,128)(2,1)}, bf16[64,4096]{1,0:T(8,128)(2,1)}, bf16[128,4096]{1,0:T(8,128)(2,1)}, bf16[128,4096]{1,0:T(8,128)(2,1)}, bf16[128,...) custom-call(f32[64,128]{1,0:T(8,128)S(1)} %get-tuple-element.35.refs_0_, f32[128,128]{1,0:T(8,128)S(1)} %get-tuple-element.36.refs_1_, ...), custom_call_target="tpu_custom_call" | custom-call | flops 8000000000 | bytes 1048576 | tf_op jit(solution)/shard_map/finish/pallas_call | solution.py:478
  30.7 0.0 collective-permute-done.10
  30.7 1.4 %collective-permute-done.8 = bf16[2,64,512]{2,1,0:T(8,128)(2,1)S(1)} collective-permute-done((bf16[2,64,512]{2,1,0:T(8,128)(2,1)S(1)}, bf16[2,64,512]{2,1,0:T(8,128)(2,1)S(1)}, u32[]{:S(2)}, u32[]{:S(2)}) %collective-permute-start.8) | collective-permute-done | bytes 131104 | tf_op jit(solution)/shard_map/ppermute | solution.py:29
  32.1 0.0 collective-permute-done.9
  32.1 0.1 fusion.6
  32.2 0.7 %fusion.7 = (bf16[1,64,512]{2,1,0:T(8,128)(2,1)}, bf16[1,64,512]{2,1,0:T(8,128)(2,1)}) fusion(bf16[2,64,512]{2,1,0:T(8,128)(2,1)S(1)} %fusion.6), kind=kLoop, calls=%fused_computation.16 | loop fusion | bytes 262144 | tf_op jit(solution)/shard_map/slice | solution.py:367
Async XLA Ops:
  1.5 7.5 %collective-permute-start = (bf16[64,1024]{1,0:T(8,128)(2,1)S(1)}, bf16[64,1024]{1,0:T(8,128)(2,1)S(1)}, u32[]{:S(2)}, u32[]{:S(2)}) collective-permute-start(bf16[64,1024]{1,0:T(8,128)(2,1)S(1)} %pad_maximum_fusion.refs_6_.refs_3_), channel_id=1, source_target_pairs={{0,1},{1,0},{2,3},{3,2},{4,5},{5,4},{6,7},{7,6},{8,9},{9,8},{10,11... | collective-permute-start | bytes 393224 | tf_op jit(solution)/shard_map/ppermute | solution.py:29
  4.5 7.8 %collective-permute-start.1 = (bf16[64,1024]{1,0:T(8,128)(2,1)S(1)}, bf16[64,1024]{1,0:T(8,128)(2,1)S(1)}, u32[]{:S(2)}, u32[]{:S(2)}) collective-permute-start(bf16[64,1024]{1,0:T(8,128)(2,1)S(1)} %pad_maximum_fusion.refs_6_.refs_3_), channel_id=1, source_target_pairs={{0,2},{1,3},{2,0},{3,1},{4,6},{5,7},{6,4},{7,5},{8,10},{9,11},{10,... | collective-permute-start | bytes 393224 | tf_op jit(solution)/shard_map/ppermute | solution.py:29
  6.0 6.3 %collective-permute-start.2 = (bf16[64,1024]{1,0:T(8,128)(2,1)S(1)}, bf16[64,1024]{1,0:T(8,128)(2,1)S(1)}, u32[]{:S(2)}, u32[]{:S(2)}) collective-permute-start(bf16[64,1024]{1,0:T(8,128)(2,1)S(1)} %pad_maximum_fusion.refs_6_.refs_3_), channel_id=1, source_target_pairs={{0,3},{1,2},{2,1},{3,0},{4,7},{5,6},{6,5},{7,4},{8,11},{9,10},{10,... | collective-permute-start | bytes 393224 | tf_op jit(solution)/shard_map/ppermute | solution.py:29
  6.1 6.8 %collective-permute-start.3 = (bf16[64,1024]{1,0:T(8,128)(2,1)S(1)}, bf16[64,1024]{1,0:T(8,128)(2,1)S(1)}, u32[]{:S(2)}, u32[]{:S(2)}) collective-permute-start(bf16[64,1024]{1,0:T(8,128)(2,1)S(1)} %pad_maximum_fusion.refs_6_.refs_3_), channel_id=1, source_target_pairs={{0,4},{4,0},{8,12},{12,8},{16,20},{20,16},{24,28},{28,24},{1,5},{5... | collective-permute-start | bytes 393224 | tf_op jit(solution)/shard_map/ppermute | solution.py:29
  6.1 7.8 %copy-start = (bf16[1,128,512]{2,1,0:T(8,128)(2,1)S(1)}, bf16[1,128,512]{2,1,0:T(8,128)(2,1)}, u32[]{:S(2)}) copy-start(bf16[1,128,512]{2,1,0:T(8,128)(2,1)} %param.19) | copy-start | bytes 393220
  6.1 7.8 %copy-start.1 = (bf16[1,128,512]{2,1,0:T(8,128)(2,1)S(1)}, bf16[1,128,512]{2,1,0:T(8,128)(2,1)}, u32[]{:S(2)}) copy-start(bf16[1,128,512]{2,1,0:T(8,128)(2,1)} %param.20) | copy-start | bytes 393220
  9.0 3.8 %collective-permute-start.4 = (bf16[64,1024]{1,0:T(8,128)(2,1)S(1)}, bf16[64,1024]{1,0:T(8,128)(2,1)S(1)}, u32[]{:S(2)}, u32[]{:S(2)}) collective-permute-start(bf16[64,1024]{1,0:T(8,128)(2,1)S(1)} %collective-permute-done.refs_7_.refs_4_), channel_id=1, source_target_pairs={{0,4},{4,0},{8,12},{12,8},{16,20},{20,16},{24,28},{28,24},{1,5},{5... | collective-permute-start | bytes 393224 | tf_op jit(solution)/shard_map/ppermute | solution.py:29
  12.3 1.3 %collective-permute-start.5 = (bf16[64,1024]{1,0:T(8,128)(2,1)S(1)}, bf16[64,1024]{1,0:T(8,128)(2,1)S(1)}, u32[]{:S(2)}, u32[]{:S(2)}) collective-permute-start(bf16[64,1024]{1,0:T(8,128)(2,1)S(1)} %collective-permute-done.1.refs_8_.refs_5_), channel_id=1, source_target_pairs={{0,4},{4,0},{8,12},{12,8},{16,20},{20,16},{24,28},{28,24},{1,5},{5... | collective-permute-start | bytes 393224 | tf_op jit(solution)/shard_map/ppermute | solution.py:29
  12.3 1.5 %collective-permute-start.6 = (bf16[64,1024]{1,0:T(8,128)(2,1)S(1)}, bf16[64,1024]{1,0:T(8,128)(2,1)S(1)}, u32[]{:S(2)}, u32[]{:S(2)}) collective-permute-start(bf16[64,1024]{1,0:T(8,128)(2,1)S(1)} %collective-permute-done.2.refs_9_.refs_6_), channel_id=1, source_target_pairs={{0,4},{4,0},{8,12},{12,8},{16,20},{20,16},{24,28},{28,24},{1,5},{5... | collective-permute-start | bytes 393224 | tf_op jit(solution)/shard_map/ppermute | solution.py:29
  19.5 3.0 %collective-permute-start.7 = (bf16[4,2,64,512]{3,2,1,0:T(8,128)(2,1)S(1)}, bf16[4,2,64,512]{3,2,1,0:T(8,128)(2,1)S(1)}, u32[]{:S(2)}, u32[]{:S(2)}) collective-permute-start(bf16[4,2,64,512]{3,2,1,0:T(8,128)(2,1)S(1)} %get-tuple-element.56), channel_id=1, source_target_pairs={{0,4},{4,0},{8,12},{12,8},{16,20},{20,16},{24,28},{28,24},{1,5},{5... | collective-permute-start | bytes 1572872 | tf_op jit(solution)/shard_map/ppermute | solution.py:29
  22.7 8.0 %collective-permute-start.10 = (bf16[2,64,512]{2,1,0:T(8,128)(2,1)S(1)}, bf16[2,64,512]{2,1,0:T(8,128)(2,1)S(1)}, u32[]{:S(2)}, u32[]{:S(2)}) collective-permute-start(bf16[2,64,512]{2,1,0:T(8,128)(2,1)S(1)} %get-tuple-element.63), channel_id=1, source_target_pairs={{0,3},{1,2},{2,1},{3,0},{4,7},{5,6},{6,5},{7,4},{8,11},{9,10},{10,... | collective-permute-start | bytes 393224 | tf_op jit(solution)/shard_map/ppermute | solution.py:29
  24.2 7.9 %collective-permute-start.8 = (bf16[2,64,512]{2,1,0:T(8,128)(2,1)S(1)}, bf16[2,64,512]{2,1,0:T(8,128)(2,1)S(1)}, u32[]{:S(2)}, u32[]{:S(2)}) collective-permute-start(bf16[2,64,512]{2,1,0:T(8,128)(2,1)S(1)} %get-tuple-element.62), channel_id=1, source_target_pairs={{0,1},{1,0},{2,3},{3,2},{4,5},{5,4},{6,7},{7,6},{8,9},{9,8},{10,11... | collective-permute-start | bytes 393224 | tf_op jit(solution)/shard_map/ppermute | solution.py:29
  25.7 6.4 %collective-permute-start.9 = (bf16[2,64,512]{2,1,0:T(8,128)(2,1)S(1)}, bf16[2,64,512]{2,1,0:T(8,128)(2,1)S(1)}, u32[]{:S(2)}, u32[]{:S(2)}) collective-permute-start(bf16[2,64,512]{2,1,0:T(8,128)(2,1)S(1)} %get-tuple-element.64), channel_id=1, source_target_pairs={{0,2},{1,3},{2,0},{3,1},{4,6},{5,7},{6,4},{7,5},{8,10},{9,11},{10,... | collective-permute-start | bytes 393224 | tf_op jit(solution)/shard_map/ppermute | solution.py:29

commit v3 on v2

--- a/solution.py
+++ b/solution.py
@@ -58,28 +58,18 @@
 def beside(a, b):
     blank = jnp.zeros_like(a)
     return jnp.concatenate(
-        [jnp.concatenate([a, blank], axis=1), jnp.concatenate([jnp.zeros_like(b), b], axis=1)], axis=0
-    )
-
-
-def softmax(scores, dprob):
-    top = jnp.max(scores, axis=-1, keepdims=True)
-    raised = jnp.exp2(scores - top)
-    probs = raised * (1.0 / jnp.sum(raised, axis=-1, keepdims=True))
-    weighted = probs * dprob
-    delta = jnp.sum(weighted, axis=-1, keepdims=True)
-    return probs.astype(BF16), ((weighted - probs * delta) * SCALE).astype(BF16)
+        [jnp.concatenate([a, blank], axis=1), jnp.concatenate([blank, b], axis=1)], axis=0
+    )
 
 
 def masked(scores, bias):
-    rows, columns = bias.shape
-    scaled = (scores * (SCALE * LOG2E)).reshape(PER, rows, columns) + bias[None]
-    return scaled.reshape(PER * rows, columns)
+    return scores * (SCALE * LOG2E) + jnp.concatenate([bias] * (scores.shape[1] // DH), axis=1)
 
 
 def prepare_kernel(
     count, prompt_table, len_table, host_table, q_p, g_p, q_r, g_r, k_r, v_r,
-    qg_p, qg_r, bias_p, bias_r, own_r, keep_p, keep_r, chosen, buf_qp, buf_gp, buf_qr, buf_gr, buf_k, buf_v, prompt_len, resp_len, resp_host, sems,
+    qg_p, qg_r, bias_p, bias_r, own_e, own_d, own_s, keep_p, keep_r, chosen,
+    buf_qp, buf_gp, buf_qr, buf_gr, buf_k, buf_v, prompt_len, resp_len, resp_host, sems,
 ):
     buffers = (buf_qr, buf_gr, buf_k, buf_v, buf_qp, buf_gp)
     copies = [
@@ -98,22 +88,25 @@
         copy.wait()
     shard = lax.axis_index("seq")
     owner, resp_length = hosted(resp_len, resp_host, count)
-    own_length = prompt_len[lax.axis_index("grp")]
-    owner_length = prompt_len[owner]
+    group = lax.axis_index("grp")
+    own_length, owner_length = prompt_len[group], prompt_len[owner]
     rows, slots = buf_qp.shape[0], buf_qr.shape[0]
-    column = lax.broadcasted_iota(jnp.int32, (1, count * rows), 1)
-    place = ((column // rows) ^ shard) * rows + column % rows
-    position = lax.broadcasted_iota(jnp.int32, (rows, 1), 0) + shard * rows
-    live_p = position < own_length
-    bias_p[...] = jnp.where((place == position) | ((place < position) & live_p), 0.0, BLOCKED)
-    slot = lax.broadcasted_iota(jnp.int32, (slots, 1), 0)
-    live_r = slot < resp_length
-    keep_p[...] = jnp.where(live_p, 1.0, 0.0) + jnp.zeros(keep_p.shape, F32)
-    keep_r[...] = jnp.where(live_r, 1.0, 0.0) + jnp.zeros(keep_r.shape, F32)
-    chosen[...] = jnp.zeros(chosen.shape, F32) + jnp.where(owner == lax.axis_index("grp"), 1.0, 0.0)
-    bias_r[...] = jnp.where(live_r & (place < owner_length), 0.0, BLOCKED)
-    other = lax.broadcasted_iota(jnp.int32, (1, slots), 1)
-    bias_own = jnp.where((other == slot) | ((other < slot) & live_r), 0.0, BLOCKED)
+    span = count * rows
+    key = lax.broadcasted_iota(jnp.int32, (span, DH), 0)
+    place = ((key // rows) ^ shard) * rows + key % rows
+    lane = lax.broadcasted_iota(jnp.int32, (span, DH), 1)
+    bias_p[...] = jnp.where(place <= lane % rows + shard * rows, 0.0, BLOCKED)
+    bias_r[...] = jnp.where(place < owner_length, 0.0, BLOCKED)
+    key = lax.broadcasted_iota(jnp.int32, (slots, DH), 0)
+    lane = lax.broadcasted_iota(jnp.int32, (slots, DH), 1)
+    bias_own = jnp.where(key <= lane % slots, 0.0, BLOCKED)
+    chosen[...] = jnp.zeros(chosen.shape, F32) + jnp.where(owner == group, 1.0, 0.0)
+    lane = lax.broadcasted_iota(jnp.int32, keep_p.shape, 1)
+    keep_p[...] = jnp.where(lane % rows + shard * rows < own_length, 1.0, 0.0)
+    lane = lax.broadcasted_iota(jnp.int32, keep_r.shape, 1)
+    keep_r[...] = jnp.where(lane % slots < resp_length, 1.0, 0.0)
+    live_p = lax.broadcasted_iota(jnp.int32, (rows, 1), 0) + shard * rows < own_length
+    live_r = lax.broadcasted_iota(jnp.int32, (slots, 1), 0) < resp_length
     for copy in copies[:4]:
         copy.wait()
     for c in range(KVH):
@@ -121,11 +114,15 @@
             to, at = slice(h * slots, (h + 1) * slots), lanes(c * PER + h)
             qg_r[c, to, :DH] = buf_qr[:, at]
             qg_r[c, to, DH:] = jnp.where(live_r, buf_gr[:, at], 0)
-        both = dot(qg_r[c], beside(buf_k[:, lanes(c)], buf_v[:, lanes(c)]), NT)
-        for h in range(PER):
-            to = slice(h * slots, (h + 1) * slots)
-            own_r[c, to, :slots] = both[to, :slots] * (SCALE * LOG2E) + bias_own
-            own_r[c, to, slots:] = both[to, slots:]
+        both = dot(beside(buf_k[:, lanes(c)], buf_v[:, lanes(c)]), qg_r[c], NT)
+        scores, dprob = masked(both[:slots], bias_own), both[slots:]
+        top = jnp.max(scores, axis=0, keepdims=True)
+        raised = jnp.exp2(scores - top)
+        own_e[c] = raised
+        own_d[c] = dprob
+        own_s[c, 0:1] = top
+        own_s[c, 1:2] = jnp.sum(raised, axis=0, keepdims=True)
+        own_s[c, 2:3] = jnp.sum(raised * dprob, axis=0, keepdims=True)
     for copy in copies[4:]:
         copy.wait()
     for c in range(KVH):
@@ -136,11 +133,11 @@
 
 
 def response_kernel(count, *refs):
-    qg, bias, own, chosen, k_r, v_r = refs[:6]
-    own_kv, pair_kv = refs[6 : 6 + count], refs[6 + count : 6 + 2 * count]
-    pds, mix, near, far, scores = refs[6 + 2 * count :]
+    qg, bias, own_s, chosen = refs[:4]
+    own_kv, pair_kv = refs[4 : 4 + count], refs[4 + count : 4 + 2 * count]
+    probs_c, dscore_c, keys, values, own_t, near, far, scores = refs[4 + 2 * count :]
     piece = own_kv[0].shape[0]
-    span, slots = count * piece, k_r.shape[0]
+    span = count * piece
     is_own = chosen[0:1, :]
     is_pair = 1.0 - is_own
     own_half, pair_half = is_own.astype(BF16), is_pair.astype(BF16)
@@ -148,30 +145,31 @@
     def first(c):
         for d in range(count):
             part = slice(d * piece, (d + 1) * piece)
-            low = slice(span + 2 * slots + d * piece, span + 2 * slots + (d + 1) * piece)
-            k = own_kv[d][:, lanes(c)] * own_half + pair_kv[d][:, lanes(c)] * pair_half
-            v = own_kv[d][:, lanes(KVH + c)] * own_half + pair_kv[d][:, lanes(KVH + c)] * pair_half
-            mix[c, part, :DH] = v
-            mix[c, part, DH:] = jnp.zeros_like(v)
-            mix[c, low, :DH] = jnp.zeros_like(k)
-            mix[c, low, DH:] = k
-        mix[c, span : span + 2 * slots] = beside(v_r[:, lanes(c)], k_r[:, lanes(c)])
-        scores[c % 2, :, :span] = dot(qg[c, :, :DH], mix[c, span + 2 * slots :, DH:], NT)
-        scores[c % 2, :, span:] = dot(qg[c, :, DH:], mix[c, :span, :DH], NT)
+            for to, at in ((keys, lanes(c)), (values, lanes(KVH + c))):
+                to[c, part] = own_kv[d][:, at] * own_half + pair_kv[d][:, at] * pair_half
+        scores[c % 2, :span] = dot(keys[c], qg[c, :, :DH], NT)
+        scores[c % 2, span:] = dot(values[c], qg[c, :, DH:], NT)
 
     def second(c):
-        block = jnp.concatenate(
-            [masked(scores[c % 2, :, :span], bias[...]), own[c, :, :slots]], axis=1
-        )
-        dprob = jnp.concatenate([scores[c % 2, :, span:], own[c, :, slots:]], axis=1)
-        probs, dscore = softmax(block, dprob)
-        pds[c, :, : span + slots] = probs
-        pds[c, :, span + slots : span + 2 * slots] = dscore[:, span:]
-        pds[c, :, span + 2 * slots :] = dscore[:, :span]
+        block = masked(scores[c % 2, :span], bias[...])
+        own_top = own_s[c, 0:1]
+        top = jnp.maximum(jnp.max(block, axis=0, keepdims=True), own_top)
+        raised = jnp.exp2(block - top)
+        own_raised = jnp.exp2(own_top - top)
+        total = jnp.sum(raised, axis=0, keepdims=True) + own_raised * own_s[c, 1:2]
+        inverse = 1.0 / total
+        probs = raised * inverse
+        weighted = probs * scores[c % 2, span:]
+        own_factor = own_raised * inverse
+        delta = jnp.sum(weighted, axis=0, keepdims=True) + own_factor * own_s[c, 2:3]
+        probs_c[c] = probs.astype(BF16)
+        dscore_c[c] = ((weighted - probs * delta) * SCALE).astype(BF16)
+        own_t[c, 0:1] = own_factor
+        own_t[c, 1:2] = delta
 
     def third(c):
-        grad_k = dot(pds[c, :, span + 2 * slots :], qg[c, :, :DH], TN)
-        grad_v = dot(pds[c, :, :span], qg[c, :, DH:], TN)
+        grad_k = dot(dscore_c[c], qg[c, :, :DH])
+        grad_v = dot(probs_c[c], qg[c, :, DH:])
         for d in range(count):
             part = slice(d * piece, (d + 1) * piece)
             for i, grad in enumerate((grad_k[part], grad_v[part])):
@@ -188,29 +186,30 @@
 
 def prompt_kernel(count, qg, bias, near_r, *refs):
     own_kv = refs[:count]
-    pds, mix, *near, scores = refs[count:]
-    rows = piece = own_kv[0].shape[0]
+    probs_c, dscore_c, keys, values, *near, scores = refs[count:]
+    piece = own_kv[0].shape[0]
     span = count * piece
 
     def first(c):
         for d in range(count):
-            part, low = slice(d * piece, (d + 1) * piece), slice(span + d * piece, span + (d + 1) * piece)
-            k, v = own_kv[d][:, lanes(c)], own_kv[d][:, lanes(KVH + c)]
-            mix[c, part, :DH] = v
-            mix[c, part, DH:] = jnp.zeros_like(v)
-            mix[c, low, :DH] = jnp.zeros_like(k)
-            mix[c, low, DH:] = k
-        scores[c % 2, :, :span] = dot(qg[c, :, :DH], mix[c, span:, DH:], NT)
-        scores[c % 2, :, span:] = dot(qg[c, :, DH:], mix[c, :span, :DH], NT)
+            part = slice(d * piece, (d + 1) * piece)
+            keys[c, part] = own_kv[d][:, lanes(c)]
+            values[c, part] = own_kv[d][:, lanes(KVH + c)]
+        scores[c % 2, :span] = dot(keys[c], qg[c, :, :DH], NT)
+        scores[c % 2, span:] = dot(values[c], qg[c, :, DH:], NT)
 
     def second(c):
-        probs, dscore = softmax(masked(scores[c % 2, :, :span], bias[...]), scores[c % 2, :, span:])
-        pds[c, :, :span] = probs
-        pds[c, :, span:] = dscore
+        block = masked(scores[c % 2, :span], bias[...])
+        raised = jnp.exp2(block - jnp.max(block, axis=0, keepdims=True))
+        probs = raised * (1.0 / jnp.sum(raised, axis=0, keepdims=True))
+        weighted = probs * scores[c % 2, span:]
+        delta = jnp.sum(weighted, axis=0, keepdims=True)
+        probs_c[c] = probs.astype(BF16)
+        dscore_c[c] = ((weighted - probs * delta) * SCALE).astype(BF16)
 
     def third(c):
-        grad_k = dot(pds[c, :, span:], qg[c, :, :DH], TN)
-        grad_v = dot(pds[c, :, :span], qg[c, :, DH:], TN)
+        grad_k = dot(dscore_c[c], qg[c, :, :DH])
+        grad_v = dot(probs_c[c], qg[c, :, DH:])
         for d in range(count):
             part = slice(d * piece, (d + 1) * piece)
             for i, grad in enumerate((grad_k[part], grad_v[part])):
@@ -224,22 +223,33 @@
         third(c)
 
 
-def kept(block, keep):
-    rows = keep.shape[0]
-    return (block.reshape(PER, rows, DH) * keep[None]).reshape(PER * rows, DH).astype(BF16)
-
-
-def finish_kernel(span, keep_p, keep_r, pds_p, mix_p, pds_r, mix_r, qg_r, out_p, dq_p, out_r, dq_r, dk_r, dv_r):
+def finish_kernel(
+    keep_p, probs_p, dscore_p, keys_p, values_p, keep_r, probs_c, dscore_c, keys_c, values_c,
+    own_e, own_d, own_t, k_r, v_r, qg_r, out_p, dq_p, out_r, dq_r, dk_r, dv_r,
+):
     c = pl.program_id(0)
-    slots = dk_r.shape[0]
-    both = dot(pds_r[c], mix_r[c])
-    out_r[...] = wide(kept(both[:, :DH], keep_r[...]))
-    dq_r[...] = wide(both[:, DH:].astype(BF16))
-    dv_r[...] = dot(pds_r[c, :, span : span + slots], qg_r[c, :, DH:], TN).astype(BF16)
-    dk_r[...] = dot(pds_r[c, :, span + slots : span + 2 * slots], qg_r[c, :, :DH], TN).astype(BF16)
-    both = dot(pds_p[c], mix_p[c])
-    out_p[...] = wide(kept(both[:, :DH], keep_p[...]))
-    dq_p[...] = wide(both[:, DH:].astype(BF16))
+    own_factor, delta = own_t[c, 0:1], own_t[c, 1:2]
+    probs = own_e[c] * own_factor
+    dscore = (probs * (own_d[c] - delta) * SCALE).astype(BF16)
+    probs = probs.astype(BF16)
+    dv_r[...] = dot(probs, qg_r[c, :, DH:]).astype(BF16)
+    dk_r[...] = dot(dscore, qg_r[c, :, :DH]).astype(BF16)
+
+    def across(block):
+        return wide(block.astype(BF16).T)
+
+    left = beside(values_c[c], keys_c[c])
+    span = keys_c.shape[1]
+    own = beside(v_r[...], k_r[...])
+    left = jnp.concatenate([left[:span], own, left[span:]], axis=0)
+    right = jnp.concatenate([probs_c[c], probs, dscore, dscore_c[c]], axis=0)
+    both = dot(left, right, TN)
+    out_r[...] = across(both[:DH] * keep_r[0:1])
+    dq_r[...] = across(both[DH:])
+    right = jnp.concatenate([probs_p[c], dscore_p[c]], axis=0)
+    both = dot(beside(values_p[c], keys_p[c]), right, TN)
+    out_p[...] = across(both[:DH] * keep_p[0:1])
+    dq_p[...] = across(both[DH:])
 
 
 def attend(queries, cotangent, keys, values, bias, live):
@@ -412,18 +422,20 @@
         total = summed(near, swapped(far, "grp", 1))
         return collected(out_p, dq_p, out_r, dq_r, dk_r, dv_r, total)
 
-    qg_p, qg_r, bias_p, bias_r, own_r, keep_p, keep_r, chosen = pl.pallas_call(
+    made = pl.pallas_call(
         lambda *refs: prepare_kernel(count, *refs),
         in_specs=[hbm] * 9,
-        out_specs=[vmem] * 8,
+        out_specs=[vmem] * 10,
         out_shape=[
             inside(KVH, PER * rows, 2 * DH),
             inside(KVH, PER * slots, 2 * DH),
-            inside(rows, span, dtype=F32),
-            inside(slots, span, dtype=F32),
-            inside(KVH, PER * slots, 2 * slots, dtype=F32),
-            inside(rows, DH, dtype=F32),
-            inside(slots, DH, dtype=F32),
+            inside(span, DH, dtype=F32),
+            inside(span, DH, dtype=F32),
+            inside(KVH, slots, PER * slots, dtype=F32),
+            inside(KVH, slots, PER * slots, dtype=F32),
+            inside(KVH, 8, PER * slots, dtype=F32),
+            inside(8, PER * rows, dtype=F32),
+            inside(8, PER * slots, dtype=F32),
             inside(8, DH, dtype=F32),
         ],
         scratch_shapes=[pltpu.VMEM((rows, HQ * DH), BF16)] * 2
@@ -439,33 +451,36 @@
         held(q_prompt[0]), held(g_prompt[0]), held(q_resp[0]), held(g_resp[0]),
         held(k_resp[0]), held(v_resp[0]),
     )
+    qg_p, qg_r, bias_p, bias_r, own_e, own_d, own_s, keep_p, keep_r, chosen = made
 
     own[1:] = [lax.optimization_barrier((part, chosen))[0] for part in own[1:]]
     pair = [swapped(part, "grp", 1) for part in own]
-    pds_r, mix_r, near_r, far = pl.pallas_call(
+    probs_c, dscore_c, keys_c, values_c, own_t, near_r, far = pl.pallas_call(
         lambda *refs: response_kernel(count, *refs),
-        in_specs=[vmem] * (6 + 2 * count),
-        out_specs=[vmem] * 4,
-        out_shape=[
-            inside(KVH, PER * slots, 2 * (span + slots)),
-            inside(KVH, 2 * (span + slots), 2 * DH),
+        in_specs=[vmem] * (4 + 2 * count),
+        out_specs=[vmem] * 7,
+        out_shape=[inside(KVH, span, PER * slots)] * 2
+        + [inside(KVH, span, DH)] * 2
+        + [
+            inside(KVH, 8, PER * slots, dtype=F32),
             inside(count, 2, rows, width, dtype=F32),
             inside(count, 2, rows, width),
         ],
-        scratch_shapes=[pltpu.VMEM((2, PER * slots, 2 * span), F32)],
+        scratch_shapes=[pltpu.VMEM((2, 2 * span, PER * slots), F32)],
         compiler_params=options(20),
         cost_estimate=cost(3 * 10**9),
         name="responses",
-    )(qg_r, bias_r, own_r, chosen, k_resp[0], v_resp[0], *own, *pair)
+    )(qg_r, bias_r, own_s, chosen, *own, *pair)
     back = swapped(far, "grp", 1)
 
-    pds_p, mix_p, *near = pl.pallas_call(
+    probs_p, dscore_p, keys_p, values_p, *near = pl.pallas_call(
         lambda *refs: prompt_kernel(count, *refs),
         in_specs=[vmem] * (3 + count),
-        out_specs=[vmem] * (2 + count),
-        out_shape=[inside(KVH, PER * rows, 2 * span), inside(KVH, 2 * span, 2 * DH)]
+        out_specs=[vmem] * (4 + count),
+        out_shape=[inside(KVH, span, PER * rows)] * 2
+        + [inside(KVH, span, DH)] * 2
         + [inside(2, rows, width, dtype=F32)] * count,
-        scratch_shapes=[pltpu.VMEM((2, PER * rows, 2 * span), F32)],
+        scratch_shapes=[pltpu.VMEM((2, 2 * span, PER * rows), F32)],
         compiler_params=options(20),
         cost_estimate=cost(2 * 10**9),
         name="prompts",
@@ -474,19 +489,22 @@
     def block(height, extent):
         return pl.BlockSpec((height, extent), lambda c: (0, c))
 
-    wide_p, wide_r = block(rows, PER * DH), block(slots, PER * DH)
+    wide_p, wide_r, own_block = block(rows, PER * DH), block(slots, PER * DH), block(slots, DH)
     out_p, dq_p, out_r, dq_r, dk_r, dv_r = pl.pallas_call(
-        lambda *refs: finish_kernel(span, *refs),
+        finish_kernel,
         grid=(KVH,),
-        in_specs=[vmem] * 7,
-        out_specs=[wide_p, wide_p, wide_r, wide_r] + [block(slots, DH)] * 2,
+        in_specs=[vmem] * 13 + [own_block] * 2 + [vmem],
+        out_specs=[wide_p, wide_p, wide_r, wide_r, own_block, own_block],
         out_shape=[jax.ShapeDtypeStruct((rows, HQ * DH), BF16)] * 2
         + [jax.ShapeDtypeStruct((slots, HQ * DH), BF16)] * 2
         + [jax.ShapeDtypeStruct((slots, width), BF16)] * 2,
         compiler_params=options(20),
         cost_estimate=cost(8 * 10**9),
         name="finish",
-    )(keep_p, keep_r, pds_p, mix_p, pds_r, mix_r, qg_r)
+    )(
+        keep_p, probs_p, dscore_p, keys_p, values_p, keep_r, probs_c, dscore_c, keys_c, values_c,
+        own_e, own_d, own_t, k_resp[0], v_resp[0], qg_r,
+    )
     return collected(out_p, dq_p, out_r, dq_r, dk_r, dv_r, summed(near, back))
 
 

time: 33 us -> 31.7 us (0.961)
  Pallas kernels: 15.7 us -> 14.9 us
  waiting for transfers between devices: 5.18 us -> 4.63 us
    pallas_call x1, Pallas kernels: 5.67 us -> 4.55 us  [shards(): pl.pallas_call(lambda *refs: response_kernel(count, *refs), in_specs=[vme...]
    ppermute x11, waiting for transfers between devices: 5.18 us -> 4.63 us  [swapped(): return lax.ppermute(block, axis, [(i, i ^ distance) for i in range(count)])]
  transfers between devices with their start and end apart: 11 -> 11, of which waited for: 4 -> 4; matrix products, arithmetic and copies ran while one was open for 0% -> 0% of each run, Pallas kernels for 30% -> 33%
where the time goes in v3:
time: 31.7 us; the launch traced here: 31.6 us
  Pallas kernels  14.9 us (47%)
  starting transfers between devices  9.58 us (30%)
  waiting for transfers between devices  4.63 us (15%)
  other arithmetic  1.09 us (3%)
  between operations  0.7 us (2%)
  local copies, waits for them, and re-layouts  0.67 us (2%)
    ppermute x11, starting transfers between devices, swapped(): return lax.ppermute(block, axis, [(i, i ^ distance) for i in range(count)])  9.58 us
    pallas_call x1, Pallas kernels, shards(): pl.pallas_call(finish_kernel, grid=(KVH,), in_specs=[vmem] * 13 + [own_bl...  4.67 us
    ppermute x11, waiting for transfers between devices, swapped(): return lax.ppermute(block, axis, [(i, i ^ distance) for i in range(count)])  4.63 us
    pallas_call x1, Pallas kernels, shards(): pl.pallas_call(lambda *refs: response_kernel(count, *refs), in_specs=[vme...  4.55 us
    pallas_call x1, Pallas kernels, shards(): pl.pallas_call(lambda *refs: prepare_kernel(count, *refs), in_specs=[hbm]...  3.22 us
    pallas_call x1, Pallas kernels, shards(): pl.pallas_call(lambda *refs: prompt_kernel(count, *refs), in_specs=[vmem]...  2.47 us
    concatenate x1, other arithmetic, shards(): mine = jnp.concatenate([k_prompt[0], v_prompt[0]], axis=1)  0.88 us
    slice x1, local copies, waits for them, and re-layouts, collected(): total[1]  0.66 us
  transfers between devices with their start and end apart: 11, of which 4 were waited for; matrix products, arithmetic and copies ran while one was open for 0% of the time, Pallas kernels for 33%

profile of v3, /device:TPU:0, one launch (start us, length us, event | category | flops | bytes accessed | tf_op | source)
XLA Modules:
  0.0 31.6 jit_solution(13980575614990682006)
XLA Ops:
  0.6 0.9 %pad_maximum_fusion.refs_4_.refs_3_ = bf16[64,1024]{1,0:T(8,128)(2,1)S(1)} fusion(bf16[64,512]{1,0:T(8,128)(2,1)} %bitcast.40, bf16[64,512]{1,0:T(8,128)(2,1)} %bitcast.41), kind=kLoop, calls=%fused_computation.15 | loop fusion | flops 262144 | bytes 262144 | tf_op jit(solution)/shard_map/concatenate | solution.py:414
  1.5 3.0 %collective-permute-start = (bf16[64,1024]{1,0:T(8,128)(2,1)S(1)}, bf16[64,1024]{1,0:T(8,128)(2,1)S(1)}, u32[]{:S(2)}, u32[]{:S(2)}) collective-permute-start(bf16[64,1024]{1,0:T(8,128)(2,1)S(1)} %pad_maximum_fusion.refs_4_.refs_3_), channel_id=1, source_target_pairs={{0,1},{1,0},{2,3},{3,2},{4,5},{5,4},{6,7},{7,6},{8,9},{9,8},{10,11... | collective-permute-start | bytes 393224 | tf_op jit(solution)/shard_map/ppermute | solution.py:29
  4.5 1.5 %collective-permute-start.1 = (bf16[64,1024]{1,0:T(8,128)(2,1)S(1)}, bf16[64,1024]{1,0:T(8,128)(2,1)S(1)}, u32[]{:S(2)}, u32[]{:S(2)}) collective-permute-start(bf16[64,1024]{1,0:T(8,128)(2,1)S(1)} %pad_maximum_fusion.refs_4_.refs_3_), channel_id=1, source_target_pairs={{0,2},{1,3},{2,0},{3,1},{4,6},{5,7},{6,4},{7,5},{8,10},{9,11},{10,... | collective-permute-start | bytes 393224 | tf_op jit(solution)/shard_map/ppermute | solution.py:29
  6.0 0.0 collective-permute-start.2
  6.1 0.0 collective-permute-start.3
  6.1 3.2 %prepare.1 = (bf16[4,512,256]{2,1,0:T(8,128)(2,1)S(1)}, bf16[4,1024,256]{2,1,0:T(8,128)(2,1)S(1)}, f32[256,128]{1,0:T(8,128)S(1)}, f32[256,128]{1,0:T(8,128)S(1)...) custom-call(s32[8]{0:T(128)} %refs_0_.1, ...), custom_call_target="tpu_custom_call" | custom-call | flops 4000000000 | bytes 1048576 | tf_op jit(solution)/shard_map/prepare/pallas_call | solution.py:425
  9.3 0.0 collective-permute-done.refs_5_.refs_4_
  9.3 0.6 %collective-permute-start.4 = (bf16[64,1024]{1,0:T(8,128)(2,1)S(1)}, bf16[64,1024]{1,0:T(8,128)(2,1)S(1)}, u32[]{:S(2)}, u32[]{:S(2)}) collective-permute-start(bf16[64,1024]{1,0:T(8,128)(2,1)S(1)} %collective-permute-done.refs_5_.refs_4_), channel_id=1, source_target_pairs={{0,4},{4,0},{8,12},{12,8},{16,20},{20,16},{24,28},{28,24},{1,5},{5... | collective-permute-start | bytes 393224 | tf_op jit(solution)/shard_map/ppermute | solution.py:29
  9.9 2.4 %collective-permute-done.1.refs_6_.refs_5_ = bf16[64,1024]{1,0:T(8,128)(2,1)S(1)} collective-permute-done((bf16[64,1024]{1,0:T(8,128)(2,1)S(1)}, bf16[64,1024]{1,0:T(8,128)(2,1)S(1)}, u32[]{:S(2)}, u32[]{:S(2)}) %collective-permute-start.1) | collective-permute-done | bytes 131104 | tf_op jit(solution)/shard_map/ppermute | solution.py:29
  12.3 0.0 collective-permute-start.5
  12.3 0.0 collective-permute-done.2.refs_7_.refs_6_
  12.3 0.5 %collective-permute-start.6 = (bf16[64,1024]{1,0:T(8,128)(2,1)S(1)}, bf16[64,1024]{1,0:T(8,128)(2,1)S(1)}, u32[]{:S(2)}, u32[]{:S(2)}) collective-permute-start(bf16[64,1024]{1,0:T(8,128)(2,1)S(1)} %collective-permute-done.2.refs_7_.refs_6_), channel_id=1, source_target_pairs={{0,4},{4,0},{8,12},{12,8},{16,20},{20,16},{24,28},{28,24},{1,5},{5... | collective-permute-start | bytes 393224 | tf_op jit(solution)/shard_map/ppermute | solution.py:29
  12.8 0.0 collective-permute-done.3.refs_8_
  12.8 0.0 collective-permute-done.4.refs_9_
  12.8 0.8 %collective-permute-done.5.refs_10_ = bf16[64,1024]{1,0:T(8,128)(2,1)S(1)} collective-permute-done((bf16[64,1024]{1,0:T(8,128)(2,1)S(1)}, bf16[64,1024]{1,0:T(8,128)(2,1)S(1)}, u32[]{:S(2)}, u32[]{:S(2)}) %collective-permute-start.5) | collective-permute-done | bytes 131104 | tf_op jit(solution)/shard_map/ppermute | solution.py:29
  13.6 0.2 collective-permute-done.6.refs_11_
  13.8 4.5 %responses.1 = (bf16[4,256,1024]{2,1,0:T(8,128)(2,1)S(1)}, bf16[4,256,1024]{2,1,0:T(8,128)(2,1)S(1)}, bf16[4,256,128]{2,1,0:T(8,128)(2,1)S(1)}, bf16[4,256,128]{...) custom-call(bf16[4,1024,256]{2,1,0:T(8,128)(2,1)S(1)} %get-tuple-ele, ...), custom_call_target="tpu_custom_call" | custom-call | flops 3000000000 | bytes 1048576 | tf_op jit(solution)/shard_map/responses/pallas_call | solution.py:458
  18.4 0.4 %collective-permute-start.7 = (bf16[4,2,64,512]{3,2,1,0:T(8,128)(2,1)S(1)}, bf16[4,2,64,512]{3,2,1,0:T(8,128)(2,1)S(1)}, u32[]{:S(2)}, u32[]{:S(2)}) collective-permute-start(bf16[4,2,64,512]{3,2,1,0:T(8,128)(2,1)S(1)} %get-tuple-element.70), channel_id=1, source_target_pairs={{0,4},{4,0},{8,12},{12,8},{16,20},{20,16},{24,28},{28,24},{1,5},{5... | collective-permute-start | bytes 1572872 | tf_op jit(solution)/shard_map/ppermute | solution.py:29
  18.8 0.0 copy-start
  18.8 0.0 copy-start.1
  18.8 2.5 %prompts.1 = (bf16[4,256,512]{2,1,0:T(8,128)(2,1)S(1)}, bf16[4,256,512]{2,1,0:T(8,128)(2,1)S(1)}, bf16[4,256,128]{2,1,0:T(8,128)(2,1)S(1)}, bf16[4,256,128]{2,1,...) custom-call(bf16[4,512,256]{2,1,0:T(8,128)(2,1)S(1)} %get-tuple-elem, ...), custom_call_target="tpu_custom_call" | custom-call | flops 2000000000 | bytes 1048576 | tf_op jit(solution)/shard_map/prompts/pallas_call | solution.py:476
  21.3 0.0 collective-permute-done.7
  21.3 0.1 fusion.2
  21.4 1.5 %collective-permute-start.10 = (bf16[2,64,512]{2,1,0:T(8,128)(2,1)S(1)}, bf16[2,64,512]{2,1,0:T(8,128)(2,1)S(1)}, u32[]{:S(2)}, u32[]{:S(2)}) collective-permute-start(bf16[2,64,512]{2,1,0:T(8,128)(2,1)S(1)} %get-tuple-element.77), channel_id=1, source_target_pairs={{0,3},{1,2},{2,1},{3,0},{4,7},{5,6},{6,5},{7,4},{8,11},{9,10},{10,... | collective-permute-start | bytes 393224 | tf_op jit(solution)/shard_map/ppermute | solution.py:29
  22.9 1.5 %collective-permute-start.8 = (bf16[2,64,512]{2,1,0:T(8,128)(2,1)S(1)}, bf16[2,64,512]{2,1,0:T(8,128)(2,1)S(1)}, u32[]{:S(2)}, u32[]{:S(2)}) collective-permute-start(bf16[2,64,512]{2,1,0:T(8,128)(2,1)S(1)} %get-tuple-element.76), channel_id=1, source_target_pairs={{0,1},{1,0},{2,3},{3,2},{4,5},{5,4},{6,7},{7,6},{8,9},{9,8},{10,11... | collective-permute-start | bytes 393224 | tf_op jit(solution)/shard_map/ppermute | solution.py:29
  24.4 0.5 %collective-permute-start.9 = (bf16[2,64,512]{2,1,0:T(8,128)(2,1)S(1)}, bf16[2,64,512]{2,1,0:T(8,128)(2,1)S(1)}, u32[]{:S(2)}, u32[]{:S(2)}) collective-permute-start(bf16[2,64,512]{2,1,0:T(8,128)(2,1)S(1)} %get-tuple-element.78), channel_id=1, source_target_pairs={{0,2},{1,3},{2,0},{3,1},{4,6},{5,7},{6,4},{7,5},{8,10},{9,11},{10,... | collective-permute-start | bytes 393224 | tf_op jit(solution)/shard_map/ppermute | solution.py:29
  25.0 0.0 copy-done
  25.0 0.0 copy-done.1
  25.0 4.7 %finish.1 = (bf16[64,4096]{1,0:T(8,128)(2,1)}, bf16[64,4096]{1,0:T(8,128)(2,1)}, bf16[128,4096]{1,0:T(8,128)(2,1)}, bf16[128,4096]{1,0:T(8,128)(2,1)}, bf16[128,...) custom-call(f32[8,512]{1,0:T(8,128)S(1)} %get-tuple-element.42.keep_p, bf16[4,256,512]{2,1,0:T(8,128)(2,1)S(1)} %get-tuple-element.53.probs_p, ...), custom_call_target="tpu_custom_call" | custom-call | flops 8000000000 | bytes 1048576 | tf_op jit(solution)/shard_map/finish/pallas_call | solution.py:493
  29.6 0.0 collective-permute-done.10
  29.6 1.2 %collective-permute-done.8 = bf16[2,64,512]{2,1,0:T(8,128)(2,1)S(1)} collective-permute-done((bf16[2,64,512]{2,1,0:T(8,128)(2,1)S(1)}, bf16[2,64,512]{2,1,0:T(8,128)(2,1)S(1)}, u32[]{:S(2)}, u32[]{:S(2)}) %collective-permute-start.8) | collective-permute-done | bytes 131104 | tf_op jit(solution)/shard_map/ppermute | solution.py:29
  30.8 0.0 collective-permute-done.9
  30.8 0.1 fusion.6
  30.9 0.7 %fusion.7 = (bf16[1,64,512]{2,1,0:T(8,128)(2,1)}, bf16[1,64,512]{2,1,0:T(8,128)(2,1)}) fusion(bf16[2,64,512]{2,1,0:T(8,128)(2,1)S(1)} %fusion.6), kind=kLoop, calls=%fused_computation.16 | loop fusion | bytes 262144 | tf_op jit(solution)/shard_map/slice | solution.py:377
Async XLA Ops:
  1.5 7.8 %collective-permute-start = (bf16[64,1024]{1,0:T(8,128)(2,1)S(1)}, bf16[64,1024]{1,0:T(8,128)(2,1)S(1)}, u32[]{:S(2)}, u32[]{:S(2)}) collective-permute-start(bf16[64,1024]{1,0:T(8,128)(2,1)S(1)} %pad_maximum_fusion.refs_4_.refs_3_), channel_id=1, source_target_pairs={{0,1},{1,0},{2,3},{3,2},{4,5},{5,4},{6,7},{7,6},{8,9},{9,8},{10,11... | collective-permute-start | bytes 393224 | tf_op jit(solution)/shard_map/ppermute | solution.py:29
  4.5 7.8 %collective-permute-start.1 = (bf16[64,1024]{1,0:T(8,128)(2,1)S(1)}, bf16[64,1024]{1,0:T(8,128)(2,1)S(1)}, u32[]{:S(2)}, u32[]{:S(2)}) collective-permute-start(bf16[64,1024]{1,0:T(8,128)(2,1)S(1)} %pad_maximum_fusion.refs_4_.refs_3_), channel_id=1, source_target_pairs={{0,2},{1,3},{2,0},{3,1},{4,6},{5,7},{6,4},{7,5},{8,10},{9,11},{10,... | collective-permute-start | bytes 393224 | tf_op jit(solution)/shard_map/ppermute | solution.py:29
  6.0 6.3 %collective-permute-start.2 = (bf16[64,1024]{1,0:T(8,128)(2,1)S(1)}, bf16[64,1024]{1,0:T(8,128)(2,1)S(1)}, u32[]{:S(2)}, u32[]{:S(2)}) collective-permute-start(bf16[64,1024]{1,0:T(8,128)(2,1)S(1)} %pad_maximum_fusion.refs_4_.refs_3_), channel_id=1, source_target_pairs={{0,3},{1,2},{2,1},{3,0},{4,7},{5,6},{6,5},{7,4},{8,11},{9,10},{10,... | collective-permute-start | bytes 393224 | tf_op jit(solution)/shard_map/ppermute | solution.py:29
  6.1 6.8 %collective-permute-start.3 = (bf16[64,1024]{1,0:T(8,128)(2,1)S(1)}, bf16[64,1024]{1,0:T(8,128)(2,1)S(1)}, u32[]{:S(2)}, u32[]{:S(2)}) collective-permute-start(bf16[64,1024]{1,0:T(8,128)(2,1)S(1)} %pad_maximum_fusion.refs_4_.refs_3_), channel_id=1, source_target_pairs={{0,4},{4,0},{8,12},{12,8},{16,20},{20,16},{24,28},{28,24},{1,5},{5... | collective-permute-start | bytes 393224 | tf_op jit(solution)/shard_map/ppermute | solution.py:29
  9.3 3.5 %collective-permute-start.4 = (bf16[64,1024]{1,0:T(8,128)(2,1)S(1)}, bf16[64,1024]{1,0:T(8,128)(2,1)S(1)}, u32[]{:S(2)}, u32[]{:S(2)}) collective-permute-start(bf16[64,1024]{1,0:T(8,128)(2,1)S(1)} %collective-permute-done.refs_5_.refs_4_), channel_id=1, source_target_pairs={{0,4},{4,0},{8,12},{12,8},{16,20},{20,16},{24,28},{28,24},{1,5},{5... | collective-permute-start | bytes 393224 | tf_op jit(solution)/shard_map/ppermute | solution.py:29
  12.3 1.3 %collective-permute-start.5 = (bf16[64,1024]{1,0:T(8,128)(2,1)S(1)}, bf16[64,1024]{1,0:T(8,128)(2,1)S(1)}, u32[]{:S(2)}, u32[]{:S(2)}) collective-permute-start(bf16[64,1024]{1,0:T(8,128)(2,1)S(1)} %collective-permute-done.1.refs_6_.refs_5_), channel_id=1, source_target_pairs={{0,4},{4,0},{8,12},{12,8},{16,20},{20,16},{24,28},{28,24},{1,5},{5... | collective-permute-start | bytes 393224 | tf_op jit(solution)/shard_map/ppermute | solution.py:29
  12.3 1.5 %collective-permute-start.6 = (bf16[64,1024]{1,0:T(8,128)(2,1)S(1)}, bf16[64,1024]{1,0:T(8,128)(2,1)S(1)}, u32[]{:S(2)}, u32[]{:S(2)}) collective-permute-start(bf16[64,1024]{1,0:T(8,128)(2,1)S(1)} %collective-permute-done.2.refs_7_.refs_6_), channel_id=1, source_target_pairs={{0,4},{4,0},{8,12},{12,8},{16,20},{20,16},{24,28},{28,24},{1,5},{5... | collective-permute-start | bytes 393224 | tf_op jit(solution)/shard_map/ppermute | solution.py:29
  18.4 2.9 %collective-permute-start.7 = (bf16[4,2,64,512]{3,2,1,0:T(8,128)(2,1)S(1)}, bf16[4,2,64,512]{3,2,1,0:T(8,128)(2,1)S(1)}, u32[]{:S(2)}, u32[]{:S(2)}) collective-permute-start(bf16[4,2,64,512]{3,2,1,0:T(8,128)(2,1)S(1)} %get-tuple-element.70), channel_id=1, source_target_pairs={{0,4},{4,0},{8,12},{12,8},{16,20},{20,16},{24,28},{28,24},{1,5},{5... | collective-permute-start | bytes 1572872 | tf_op jit(solution)/shard_map/ppermute | solution.py:29
  18.8 6.2 %copy-start = (bf16[1,128,512]{2,1,0:T(8,128)(2,1)S(1)}, bf16[1,128,512]{2,1,0:T(8,128)(2,1)}, u32[]{:S(2)}) copy-start(bf16[1,128,512]{2,1,0:T(8,128)(2,1)} %param.19) | copy-start | bytes 393220
  18.8 6.2 %copy-start.1 = (bf16[1,128,512]{2,1,0:T(8,128)(2,1)S(1)}, bf16[1,128,512]{2,1,0:T(8,128)(2,1)}, u32[]{:S(2)}) copy-start(bf16[1,128,512]{2,1,0:T(8,128)(2,1)} %param.20) | copy-start | bytes 393220
  21.4 8.2 %collective-permute-start.10 = (bf16[2,64,512]{2,1,0:T(8,128)(2,1)S(1)}, bf16[2,64,512]{2,1,0:T(8,128)(2,1)S(1)}, u32[]{:S(2)}, u32[]{:S(2)}) collective-permute-start(bf16[2,64,512]{2,1,0:T(8,128)(2,1)S(1)} %get-tuple-element.77), channel_id=1, source_target_pairs={{0,3},{1,2},{2,1},{3,0},{4,7},{5,6},{6,5},{7,4},{8,11},{9,10},{10,... | collective-permute-start | bytes 393224 | tf_op jit(solution)/shard_map/ppermute | solution.py:29
  22.9 7.9 %collective-permute-start.8 = (bf16[2,64,512]{2,1,0:T(8,128)(2,1)S(1)}, bf16[2,64,512]{2,1,0:T(8,128)(2,1)S(1)}, u32[]{:S(2)}, u32[]{:S(2)}) collective-permute-start(bf16[2,64,512]{2,1,0:T(8,128)(2,1)S(1)} %get-tuple-element.76), channel_id=1, source_target_pairs={{0,1},{1,0},{2,3},{3,2},{4,5},{5,4},{6,7},{7,6},{8,9},{9,8},{10,11... | collective-permute-start | bytes 393224 | tf_op jit(solution)/shard_map/ppermute | solution.py:29
  24.4 6.4 %collective-permute-start.9 = (bf16[2,64,512]{2,1,0:T(8,128)(2,1)S(1)}, bf16[2,64,512]{2,1,0:T(8,128)(2,1)S(1)}, u32[]{:S(2)}, u32[]{:S(2)}) collective-permute-start(bf16[2,64,512]{2,1,0:T(8,128)(2,1)S(1)} %get-tuple-element.78), channel_id=1, source_target_pairs={{0,2},{1,3},{2,0},{3,1},{4,6},{5,7},{6,4},{7,5},{8,10},{9,11},{10,... | collective-permute-start | bytes 393224 | tf_op jit(solution)/shard_map/ppermute | solution.py:29

commit v4 on v3

--- a/solution.py
+++ b/solution.py
@@ -13,6 +13,7 @@
 LOG2E = 1.4426950408889634
 BLOCKED = -1e30
 LONG = 512
+ORDER = (3, 2, 1)
 BF16 = jnp.bfloat16
 F32 = jnp.float32
 NN = (((1,), (0,)), ((), ()))
@@ -62,22 +63,18 @@
     )
 
 
-def masked(scores, bias):
-    return scores * (SCALE * LOG2E) + jnp.concatenate([bias] * (scores.shape[1] // DH), axis=1)
-
-
 def prepare_kernel(
-    count, prompt_table, len_table, host_table, q_p, g_p, q_r, g_r, k_r, v_r,
-    qg_p, qg_r, bias_p, bias_r, own_e, own_d, own_s, keep_p, keep_r, chosen,
-    buf_qp, buf_gp, buf_qr, buf_gr, buf_k, buf_v, prompt_len, resp_len, resp_host, sems,
+    count, prompt_table, len_table, host_table, q_p, g_p, q_r, g_r,
+    qp_x, gp_x, gp_m, qr_x, gr_x, gr_m, mask_p, mask_r, mask_own, keep_p, keep_r, chosen,
+    buf_qp, buf_gp, buf_qr, buf_gr, prompt_len, resp_len, resp_host, sems,
 ):
-    buffers = (buf_qr, buf_gr, buf_k, buf_v, buf_qp, buf_gp)
+    buffers = (buf_qr, buf_gr, buf_qp, buf_gp)
     copies = [
         pltpu.make_async_copy(src, dst, sems.at[i])
-        for i, (src, dst) in enumerate(zip((q_r, g_r, k_r, v_r, q_p, g_p), buffers))
+        for i, (src, dst) in enumerate(zip((q_r, g_r, q_p, g_p), buffers))
     ]
     tables = [
-        pltpu.make_async_copy(src, dst, sems.at[6 + i])
+        pltpu.make_async_copy(src, dst, sems.at[4 + i])
         for i, (src, dst) in enumerate(
             ((prompt_table, prompt_len), (len_table, resp_len), (host_table, resp_host))
         )
@@ -95,11 +92,16 @@
     key = lax.broadcasted_iota(jnp.int32, (span, DH), 0)
     place = ((key // rows) ^ shard) * rows + key % rows
     lane = lax.broadcasted_iota(jnp.int32, (span, DH), 1)
-    bias_p[...] = jnp.where(place <= lane % rows + shard * rows, 0.0, BLOCKED)
-    bias_r[...] = jnp.where(place < owner_length, 0.0, BLOCKED)
+    blocked_p = (place > lane + shard * rows) & (lane < rows)
+    mask_p[...] = jnp.where(blocked_p, BLOCKED, 0.0).astype(BF16)
+    mask_r[...] = jnp.where(place >= owner_length, BLOCKED, 0.0).astype(BF16)
     key = lax.broadcasted_iota(jnp.int32, (slots, DH), 0)
     lane = lax.broadcasted_iota(jnp.int32, (slots, DH), 1)
-    bias_own = jnp.where(key <= lane % slots, 0.0, BLOCKED)
+    mask_own[...] = jnp.where((key > lane) & (lane < slots), BLOCKED, 0.0).astype(BF16)
+    hot_r = jnp.where(key == lane, 1.0, 0.0).astype(BF16)
+    key = lax.broadcasted_iota(jnp.int32, (rows, DH), 0)
+    lane = lax.broadcasted_iota(jnp.int32, (rows, DH), 1)
+    hot_p = jnp.where(key == lane, 1.0, 0.0).astype(BF16)
     chosen[...] = jnp.zeros(chosen.shape, F32) + jnp.where(owner == group, 1.0, 0.0)
     lane = lax.broadcasted_iota(jnp.int32, keep_p.shape, 1)
     keep_p[...] = jnp.where(lane % rows + shard * rows < own_length, 1.0, 0.0)
@@ -107,141 +109,194 @@
     keep_r[...] = jnp.where(lane % slots < resp_length, 1.0, 0.0)
     live_p = lax.broadcasted_iota(jnp.int32, (rows, 1), 0) + shard * rows < own_length
     live_r = lax.broadcasted_iota(jnp.int32, (slots, 1), 0) < resp_length
-    for copy in copies[:4]:
+    def lay(c, height, q, g, live, hot, to_q, to_g, to_m):
+        for h in range(PER):
+            to, at = slice(h * height, (h + 1) * height), lanes(c * PER + h)
+            to_q[c, to, :DH] = q[:, at]
+            to_q[c, to, DH:] = hot
+            kept = jnp.where(live, g[:, at], 0)
+            to_m[c, to] = kept
+            scaled = kept.astype(F32) * SCALE
+            high = scaled.astype(BF16)
+            to_g[c, to, :DH] = high
+            to_g[c, to, DH:] = (scaled - high.astype(F32)).astype(BF16)
+
+    for copy in copies[:2]:
         copy.wait()
     for c in range(KVH):
-        for h in range(PER):
-            to, at = slice(h * slots, (h + 1) * slots), lanes(c * PER + h)
-            qg_r[c, to, :DH] = buf_qr[:, at]
-            qg_r[c, to, DH:] = jnp.where(live_r, buf_gr[:, at], 0)
-        both = dot(beside(buf_k[:, lanes(c)], buf_v[:, lanes(c)]), qg_r[c], NT)
-        scores, dprob = masked(both[:slots], bias_own), both[slots:]
-        top = jnp.max(scores, axis=0, keepdims=True)
-        raised = jnp.exp2(scores - top)
-        own_e[c] = raised
-        own_d[c] = dprob
-        own_s[c, 0:1] = top
-        own_s[c, 1:2] = jnp.sum(raised, axis=0, keepdims=True)
-        own_s[c, 2:3] = jnp.sum(raised * dprob, axis=0, keepdims=True)
-    for copy in copies[4:]:
+        lay(c, slots, buf_qr, buf_gr, live_r, hot_r, qr_x, gr_x, gr_m)
+    for copy in copies[2:]:
         copy.wait()
     for c in range(KVH):
-        for h in range(PER):
-            to, at = slice(h * rows, (h + 1) * rows), lanes(c * PER + h)
-            qg_p[c, to, :DH] = buf_qp[:, at]
-            qg_p[c, to, DH:] = jnp.where(live_p, buf_gp[:, at], 0)
-
-
-def response_kernel(count, *refs):
-    qg, bias, own_s, chosen = refs[:4]
-    own_kv, pair_kv = refs[4 : 4 + count], refs[4 + count : 4 + 2 * count]
-    probs_c, dscore_c, keys, values, own_t, near, far, scores = refs[4 + 2 * count :]
-    piece = own_kv[0].shape[0]
-    span = count * piece
+        lay(c, rows, buf_qp, buf_gp, live_p, hot_p, qp_x, gp_x, gp_m)
+
+
+def in_turn(*stages):
+    stages[0](0)
+    for c in range(KVH):
+        if c + 1 < KVH:
+            stages[0](c + 1)
+        for stage in stages[1:]:
+            stage(c)
+
+
+def chosen_pieces(chosen, own, pair, c, to, skip=0):
+    own_half, pair_half = chosen[0:1, :].astype(BF16), (1.0 - chosen[0:1, :]).astype(BF16)
+    piece = own[0].shape[0]
+    for d in range(len(own)):
+        to[c, d * piece : (d + 1) * piece] = (
+            own[d][:, lanes(skip + c)] * own_half + pair[d][:, lanes(skip + c)] * pair_half
+        )
+
+
+def halves(block):
+    return jnp.concatenate([block, block], axis=1)
+
+
+def early_kernel(count, q_x, g_x, mask_r, mask_own, chosen, k_r, v_r, *refs):
+    own, pair = refs[:count], refs[count : 2 * count]
+    keys, values, raised_a, dprob_a, stats, scores = refs[2 * count :]
+    span = keys.shape[1]
+
+    def first(c):
+        chosen_pieces(chosen, own, pair, c, keys)
+        chosen_pieces(chosen, own, pair, c, values, KVH)
+        key = jnp.concatenate([k_r[:, lanes(c)], keys[c]], axis=0)
+        mask = jnp.concatenate([mask_own[...], mask_r[:span]], axis=0)
+        value = jnp.concatenate([v_r[:, lanes(c)], values[c]], axis=0)
+        scores[c % 2] = dot(jnp.concatenate([key, mask], axis=1), q_x[c], NT)
+        dprob_a[c] = dot(halves(value), g_x[c], NT)
+
+    def second(c):
+        block = scores[c % 2] * (SCALE * LOG2E)
+        top = jnp.max(block, axis=0, keepdims=True)
+        raised = jnp.exp2(block - top)
+        raised_a[c] = raised
+        stats[c, 0:1] = top
+        stats[c, 1:2] = jnp.sum(raised, axis=0, keepdims=True)
+        stats[c, 2:3] = jnp.sum(raised * dprob_a[c], axis=0, keepdims=True)
+
+    in_turn(first, second)
+
+
+def response_kernel(count, q_x, g_x, g_m, mask_r, stats, raised_a, dprob_a, chosen, *refs):
+    own, pair = refs[:count], refs[count : 2 * count]
+    probs_c, dscore_c, keys, values, own_t, near, far, scores = refs[2 * count :]
+    piece = own[0].shape[0]
+    late = count * piece
+    early = probs_c.shape[1] - late
+    slots = raised_a.shape[1] - early
     is_own = chosen[0:1, :]
     is_pair = 1.0 - is_own
-    own_half, pair_half = is_own.astype(BF16), is_pair.astype(BF16)
 
     def first(c):
-        for d in range(count):
-            part = slice(d * piece, (d + 1) * piece)
-            for to, at in ((keys, lanes(c)), (values, lanes(KVH + c))):
-                to[c, part] = own_kv[d][:, at] * own_half + pair_kv[d][:, at] * pair_half
-        scores[c % 2, :span] = dot(keys[c], qg[c, :, :DH], NT)
-        scores[c % 2, span:] = dot(values[c], qg[c, :, DH:], NT)
+        chosen_pieces(chosen, own, pair, c, keys)
+        chosen_pieces(chosen, own, pair, c, values, KVH)
+        scores[c % 2, :late] = dot(jnp.concatenate([keys[c], mask_r[early:]], axis=1), q_x[c], NT)
+        scores[c % 2, late:] = dot(halves(values[c]), g_x[c], NT)
 
     def second(c):
-        block = masked(scores[c % 2, :span], bias[...])
-        own_top = own_s[c, 0:1]
-        top = jnp.maximum(jnp.max(block, axis=0, keepdims=True), own_top)
+        block = scores[c % 2, :late] * (SCALE * LOG2E)
+        early_top = stats[c, 0:1]
+        top = jnp.maximum(jnp.max(block, axis=0, keepdims=True), early_top)
         raised = jnp.exp2(block - top)
-        own_raised = jnp.exp2(own_top - top)
-        total = jnp.sum(raised, axis=0, keepdims=True) + own_raised * own_s[c, 1:2]
+        early_raised = jnp.exp2(early_top - top)
+        total = jnp.sum(raised, axis=0, keepdims=True) + early_raised * stats[c, 1:2]
         inverse = 1.0 / total
+        factor = early_raised * inverse
         probs = raised * inverse
-        weighted = probs * scores[c % 2, span:]
-        own_factor = own_raised * inverse
-        delta = jnp.sum(weighted, axis=0, keepdims=True) + own_factor * own_s[c, 2:3]
-        probs_c[c] = probs.astype(BF16)
-        dscore_c[c] = ((weighted - probs * delta) * SCALE).astype(BF16)
-        own_t[c, 0:1] = own_factor
+        weighted = probs * scores[c % 2, late:]
+        delta = jnp.sum(weighted, axis=0, keepdims=True) + factor * stats[c, 2:3]
+        probs_c[c, early:] = probs.astype(BF16)
+        dscore_c[c, early:] = (weighted - probs * delta).astype(BF16)
+        probs = raised_a[c, slots:] * factor
+        probs_c[c, :early] = probs.astype(BF16)
+        dscore_c[c, :early] = (probs * (dprob_a[c, slots:] - delta)).astype(BF16)
+        own_t[c, 0:1] = factor
         own_t[c, 1:2] = delta
 
     def third(c):
-        grad_k = dot(dscore_c[c], qg[c, :, :DH])
-        grad_v = dot(probs_c[c], qg[c, :, DH:])
-        for d in range(count):
+        grad_k = dot(dscore_c[c], q_x[c, :, :DH])
+        grad_v = dot(probs_c[c], g_m[c])
+        for d in range((early + late) // piece):
             part = slice(d * piece, (d + 1) * piece)
             for i, grad in enumerate((grad_k[part], grad_v[part])):
                 near[d, i, :, lanes(c)] = grad * is_own
                 far[d, i, :, lanes(c)] = (grad * is_pair).astype(BF16)
 
-    first(0)
-    for c in range(KVH):
-        if c + 1 < KVH:
-            first(c + 1)
-        second(c)
-        third(c)
-
-
-def prompt_kernel(count, qg, bias, near_r, *refs):
+    in_turn(first, second, third)
+
+
+def prompt_probs_kernel(count, q_x, g_m, mask, *refs):
     own_kv = refs[:count]
-    probs_c, dscore_c, keys, values, *near, scores = refs[count:]
+    exact, probs_p, keys, near, scores = refs[count:]
     piece = own_kv[0].shape[0]
-    span = count * piece
 
     def first(c):
         for d in range(count):
-            part = slice(d * piece, (d + 1) * piece)
-            keys[c, part] = own_kv[d][:, lanes(c)]
-            values[c, part] = own_kv[d][:, lanes(KVH + c)]
-        scores[c % 2, :span] = dot(keys[c], qg[c, :, :DH], NT)
-        scores[c % 2, span:] = dot(values[c], qg[c, :, DH:], NT)
+            keys[c, d * piece : (d + 1) * piece] = own_kv[d][:, lanes(c)]
+        scores[c % 2] = dot(jnp.concatenate([keys[c], mask[...]], axis=1), q_x[c], NT)
 
     def second(c):
-        block = masked(scores[c % 2, :span], bias[...])
+        block = scores[c % 2] * (SCALE * LOG2E)
         raised = jnp.exp2(block - jnp.max(block, axis=0, keepdims=True))
         probs = raised * (1.0 / jnp.sum(raised, axis=0, keepdims=True))
-        weighted = probs * scores[c % 2, span:]
+        exact[c] = probs
+        probs_p[c] = probs.astype(BF16)
+
+    def third(c):
+        grad = dot(probs_p[c], g_m[c])
+        for d in range(count):
+            near[d, :, lanes(c)] = grad[d * piece : (d + 1) * piece]
+
+    in_turn(first, second, third)
+
+
+def prompt_grads_kernel(count, q_x, g_x, exact, near_v, near_r, *refs):
+    own_kv = refs[:count]
+    dscore_p, values, *near, dprob = refs[count:]
+    piece = own_kv[0].shape[0]
+
+    def first(c):
+        for d in range(count):
+            values[c, d * piece : (d + 1) * piece] = own_kv[d][:, lanes(KVH + c)]
+        dprob[c % 2] = dot(jnp.concatenate([values[c], values[c]], axis=1), g_x[c], NT)
+
+    def second(c):
+        probs = exact[c]
+        weighted = probs * dprob[c % 2]
         delta = jnp.sum(weighted, axis=0, keepdims=True)
-        probs_c[c] = probs.astype(BF16)
-        dscore_c[c] = ((weighted - probs * delta) * SCALE).astype(BF16)
+        dscore_p[c] = (weighted - probs * delta).astype(BF16)
 
     def third(c):
-        grad_k = dot(dscore_c[c], qg[c, :, :DH])
-        grad_v = dot(probs_c[c], qg[c, :, DH:])
+        grad = dot(dscore_p[c], q_x[c, :, :DH])
         for d in range(count):
-            part = slice(d * piece, (d + 1) * piece)
-            for i, grad in enumerate((grad_k[part], grad_v[part])):
-                near[d][i, :, lanes(c)] = near_r[d, i, :, lanes(c)] + grad
-
-    first(0)
-    for c in range(KVH):
-        if c + 1 < KVH:
-            first(c + 1)
-        second(c)
-        third(c)
+            part = grad[d * piece : (d + 1) * piece]
+            near[d][0, :, lanes(c)] = near_r[d, 0, :, lanes(c)] + part
+            near[d][1, :, lanes(c)] = near_r[d, 1, :, lanes(c)] + near_v[d, :, lanes(c)]
+
+    in_turn(first, second, third)
 
 
 def finish_kernel(
-    keep_p, probs_p, dscore_p, keys_p, values_p, keep_r, probs_c, dscore_c, keys_c, values_c,
-    own_e, own_d, own_t, k_r, v_r, qg_r, out_p, dq_p, out_r, dq_r, dk_r, dv_r,
+    keep_p, probs_p, dscore_p, keys_p, values_p, keep_r, probs_c, dscore_c, keys_a, values_a,
+    keys_b, values_b, raised_a, dprob_a, own_t, k_r, v_r, q_x, g_m, out_p, dq_p, out_r, dq_r, dk_r, dv_r,
 ):
     c = pl.program_id(0)
     own_factor, delta = own_t[c, 0:1], own_t[c, 1:2]
-    probs = own_e[c] * own_factor
-    dscore = (probs * (own_d[c] - delta) * SCALE).astype(BF16)
+    slots = k_r.shape[0]
+    probs = raised_a[c, :slots] * own_factor
+    dscore = (probs * (dprob_a[c, :slots] - delta)).astype(BF16)
     probs = probs.astype(BF16)
-    dv_r[...] = dot(probs, qg_r[c, :, DH:]).astype(BF16)
-    dk_r[...] = dot(dscore, qg_r[c, :, :DH]).astype(BF16)
+    dv_r[...] = dot(probs, g_m[c]).astype(BF16)
+    dk_r[...] = dot(dscore, q_x[c, :, :DH]).astype(BF16)
 
     def across(block):
         return wide(block.astype(BF16).T)
 
-    left = beside(values_c[c], keys_c[c])
-    span = keys_c.shape[1]
-    own = beside(v_r[...], k_r[...])
-    left = jnp.concatenate([left[:span], own, left[span:]], axis=0)
+    values = jnp.concatenate([values_a[c], values_b[c], v_r[...]], axis=0)
+    keys = jnp.concatenate([k_r[...], keys_a[c], keys_b[c]], axis=0)
+    left = beside(values, keys)
     right = jnp.concatenate([probs_c[c], probs, dscore, dscore_c[c]], axis=0)
     both = dot(left, right, TN)
     out_r[...] = across(both[:DH] * keep_r[0:1])
@@ -365,10 +420,12 @@
 
 
 def summed(near, back):
+    parts = {}
+    for d in range(1, len(near)):
+        parts[d] = swapped((near[d] + back[d].astype(F32)).astype(BF16), "seq", d)
     total = near[0] + back[0].astype(F32)
-    for d in range(1, len(near)):
-        part = (near[d] + back[d].astype(F32)).astype(BF16)
-        total = total + swapped(part, "seq", d).astype(F32)
+    for d in ORDER if len(near) == 4 else parts:
+        total = total + parts[d].astype(F32)
     return total.astype(BF16)
 
 
@@ -413,7 +470,7 @@
 
     mine = jnp.concatenate([k_prompt[0], v_prompt[0]], axis=1)
     own = [mine] + [swapped(mine, "seq", d) for d in range(1, count)]
-    if span > LONG:
+    if span > LONG or max(rows, slots) > DH:
         pair = [swapped(part, "grp", 1) for part in own]
         out_p, dq_p, out_r, dq_r, dk_r, dv_r, far, *near = long_prompts(
             prompt_len, resp_len, resp_host, q_prompt[0], g_prompt[0], q_resp[0], g_resp[0],
@@ -424,67 +481,99 @@
 
     made = pl.pallas_call(
         lambda *refs: prepare_kernel(count, *refs),
-        in_specs=[hbm] * 9,
-        out_specs=[vmem] * 10,
-        out_shape=[
-            inside(KVH, PER * rows, 2 * DH),
-            inside(KVH, PER * slots, 2 * DH),
-            inside(span, DH, dtype=F32),
-            inside(span, DH, dtype=F32),
-            inside(KVH, slots, PER * slots, dtype=F32),
-            inside(KVH, slots, PER * slots, dtype=F32),
-            inside(KVH, 8, PER * slots, dtype=F32),
+        in_specs=[hbm] * 7,
+        out_specs=[vmem] * 12,
+        out_shape=[inside(KVH, PER * rows, 2 * DH)] * 2
+        + [inside(KVH, PER * rows, DH)]
+        + [inside(KVH, PER * slots, 2 * DH)] * 2
+        + [inside(KVH, PER * slots, DH)]
+        + [inside(span, DH)] * 2
+        + [
+            inside(slots, DH),
             inside(8, PER * rows, dtype=F32),
             inside(8, PER * slots, dtype=F32),
             inside(8, DH, dtype=F32),
         ],
         scratch_shapes=[pltpu.VMEM((rows, HQ * DH), BF16)] * 2
         + [pltpu.VMEM((slots, HQ * DH), BF16)] * 2
-        + [pltpu.VMEM((slots, width), BF16)] * 2
         + [pltpu.SMEM(t.shape, jnp.int32) for t in (prompt_len, resp_len, resp_host)]
-        + [pltpu.SemaphoreType.DMA((9,))],
+        + [pltpu.SemaphoreType.DMA((7,))],
         compiler_params=options(20),
         cost_estimate=cost(4 * 10**9),
         name="prepare",
     )(
         held(prompt_len), held(resp_len), held(resp_host),
         held(q_prompt[0]), held(g_prompt[0]), held(q_resp[0]), held(g_resp[0]),
-        held(k_resp[0]), held(v_resp[0]),
-    )
-    qg_p, qg_r, bias_p, bias_r, own_e, own_d, own_s, keep_p, keep_r, chosen = made
-
-    own[1:] = [lax.optimization_barrier((part, chosen))[0] for part in own[1:]]
-    pair = [swapped(part, "grp", 1) for part in own]
-    probs_c, dscore_c, keys_c, values_c, own_t, near_r, far = pl.pallas_call(
-        lambda *refs: response_kernel(count, *refs),
-        in_specs=[vmem] * (4 + 2 * count),
+    )
+    qp_x, gp_x, gp_m, qr_x, gr_x, gr_m, mask_p, mask_r, mask_own, *rest = made
+    keep_p, keep_r, chosen = rest
+
+    here = 1
+    pair = [swapped(part, "grp", 1) for part in own[:here]]
+    keys_a, values_a, raised_a, dprob_a, stats = pl.pallas_call(
+        lambda *refs: early_kernel(here, *refs),
+        in_specs=[vmem] * (7 + 2 * here),
+        out_specs=[vmem] * 5,
+        out_shape=[inside(KVH, here * rows, DH)] * 2
+        + [inside(KVH, slots + here * rows, PER * slots, dtype=F32)] * 2
+        + [inside(KVH, 8, PER * slots, dtype=F32)],
+        scratch_shapes=[pltpu.VMEM((2, slots + here * rows, PER * slots), F32)],
+        compiler_params=options(16),
+        cost_estimate=cost(3 * 10**9),
+        name="early",
+    )(qr_x, gr_x, mask_r, mask_own, chosen, k_resp[0], v_resp[0], *own[:here], *pair)
+    own[here:] = [lax.optimization_barrier((part, stats))[0] for part in own[here:]]
+    pair += [swapped(part, "grp", 1) for part in own[here:]]
+
+    exact, probs_p, keys_p, near_v = pl.pallas_call(
+        lambda *refs: prompt_probs_kernel(count, *refs),
+        in_specs=[vmem] * (3 + count),
+        out_specs=[vmem] * 4,
+        out_shape=[
+            inside(KVH, span, PER * rows, dtype=F32),
+            inside(KVH, span, PER * rows),
+            inside(KVH, span, DH),
+            inside(count, rows, width, dtype=F32),
+        ],
+        scratch_shapes=[pltpu.VMEM((2, span, PER * rows), F32)],
+        compiler_params=options(12),
+        cost_estimate=cost(2 * 10**9),
+        name="prompt_probs",
+    )(qp_x, gp_m, mask_p, *own)
+
+    stats, near_v = lax.optimization_barrier((stats, near_v))
+    late = count - here
+    probs_c, dscore_c, keys_b, values_b, own_t, near_r, far = pl.pallas_call(
+        lambda *refs: response_kernel(late, *refs),
+        in_specs=[vmem] * (8 + 2 * late),
         out_specs=[vmem] * 7,
         out_shape=[inside(KVH, span, PER * slots)] * 2
-        + [inside(KVH, span, DH)] * 2
+        + [inside(KVH, late * rows, DH)] * 2
         + [
             inside(KVH, 8, PER * slots, dtype=F32),
             inside(count, 2, rows, width, dtype=F32),
             inside(count, 2, rows, width),
         ],
-        scratch_shapes=[pltpu.VMEM((2, 2 * span, PER * slots), F32)],
+        scratch_shapes=[pltpu.VMEM((2, 2 * late * rows, PER * slots), F32)],
         compiler_params=options(20),
         cost_estimate=cost(3 * 10**9),
         name="responses",
-    )(qg_r, bias_r, own_s, chosen, *own, *pair)
+    )(
+        qr_x, gr_x, gr_m, mask_r, stats, raised_a, dprob_a, chosen, *own[here:], *pair[here:]
+    )
     back = swapped(far, "grp", 1)
 
-    probs_p, dscore_p, keys_p, values_p, *near = pl.pallas_call(
-        lambda *refs: prompt_kernel(count, *refs),
-        in_specs=[vmem] * (3 + count),
-        out_specs=[vmem] * (4 + count),
-        out_shape=[inside(KVH, span, PER * rows)] * 2
-        + [inside(KVH, span, DH)] * 2
+    dscore_p, values_p, *near = pl.pallas_call(
+        lambda *refs: prompt_grads_kernel(count, *refs),
+        in_specs=[vmem] * (5 + count),
+        out_specs=[vmem] * (2 + count),
+        out_shape=[inside(KVH, span, PER * rows), inside(KVH, span, DH)]
         + [inside(2, rows, width, dtype=F32)] * count,
-        scratch_shapes=[pltpu.VMEM((2, 2 * span, PER * rows), F32)],
-        compiler_params=options(20),
+        scratch_shapes=[pltpu.VMEM((2, span, PER * rows), F32)],
+        compiler_params=options(12),
         cost_estimate=cost(2 * 10**9),
-        name="prompts",
-    )(qg_p, bias_p, near_r, *own)
+        name="prompt_grads",
+    )(qp_x, gp_x, exact, near_v, near_r, *own)
 
     def block(height, extent):
         return pl.BlockSpec((height, extent), lambda c: (0, c))
@@ -493,7 +582,7 @@
     out_p, dq_p, out_r, dq_r, dk_r, dv_r = pl.pallas_call(
         finish_kernel,
         grid=(KVH,),
-        in_specs=[vmem] * 13 + [own_block] * 2 + [vmem],
+        in_specs=[vmem] * 15 + [own_block] * 2 + [vmem] * 2,
         out_specs=[wide_p, wide_p, wide_r, wide_r, own_block, own_block],
         out_shape=[jax.ShapeDtypeStruct((rows, HQ * DH), BF16)] * 2
         + [jax.ShapeDtypeStruct((slots, HQ * DH), BF16)] * 2
@@ -502,8 +591,8 @@
         cost_estimate=cost(8 * 10**9),
         name="finish",
     )(
-        keep_p, probs_p, dscore_p, keys_p, values_p, keep_r, probs_c, dscore_c, keys_c, values_c,
-        own_e, own_d, own_t, k_resp[0], v_resp[0], qg_r,
+        keep_p, probs_p, dscore_p, keys_p, values_p, keep_r, probs_c, dscore_c, keys_a, values_a,
+        keys_b, values_b, raised_a, dprob_a, own_t, k_resp[0], v_resp[0], qr_x, gr_m,
     )
     return collected(out_p, dq_p, out_r, dq_r, dk_r, dv_r, summed(near, back))
 

time: 31.7 us -> 31 us (0.978)
  waiting for transfers between devices: 4.63 us -> 2.39 us
  Pallas kernels: 14.9 us -> 16.7 us
  starting transfers between devices: 9.58 us -> 9.26 us
    ppermute x11, waiting for transfers between devices: 4.63 us -> 2.39 us  [swapped(): return lax.ppermute(block, axis, [(i, i ^ distance) for i in range(count)])]
    pallas_call x3 -> x5, Pallas kernels: 11.7 us -> 13.7 us  [the longest x1 4.7 us: shards(): pl.pallas_call(finish_kernel, grid=(KVH,), in_specs=[vmem] * 15 + [own_bl...]
    ppermute x11, starting transfers between devices: 9.58 us -> 9.26 us  [swapped(): return lax.ppermute(block, axis, [(i, i ^ distance) for i in range(count)])]
  transfers between devices with their start and end apart: 11 -> 11, of which waited for: 4 -> 4; matrix products, arithmetic and copies ran while one was open for 0% -> 0% of each run, Pallas kernels for 33% -> 41%
where the time goes in v4:
time: 31 us; the launch traced here: 30.9 us
  Pallas kernels  16.7 us (54%)
  starting transfers between devices  9.26 us (30%)
  waiting for transfers between devices  2.39 us (8%)
  other arithmetic  1.1 us (4%)
  between operations  0.74 us (2%)
  local copies, waits for them, and re-layouts  0.67 us (2%)
    ppermute x11, starting transfers between devices, swapped(): return lax.ppermute(block, axis, [(i, i ^ distance) for i in range(count)])  9.26 us
    pallas_call x1, Pallas kernels, shards(): pl.pallas_call(finish_kernel, grid=(KVH,), in_specs=[vmem] * 15 + [own_bl...  4.7 us
    pallas_call x1, Pallas kernels, shards(): pl.pallas_call(lambda *refs: response_kernel(late, *refs), in_specs=[vmem...  4.14 us
    pallas_call x1, Pallas kernels, shards(): pl.pallas_call(lambda *refs: prepare_kernel(count, *refs), in_specs=[hbm]...  3.03 us
    ppermute x11, waiting for transfers between devices, swapped(): return lax.ppermute(block, axis, [(i, i ^ distance) for i in range(count)])  2.39 us
    pallas_call x1, Pallas kernels, shards(): pl.pallas_call(lambda *refs: early_kernel(here, *refs), in_specs=[vmem] *...  1.96 us
    pallas_call x1, Pallas kernels, shards(): pl.pallas_call(lambda *refs: prompt_probs_kernel(count, *refs), in_specs=...  1.54 us
    pallas_call x1, Pallas kernels, shards(): pl.pallas_call(lambda *refs: prompt_grads_kernel(count, *refs), in_specs=...  1.34 us
  transfers between devices with their start and end apart: 11, of which 4 were waited for; matrix products, arithmetic and copies ran while one was open for 0% of the time, Pallas kernels for 41%

profile of v4, /device:TPU:0, one launch (start us, length us, event | category | flops | bytes accessed | tf_op | source)
XLA Modules:
  0.0 30.9 jit_solution(7044200844924345780)
XLA Ops:
  0.6 0.9 %pad_maximum_fusion.refs_7_.refs_3_.refs_5_ = bf16[64,1024]{1,0:T(8,128)(2,1)S(1)} fusion(bf16[64,512]{1,0:T(8,128)(2,1)} %bitcast.40, bf16[64,512]{1,0:T(8,128)(2,1)} %bitcast.41), kind=kLoop, calls=%fused_computation.15 | loop fusion | flops 262144 | bytes 262144 | tf_op jit(solution)/shard_map/concatenate | solution.py:471
  1.5 4.0 %collective-permute-start.3 = (bf16[64,1024]{1,0:T(8,128)(2,1)S(1)}, bf16[64,1024]{1,0:T(8,128)(2,1)S(1)}, u32[]{:S(2)}, u32[]{:S(2)}) collective-permute-start(bf16[64,1024]{1,0:T(8,128)(2,1)S(1)} %pad_maximum_fusion.refs_7_.refs_3_.refs_5_), channel_id=1, source_target_pairs={{0,3},{1,2},{2,1},{3,0},{4,7},{5,6},{6,5},{7,4},{8,11},{9,10},{10,... | collective-permute-start | bytes 393224 | tf_op jit(solution)/shard_map/ppermute | solution.py:30
  5.5 0.5 %collective-permute-start.2 = (bf16[64,1024]{1,0:T(8,128)(2,1)S(1)}, bf16[64,1024]{1,0:T(8,128)(2,1)S(1)}, u32[]{:S(2)}, u32[]{:S(2)}) collective-permute-start(bf16[64,1024]{1,0:T(8,128)(2,1)S(1)} %pad_maximum_fusion.refs_7_.refs_3_.refs_5_), channel_id=1, source_target_pairs={{0,2},{1,3},{2,0},{3,1},{4,6},{5,7},{6,4},{7,5},{8,10},{9,11},{10,... | collective-permute-start | bytes 393224 | tf_op jit(solution)/shard_map/ppermute | solution.py:30
  6.0 0.0 collective-permute-start.1
  6.0 0.1 collective-permute-start
  6.1 0.0 copy-start
  6.1 0.0 copy-start.1
  6.1 3.0 %prepare.1 = (bf16[4,512,256]{2,1,0:T(8,128)(2,1)S(1)}, bf16[4,512,256]{2,1,0:T(8,128)(2,1)S(1)}, bf16[4,512,128]{2,1,0:T(8,128)(2,1)S(1)}, bf16[4,1024,256]{2,1...) custom-call(s32[8]{0:T(128)} %refs_0_.1, ...), custom_call_target="tpu_custom_call" | custom-call | flops 4000000000 | bytes 1048576 | tf_op jit(solution)/shard_map/prepare/pallas_call | solution.py:482
  9.2 0.0 collective-permute-done.1.refs_8_
  9.2 0.0 copy-done
  9.2 0.0 copy-done.1
  9.2 2.0 %early.1 = (bf16[4,64,128]{2,1,0:T(8,128)(2,1)S(1)}, bf16[4,64,128]{2,1,0:T(8,128)(2,1)S(1)}, f32[4,192,1024]{2,1,0:T(8,128)S(1)}, f32[4,192,1024]{2,1,0:T(8,128)S(1)}, f32[4,8,1024]{2,1,0:T(8,128)S(1)}) custom-call(bf16[4,1024,256]{2,1,0:T(8,128)(2,1)S(1)} %get-tuple-element.57.refs_0_.q_x, bf16[4,1024,256]{2,1,0:T(8,128)(2,1)S(1)} %get-tuple-element.58.refs_1_, ...), custom_call_target="tpu_custom_call" | custom-call | flops 3000000000 | bytes 1048576 | tf_op jit(solution)/shard_map/early/pallas_call | solution.py:513
  11.2 0.0 collective-permute-done.3.refs_6_.refs_10_.refs_8_
  11.2 0.6 %collective-permute-done.2.refs_5_.refs_9_.refs_7_ = bf16[64,1024]{1,0:T(8,128)(2,1)S(1)} collective-permute-done((bf16[64,1024]{1,0:T(8,128)(2,1)S(1)}, bf16[64,1024]{1,0:T(8,128)(2,1)S(1)}, u32[]{:S(2)}, u32[]{:S(2)}) %collective-permute-start.2) | collective-permute-done | bytes 131104 | tf_op jit(solution)/shard_map/ppermute | solution.py:30
  11.8 0.3 collective-permute-done.refs_4_.refs_8_.refs_6_
  12.1 0.0 collective-permute-start.4
  12.1 0.5 %collective-permute-start.5 = (bf16[64,1024]{1,0:T(8,128)(2,1)S(1)}, bf16[64,1024]{1,0:T(8,128)(2,1)S(1)}, u32[]{:S(2)}, u32[]{:S(2)}) collective-permute-start(bf16[64,1024]{1,0:T(8,128)(2,1)S(1)} %collective-permute-done.2.refs_5_.refs_9_.refs_7_), channel_id=1, source_target_pairs={{0,4},{4,0},{8,12},{12,8},{16,20},{20,16},{24,28},{28,24},{1,5},{5... | collective-permute-start | bytes 393224 | tf_op jit(solution)/shard_map/ppermute | solution.py:30
  12.6 0.0 collective-permute-start.6
  12.6 1.5 %prompt_probs.1 = (f32[4,256,512]{2,1,0:T(8,128)S(1)}, bf16[4,256,512]{2,1,0:T(8,128)(2,1)S(1)}, bf16[4,256,128]{2,1,0:T(8,128)(2,1)S(1)}, f32[4,64,512]{2,1,0:T(8,128)S(1)}) custom-call(bf16[4,512,256]{2,1,0:T(8,128)(2,1)S(1)} %get-tuple-element.54.refs_0_, bf16[4,512,128]{2,1,0:T(8,128)(2,1)S(1)} %get-tuple-element.55.refs_1_, ...), custom_call_target="tpu_custom_call" | custom-call | flops 2000000000 | bytes 1048576 | tf_op jit(solution)/shard_map/prompt_probs/pallas_call | solution.py:528
  14.1 0.0 collective-permute-done.4.refs_11_
  14.1 0.0 collective-permute-done.5.refs_12_
  14.2 0.0 collective-permute-done.6.refs_13_
  14.2 4.1 %responses.1 = (bf16[4,256,1024]{2,1,0:T(8,128)(2,1)S(1)}, bf16[4,256,1024]{2,1,0:T(8,128)(2,1)S(1)}, bf16[4,192,128]{2,1,0:T(8,128)(2,1)S(1)}, bf16[4,192,128]{...) custom-call(bf16[4,1024,256]{2,1,0:T(8,128)(2,1)S(1)} %get-tuple-ele, ...), custom_call_target="tpu_custom_call" | custom-call | flops 3000000000 | bytes 1048576 | tf_op jit(solution)/shard_map/responses/pallas_call | solution.py:546
  18.3 0.6 %collective-permute-start.7 = (bf16[4,2,64,512]{3,2,1,0:T(8,128)(2,1)S(1)}, bf16[4,2,64,512]{3,2,1,0:T(8,128)(2,1)S(1)}, u32[]{:S(2)}, u32[]{:S(2)}) collective-permute-start(bf16[4,2,64,512]{3,2,1,0:T(8,128)(2,1)S(1)} %get-tuple-element.92), channel_id=1, source_target_pairs={{0,4},{4,0},{8,12},{12,8},{16,20},{20,16},{24,28},{28,24},{1,5},{5... | collective-permute-start | bytes 1572872 | tf_op jit(solution)/shard_map/ppermute | solution.py:30
  18.9 1.3 %prompt_grads.1 = (bf16[4,256,512]{2,1,0:T(8,128)(2,1)S(1)}, bf16[4,256,128]{2,1,0:T(8,128)(2,1)S(1)}, f32[2,64,512]{2,1,0:T(8,128)S(1)}, f32[2,64,512]{2,1,0:T(...) custom-call(bf16[4,512,256]{2,1,0:T(8,128)(2,1)S(1)} %get-tuple-element.54.refs_0_, ...), custom_call_target="tpu_custom_call" | custom-call | flops 2000000000 | bytes 1048576 | tf_op jit(solution)/shard_map/prompt_grads/pallas_call | solution.py:566
  20.2 0.2 collective-permute-done.7
  20.4 0.1 fusion.2
  20.6 2.2 %collective-permute-start.8 = (bf16[2,64,512]{2,1,0:T(8,128)(2,1)S(1)}, bf16[2,64,512]{2,1,0:T(8,128)(2,1)S(1)}, u32[]{:S(2)}, u32[]{:S(2)}) collective-permute-start(bf16[2,64,512]{2,1,0:T(8,128)(2,1)S(1)} %get-tuple-element.98), channel_id=1, source_target_pairs={{0,3},{1,2},{2,1},{3,0},{4,7},{5,6},{6,5},{7,4},{8,11},{9,10},{10,... | collective-permute-start | bytes 393224 | tf_op jit(solution)/shard_map/ppermute | solution.py:30
  22.7 0.8 %collective-permute-start.10 = (bf16[2,64,512]{2,1,0:T(8,128)(2,1)S(1)}, bf16[2,64,512]{2,1,0:T(8,128)(2,1)S(1)}, u32[]{:S(2)}, u32[]{:S(2)}) collective-permute-start(bf16[2,64,512]{2,1,0:T(8,128)(2,1)S(1)} %get-tuple-element.99), channel_id=1, source_target_pairs={{0,1},{1,0},{2,3},{3,2},{4,5},{5,4},{6,7},{7,6},{8,9},{9,8},{10,11... | collective-permute-start | bytes 393224 | tf_op jit(solution)/shard_map/ppermute | solution.py:30
  23.5 0.6 %collective-permute-start.9 = (bf16[2,64,512]{2,1,0:T(8,128)(2,1)S(1)}, bf16[2,64,512]{2,1,0:T(8,128)(2,1)S(1)}, u32[]{:S(2)}, u32[]{:S(2)}) collective-permute-start(bf16[2,64,512]{2,1,0:T(8,128)(2,1)S(1)} %get-tuple-element.100), channel_id=1, source_target_pairs={{0,2},{1,3},{2,0},{3,1},{4,6},{5,7},{6,4},{7,5},{8,10},{9,11},{10,... | collective-permute-start | bytes 393224 | tf_op jit(solution)/shard_map/ppermute | solution.py:30
  24.1 4.7 %finish.1 = (bf16[64,4096]{1,0:T(8,128)(2,1)}, bf16[64,4096]{1,0:T(8,128)(2,1)}, bf16[128,4096]{1,0:T(8,128)(2,1)}, bf16[128,4096]{1,0:T(8,128)(2,1)}, bf16[128,...) custom-call(f32[8,512]{1,0:T(8,128)S(1)} %get-tuple-element.53.keep_p, bf16[4,256,512]{2,1,0:T(8,128)(2,1)S(1)} %get-tuple-element.66.probs_p, ...), custom_call_target="tpu_custom_call" | custom-call | flops 8000000000 | bytes 1048576 | tf_op jit(solution)/shard_map/finish/pallas_call | solution.py:582
  28.8 0.0 collective-permute-done.8
  28.8 1.2 %collective-permute-done.10 = bf16[2,64,512]{2,1,0:T(8,128)(2,1)S(1)} collective-permute-done((bf16[2,64,512]{2,1,0:T(8,128)(2,1)S(1)}, bf16[2,64,512]{2,1,0:T(8,128)(2,1)S(1)}, u32[]{:S(2)}, u32[]{:S(2)}) %collective-permute-start.10) | collective-permute-done | bytes 131104 | tf_op jit(solution)/shard_map/ppermute | solution.py:30
  30.1 0.0 collective-permute-done.9
  30.1 0.1 fusion.6
  30.2 0.7 %fusion.7 = (bf16[1,64,512]{2,1,0:T(8,128)(2,1)}, bf16[1,64,512]{2,1,0:T(8,128)(2,1)}) fusion(bf16[2,64,512]{2,1,0:T(8,128)(2,1)S(1)} %fusion.6), kind=kLoop, calls=%fused_computation.16 | loop fusion | bytes 262144 | tf_op jit(solution)/shard_map/slice | solution.py:434
Async XLA Ops:
  1.5 9.6 %collective-permute-start.3 = (bf16[64,1024]{1,0:T(8,128)(2,1)S(1)}, bf16[64,1024]{1,0:T(8,128)(2,1)S(1)}, u32[]{:S(2)}, u32[]{:S(2)}) collective-permute-start(bf16[64,1024]{1,0:T(8,128)(2,1)S(1)} %pad_maximum_fusion.refs_7_.refs_3_.refs_5_), channel_id=1, source_target_pairs={{0,3},{1,2},{2,1},{3,0},{4,7},{5,6},{6,5},{7,4},{8,11},{9,10},{10,... | collective-permute-start | bytes 393224 | tf_op jit(solution)/shard_map/ppermute | solution.py:30
  5.5 6.3 %collective-permute-start.2 = (bf16[64,1024]{1,0:T(8,128)(2,1)S(1)}, bf16[64,1024]{1,0:T(8,128)(2,1)S(1)}, u32[]{:S(2)}, u32[]{:S(2)}) collective-permute-start(bf16[64,1024]{1,0:T(8,128)(2,1)S(1)} %pad_maximum_fusion.refs_7_.refs_3_.refs_5_), channel_id=1, source_target_pairs={{0,2},{1,3},{2,0},{3,1},{4,6},{5,7},{6,4},{7,5},{8,10},{9,11},{10,... | collective-permute-start | bytes 393224 | tf_op jit(solution)/shard_map/ppermute | solution.py:30
  6.0 3.2 %collective-permute-start.1 = (bf16[64,1024]{1,0:T(8,128)(2,1)S(1)}, bf16[64,1024]{1,0:T(8,128)(2,1)S(1)}, u32[]{:S(2)}, u32[]{:S(2)}) collective-permute-start(bf16[64,1024]{1,0:T(8,128)(2,1)S(1)} %pad_maximum_fusion.refs_7_.refs_3_.refs_5_), channel_id=1, source_target_pairs={{0,4},{4,0},{8,12},{12,8},{16,20},{20,16},{24,28},{28,24},{1,5},{5... | collective-permute-start | bytes 393224 | tf_op jit(solution)/shard_map/ppermute | solution.py:30
  6.0 6.1 %collective-permute-start = (bf16[64,1024]{1,0:T(8,128)(2,1)S(1)}, bf16[64,1024]{1,0:T(8,128)(2,1)S(1)}, u32[]{:S(2)}, u32[]{:S(2)}) collective-permute-start(bf16[64,1024]{1,0:T(8,128)(2,1)S(1)} %pad_maximum_fusion.refs_7_.refs_3_.refs_5_), channel_id=1, source_target_pairs={{0,1},{1,0},{2,3},{3,2},{4,5},{5,4},{6,7},{7,6},{8,9},{9,8},{10,11... | collective-permute-start | bytes 393224 | tf_op jit(solution)/shard_map/ppermute | solution.py:30
  6.1 3.1 %copy-start = (bf16[1,128,512]{2,1,0:T(8,128)(2,1)S(1)}, bf16[1,128,512]{2,1,0:T(8,128)(2,1)}, u32[]{:S(2)}) copy-start(bf16[1,128,512]{2,1,0:T(8,128)(2,1)} %param.19) | copy-start | bytes 393220
  6.1 3.1 %copy-start.1 = (bf16[1,128,512]{2,1,0:T(8,128)(2,1)S(1)}, bf16[1,128,512]{2,1,0:T(8,128)(2,1)}, u32[]{:S(2)}) copy-start(bf16[1,128,512]{2,1,0:T(8,128)(2,1)} %param.20) | copy-start | bytes 393220
  12.1 2.1 %collective-permute-start.4 = (bf16[64,1024]{1,0:T(8,128)(2,1)S(1)}, bf16[64,1024]{1,0:T(8,128)(2,1)S(1)}, u32[]{:S(2)}, u32[]{:S(2)}) collective-permute-start(bf16[64,1024]{1,0:T(8,128)(2,1)S(1)} %collective-permute-done.refs_4_.refs_8_.refs_6_), channel_id=1, source_target_pairs={{0,4},{4,0},{8,12},{12,8},{16,20},{20,16},{24,28},{28,24},{1,5},{5... | collective-permute-start | bytes 393224 | tf_op jit(solution)/shard_map/ppermute | solution.py:30
  12.1 2.1 %collective-permute-start.5 = (bf16[64,1024]{1,0:T(8,128)(2,1)S(1)}, bf16[64,1024]{1,0:T(8,128)(2,1)S(1)}, u32[]{:S(2)}, u32[]{:S(2)}) collective-permute-start(bf16[64,1024]{1,0:T(8,128)(2,1)S(1)} %collective-permute-done.2.refs_5_.refs_9_.refs_7_), channel_id=1, source_target_pairs={{0,4},{4,0},{8,12},{12,8},{16,20},{20,16},{24,28},{28,24},{1,5},{5... | collective-permute-start | bytes 393224 | tf_op jit(solution)/shard_map/ppermute | solution.py:30
  12.6 1.6 %collective-permute-start.6 = (bf16[64,1024]{1,0:T(8,128)(2,1)S(1)}, bf16[64,1024]{1,0:T(8,128)(2,1)S(1)}, u32[]{:S(2)}, u32[]{:S(2)}) collective-permute-start(bf16[64,1024]{1,0:T(8,128)(2,1)S(1)} %collective-permute-done.3.refs_6_.refs_10_.refs_8_), channel_id=1, source_target_pairs={{0,4},{4,0},{8,12},{12,8},{16,20},{20,16},{24,28},{28,24},{1,5},{5... | collective-permute-start | bytes 393224 | tf_op jit(solution)/shard_map/ppermute | solution.py:30
  18.3 2.1 %collective-permute-start.7 = (bf16[4,2,64,512]{3,2,1,0:T(8,128)(2,1)S(1)}, bf16[4,2,64,512]{3,2,1,0:T(8,128)(2,1)S(1)}, u32[]{:S(2)}, u32[]{:S(2)}) collective-permute-start(bf16[4,2,64,512]{3,2,1,0:T(8,128)(2,1)S(1)} %get-tuple-element.92), channel_id=1, source_target_pairs={{0,4},{4,0},{8,12},{12,8},{16,20},{20,16},{24,28},{28,24},{1,5},{5... | collective-permute-start | bytes 1572872 | tf_op jit(solution)/shard_map/ppermute | solution.py:30
  20.6 8.3 %collective-permute-start.8 = (bf16[2,64,512]{2,1,0:T(8,128)(2,1)S(1)}, bf16[2,64,512]{2,1,0:T(8,128)(2,1)S(1)}, u32[]{:S(2)}, u32[]{:S(2)}) collective-permute-start(bf16[2,64,512]{2,1,0:T(8,128)(2,1)S(1)} %get-tuple-element.98), channel_id=1, source_target_pairs={{0,3},{1,2},{2,1},{3,0},{4,7},{5,6},{6,5},{7,4},{8,11},{9,10},{10,... | collective-permute-start | bytes 393224 | tf_op jit(solution)/shard_map/ppermute | solution.py:30
  22.7 7.3 %collective-permute-start.10 = (bf16[2,64,512]{2,1,0:T(8,128)(2,1)S(1)}, bf16[2,64,512]{2,1,0:T(8,128)(2,1)S(1)}, u32[]{:S(2)}, u32[]{:S(2)}) collective-permute-start(bf16[2,64,512]{2,1,0:T(8,128)(2,1)S(1)} %get-tuple-element.99), channel_id=1, source_target_pairs={{0,1},{1,0},{2,3},{3,2},{4,5},{5,4},{6,7},{7,6},{8,9},{9,8},{10,11... | collective-permute-start | bytes 393224 | tf_op jit(solution)/shard_map/ppermute | solution.py:30
  23.5 6.6 %collective-permute-start.9 = (bf16[2,64,512]{2,1,0:T(8,128)(2,1)S(1)}, bf16[2,64,512]{2,1,0:T(8,128)(2,1)S(1)}, u32[]{:S(2)}, u32[]{:S(2)}) collective-permute-start(bf16[2,64,512]{2,1,0:T(8,128)(2,1)S(1)} %get-tuple-element.100), channel_id=1, source_target_pairs={{0,2},{1,3},{2,0},{3,1},{4,6},{5,7},{6,4},{7,5},{8,10},{9,11},{10,... | collective-permute-start | bytes 393224 | tf_op jit(solution)/shard_map/ppermute | solution.py:30

commit v5 on v4

--- a/solution.py
+++ b/solution.py
@@ -179,13 +179,12 @@
     in_turn(first, second)
 
 
-def response_kernel(count, q_x, g_x, g_m, mask_r, stats, raised_a, dprob_a, chosen, *refs):
+def response_kernel(count, q_x, g_x, g_m, mask_r, stats, chosen, *refs):
     own, pair = refs[:count], refs[count : 2 * count]
     probs_c, dscore_c, keys, values, own_t, near, far, scores = refs[2 * count :]
     piece = own[0].shape[0]
     late = count * piece
-    early = probs_c.shape[1] - late
-    slots = raised_a.shape[1] - early
+    early = mask_r.shape[0] - late
     is_own = chosen[0:1, :]
     is_pair = 1.0 - is_own
 
@@ -207,18 +206,15 @@
         probs = raised * inverse
         weighted = probs * scores[c % 2, late:]
         delta = jnp.sum(weighted, axis=0, keepdims=True) + factor * stats[c, 2:3]
-        probs_c[c, early:] = probs.astype(BF16)
-        dscore_c[c, early:] = (weighted - probs * delta).astype(BF16)
-        probs = raised_a[c, slots:] * factor
-        probs_c[c, :early] = probs.astype(BF16)
-        dscore_c[c, :early] = (probs * (dprob_a[c, slots:] - delta)).astype(BF16)
+        probs_c[c] = probs.astype(BF16)
+        dscore_c[c] = (weighted - probs * delta).astype(BF16)
         own_t[c, 0:1] = factor
         own_t[c, 1:2] = delta
 
     def third(c):
         grad_k = dot(dscore_c[c], q_x[c, :, :DH])
         grad_v = dot(probs_c[c], g_m[c])
-        for d in range((early + late) // piece):
+        for d in range(count):
             part = slice(d * piece, (d + 1) * piece)
             for i, grad in enumerate((grad_k[part], grad_v[part])):
                 near[d, i, :, lanes(c)] = grad * is_own
@@ -245,8 +241,8 @@
         probs_p[c] = probs.astype(BF16)
 
     def third(c):
-        grad = dot(probs_p[c], g_m[c])
-        for d in range(count):
+        grad = dot(probs_p[c, piece:], g_m[c])
+        for d in range(count - 1):
             near[d, :, lanes(c)] = grad[d * piece : (d + 1) * piece]
 
     in_turn(first, second, third)
@@ -269,13 +265,29 @@
         dscore_p[c] = (weighted - probs * delta).astype(BF16)
 
     def third(c):
-        grad = dot(dscore_p[c], q_x[c, :, :DH])
-        for d in range(count):
+        grad = dot(dscore_p[c, piece:], q_x[c, :, :DH])
+        for d in range(count - 1):
             part = grad[d * piece : (d + 1) * piece]
             near[d][0, :, lanes(c)] = near_r[d, 0, :, lanes(c)] + part
             near[d][1, :, lanes(c)] = near_r[d, 1, :, lanes(c)] + near_v[d, :, lanes(c)]
 
     in_turn(first, second, third)
+
+
+def first_piece_kernel(
+    probs_p, dscore_p, qp_x, gp_m, raised_a, dprob_a, own_t, qr_x, gr_m, chosen, near, far
+):
+    piece = near.shape[1]
+    slots = raised_a.shape[1] - piece
+    is_own = chosen[0:1, :]
+    for c in range(KVH):
+        probs = raised_a[c, slots:] * own_t[c, 0:1]
+        dscore = (probs * (dprob_a[c, slots:] - own_t[c, 1:2])).astype(BF16)
+        grads = dot(dscore, qr_x[c, :, :DH]), dot(probs.astype(BF16), gr_m[c])
+        own = dot(dscore_p[c, :piece], qp_x[c, :, :DH]), dot(probs_p[c, :piece], gp_m[c])
+        for i in range(2):
+            near[i, :, lanes(c)] = own[i] + grads[i] * is_own
+            far[i, :, lanes(c)] = (grads[i] * (1.0 - is_own)).astype(BF16)
 
 
 def finish_kernel(
@@ -285,19 +297,19 @@
     c = pl.program_id(0)
     own_factor, delta = own_t[c, 0:1], own_t[c, 1:2]
     slots = k_r.shape[0]
-    probs = raised_a[c, :slots] * own_factor
-    dscore = (probs * (dprob_a[c, :slots] - delta)).astype(BF16)
+    probs = raised_a[c] * own_factor
+    dscore = (probs * (dprob_a[c] - delta)).astype(BF16)
     probs = probs.astype(BF16)
-    dv_r[...] = dot(probs, g_m[c]).astype(BF16)
-    dk_r[...] = dot(dscore, q_x[c, :, :DH]).astype(BF16)
+    dv_r[...] = dot(probs[:slots], g_m[c]).astype(BF16)
+    dk_r[...] = dot(dscore[:slots], q_x[c, :, :DH]).astype(BF16)
 
     def across(block):
         return wide(block.astype(BF16).T)
 
-    values = jnp.concatenate([values_a[c], values_b[c], v_r[...]], axis=0)
+    values = jnp.concatenate([v_r[...], values_a[c], values_b[c]], axis=0)
     keys = jnp.concatenate([k_r[...], keys_a[c], keys_b[c]], axis=0)
     left = beside(values, keys)
-    right = jnp.concatenate([probs_c[c], probs, dscore, dscore_c[c]], axis=0)
+    right = jnp.concatenate([probs, probs_c[c], dscore, dscore_c[c]], axis=0)
     both = dot(left, right, TN)
     out_r[...] = across(both[:DH] * keep_r[0:1])
     dq_r[...] = across(both[DH:])
@@ -419,13 +431,17 @@
     )(prompt_len, resp_len, resp_host, q_p, g_p, q_r, g_r, k_r, v_r, *own, *own, *pair, *pair)
 
 
-def summed(near, back):
-    parts = {}
-    for d in range(1, len(near)):
-        parts[d] = swapped((near[d] + back[d].astype(F32)).astype(BF16), "seq", d)
-    total = near[0] + back[0].astype(F32)
-    for d in ORDER if len(near) == 4 else parts:
-        total = total + parts[d].astype(F32)
+def sent(near, back):
+    return [
+        swapped((a + back[d].astype(F32)).astype(BF16), "seq", d + 1) for d, a in enumerate(near)
+    ]
+
+
+def summed(near, back, parts):
+    total = near + back.astype(F32)
+    order = ORDER if len(parts) == len(ORDER) else range(1, len(parts) + 1)
+    for d in order:
+        total = total + parts[d - 1].astype(F32)
     return total.astype(BF16)
 
 
@@ -476,7 +492,8 @@
             prompt_len, resp_len, resp_host, q_prompt[0], g_prompt[0], q_resp[0], g_resp[0],
             k_resp[0], v_resp[0], own, pair,
         )
-        total = summed(near, swapped(far, "grp", 1))
+        back = swapped(far, "grp", 1)
+        total = summed(near[0], back[0], sent(near[1:], back[1:]))
         return collected(out_p, dq_p, out_r, dq_r, dk_r, dv_r, total)
 
     made = pl.pallas_call(
@@ -533,7 +550,7 @@
             inside(KVH, span, PER * rows, dtype=F32),
             inside(KVH, span, PER * rows),
             inside(KVH, span, DH),
-            inside(count, rows, width, dtype=F32),
+            inside(count - 1, rows, width, dtype=F32),
         ],
         scratch_shapes=[pltpu.VMEM((2, span, PER * rows), F32)],
         compiler_params=options(12),
@@ -545,35 +562,48 @@
     late = count - here
     probs_c, dscore_c, keys_b, values_b, own_t, near_r, far = pl.pallas_call(
         lambda *refs: response_kernel(late, *refs),
-        in_specs=[vmem] * (8 + 2 * late),
+        in_specs=[vmem] * (6 + 2 * late),
         out_specs=[vmem] * 7,
-        out_shape=[inside(KVH, span, PER * slots)] * 2
+        out_shape=[inside(KVH, late * rows, PER * slots)] * 2
         + [inside(KVH, late * rows, DH)] * 2
         + [
             inside(KVH, 8, PER * slots, dtype=F32),
-            inside(count, 2, rows, width, dtype=F32),
-            inside(count, 2, rows, width),
+            inside(late, 2, rows, width, dtype=F32),
+            inside(late, 2, rows, width),
         ],
         scratch_shapes=[pltpu.VMEM((2, 2 * late * rows, PER * slots), F32)],
         compiler_params=options(20),
         cost_estimate=cost(3 * 10**9),
         name="responses",
     )(
-        qr_x, gr_x, gr_m, mask_r, stats, raised_a, dprob_a, chosen, *own[here:], *pair[here:]
+        qr_x, gr_x, gr_m, mask_r, stats, chosen, *own[here:], *pair[here:]
     )
     back = swapped(far, "grp", 1)
 
     dscore_p, values_p, *near = pl.pallas_call(
         lambda *refs: prompt_grads_kernel(count, *refs),
         in_specs=[vmem] * (5 + count),
-        out_specs=[vmem] * (2 + count),
+        out_specs=[vmem] * (1 + count),
         out_shape=[inside(KVH, span, PER * rows), inside(KVH, span, DH)]
-        + [inside(2, rows, width, dtype=F32)] * count,
+        + [inside(2, rows, width, dtype=F32)] * (count - 1),
         scratch_shapes=[pltpu.VMEM((2, span, PER * rows), F32)],
         compiler_params=options(12),
         cost_estimate=cost(2 * 10**9),
         name="prompt_grads",
     )(qp_x, gp_x, exact, near_v, near_r, *own)
+
+    parts = sent(near, back)
+
+    near, far = pl.pallas_call(
+        first_piece_kernel,
+        in_specs=[vmem] * 10,
+        out_specs=[vmem] * 2,
+        out_shape=[inside(2, rows, width, dtype=F32), inside(2, rows, width)],
+        compiler_params=options(8),
+        cost_estimate=cost(10**9),
+        name="first_piece",
+    )(probs_p, dscore_p, qp_x, gp_m, raised_a, dprob_a, own_t, qr_x, gr_m, chosen)
+    back = swapped(far, "grp", 1)
 
     def block(height, extent):
         return pl.BlockSpec((height, extent), lambda c: (0, c))
@@ -594,7 +624,7 @@
         keep_p, probs_p, dscore_p, keys_p, values_p, keep_r, probs_c, dscore_c, keys_a, values_a,
         keys_b, values_b, raised_a, dprob_a, own_t, k_resp[0], v_resp[0], qr_x, gr_m,
     )
-    return collected(out_p, dq_p, out_r, dq_r, dk_r, dv_r, summed(near, back))
+    return collected(out_p, dq_p, out_r, dq_r, dk_r, dv_r, summed(near, back, parts))
 
 
 def solution(mesh):

time: 31 us -> 30.6 us (0.987)
  Pallas kernels: 16.7 us -> 16.1 us
    pallas_call x1, Pallas kernels: 4.14 us -> 3.38 us  [shards(): pl.pallas_call(lambda *refs: response_kernel(late, *refs), in_specs=[vmem...]
    pallas_call x0 -> x1, Pallas kernels: none -> 0.73 us  [shards(): pl.pallas_call(first_piece_kernel, in_specs=[vmem] * 10, out_specs=[vmem]...]
    ppermute x11 -> x12, waiting for transfers between devices: 2.39 us -> 2.47 us  [swapped(): return lax.ppermute(block, axis, [(i, i ^ distance) for i in range(count)])]
    ppermute x11 -> x12, starting transfers between devices: 9.26 us -> 9.32 us  [swapped(): return lax.ppermute(block, axis, [(i, i ^ distance) for i in range(count)])]
  transfers between devices with their start and end apart: 11 -> 12, of which waited for: 4 -> 3; matrix products, arithmetic and copies ran while one was open for 0% -> 0% of each run, Pallas kernels for 41% -> 42%
where the time goes in v5:
time: 30.6 us; the launch traced here: 30.4 us
  Pallas kernels  16.1 us (53%)
  starting transfers between devices  9.32 us (30%)
  waiting for transfers between devices  2.47 us (8%)
  other arithmetic  1.09 us (4%)
  between operations  0.76 us (2%)
  local copies, waits for them, and re-layouts  0.67 us (2%)
    ppermute x12, starting transfers between devices, swapped(): return lax.ppermute(block, axis, [(i, i ^ distance) for i in range(count)])  9.32 us
    pallas_call x1, Pallas kernels, shards(): pl.pallas_call(finish_kernel, grid=(KVH,), in_specs=[vmem] * 15 + [own_bl...  4.61 us
    pallas_call x1, Pallas kernels, shards(): pl.pallas_call(lambda *refs: response_kernel(late, *refs), in_specs=[vmem...  3.38 us
    pallas_call x1, Pallas kernels, shards(): pl.pallas_call(lambda *refs: prepare_kernel(count, *refs), in_specs=[hbm]...  3.03 us
    ppermute x12, waiting for transfers between devices, swapped(): return lax.ppermute(block, axis, [(i, i ^ distance) for i in range(count)])  2.47 us
    pallas_call x1, Pallas kernels, shards(): pl.pallas_call(lambda *refs: early_kernel(here, *refs), in_specs=[vmem] *...  1.89 us
    pallas_call x1, Pallas kernels, shards(): pl.pallas_call(lambda *refs: prompt_probs_kernel(count, *refs), in_specs=...  1.39 us
    pallas_call x1, Pallas kernels, shards(): pl.pallas_call(lambda *refs: prompt_grads_kernel(count, *refs), in_specs=...  1.09 us
  transfers between devices with their start and end apart: 12, of which 3 were waited for; matrix products, arithmetic and copies ran while one was open for 0% of the time, Pallas kernels for 42%

profile of v5, /device:TPU:0, one launch (start us, length us, event | category | flops | bytes accessed | tf_op | source)
XLA Modules:
  0.0 30.4 jit_solution(14619438101445751336)
XLA Ops:
  0.6 0.9 %pad_maximum_fusion.refs_7_.refs_3_.refs_5_ = bf16[64,1024]{1,0:T(8,128)(2,1)S(1)} fusion(bf16[64,512]{1,0:T(8,128)(2,1)} %bitcast.35, bf16[64,512]{1,0:T(8,128)(2,1)} %bitcast.36), kind=kLoop, calls=%fused_computation.10 | loop fusion | flops 262144 | bytes 262144 | tf_op jit(solution)/shard_map/concatenate | solution.py:487
  1.5 4.0 %collective-permute-start.3 = (bf16[64,1024]{1,0:T(8,128)(2,1)S(1)}, bf16[64,1024]{1,0:T(8,128)(2,1)S(1)}, u32[]{:S(2)}, u32[]{:S(2)}) collective-permute-start(bf16[64,1024]{1,0:T(8,128)(2,1)S(1)} %pad_maximum_fusion.refs_7_.refs_3_.refs_5_), channel_id=1, source_target_pairs={{0,3},{1,2},{2,1},{3,0},{4,7},{5,6},{6,5},{7,4},{8,11},{9,10},{10,... | collective-permute-start | bytes 393224 | tf_op jit(solution)/shard_map/ppermute | solution.py:30
  5.5 0.5 %collective-permute-start.2 = (bf16[64,1024]{1,0:T(8,128)(2,1)S(1)}, bf16[64,1024]{1,0:T(8,128)(2,1)S(1)}, u32[]{:S(2)}, u32[]{:S(2)}) collective-permute-start(bf16[64,1024]{1,0:T(8,128)(2,1)S(1)} %pad_maximum_fusion.refs_7_.refs_3_.refs_5_), channel_id=1, source_target_pairs={{0,2},{1,3},{2,0},{3,1},{4,6},{5,7},{6,4},{7,5},{8,10},{9,11},{10,... | collective-permute-start | bytes 393224 | tf_op jit(solution)/shard_map/ppermute | solution.py:30
  6.0 0.0 collective-permute-start.1
  6.0 0.1 collective-permute-start
  6.1 0.0 copy-start
  6.1 0.0 copy-start.1
  6.1 3.0 %prepare.1 = (bf16[4,512,256]{2,1,0:T(8,128)(2,1)S(1)}, bf16[4,512,256]{2,1,0:T(8,128)(2,1)S(1)}, bf16[4,512,128]{2,1,0:T(8,128)(2,1)S(1)}, bf16[4,1024,256]{2,1...) custom-call(s32[8]{0:T(128)} %refs_0_.1, ...), custom_call_target="tpu_custom_call" | custom-call | flops 4000000000 | bytes 1048576 | tf_op jit(solution)/shard_map/prepare/pallas_call | solution.py:499
  9.2 0.0 collective-permute-done.1.refs_8_
  9.2 0.0 copy-done
  9.2 0.0 copy-done.1
  9.2 1.9 %early.1 = (bf16[4,64,128]{2,1,0:T(8,128)(2,1)S(1)}, bf16[4,64,128]{2,1,0:T(8,128)(2,1)S(1)}, f32[4,192,1024]{2,1,0:T(8,128)S(1)}, f32[4,192,1024]{2,1,0:T(8,128)S(1)}, f32[4,8,1024]{2,1,0:T(8,128)S(1)}) custom-call(bf16[4,1024,256]{2,1,0:T(8,128)(2,1)S(1)} %get-tuple-element.58.refs_0_.q_x.qr_x, bf16[4,1024,256]{2,1,0:T(8,128)(2,1)S(1)} %get-tuple-element.59.refs_1_, ...), custom_call_target="tpu_custom_call" | custom-call | flops 3000000000 | bytes 1048576 | tf_op jit(solution)/shard_map/early/pallas_call | solution.py:530
  11.1 0.0 collective-permute-done.3.refs_6_.refs_8_
  11.1 0.7 %collective-permute-done.2.refs_5_.refs_7_ = bf16[64,1024]{1,0:T(8,128)(2,1)S(1)} collective-permute-done((bf16[64,1024]{1,0:T(8,128)(2,1)S(1)}, bf16[64,1024]{1,0:T(8,128)(2,1)S(1)}, u32[]{:S(2)}, u32[]{:S(2)}) %collective-permute-start.2) | collective-permute-done | bytes 131104 | tf_op jit(solution)/shard_map/ppermute | solution.py:30
  11.8 0.3 collective-permute-done.refs_4_.refs_6_
  12.1 0.0 collective-permute-start.4
  12.1 0.5 %collective-permute-start.5 = (bf16[64,1024]{1,0:T(8,128)(2,1)S(1)}, bf16[64,1024]{1,0:T(8,128)(2,1)S(1)}, u32[]{:S(2)}, u32[]{:S(2)}) collective-permute-start(bf16[64,1024]{1,0:T(8,128)(2,1)S(1)} %collective-permute-done.2.refs_5_.refs_7_), channel_id=1, source_target_pairs={{0,4},{4,0},{8,12},{12,8},{16,20},{20,16},{24,28},{28,24},{1,5},{5... | collective-permute-start | bytes 393224 | tf_op jit(solution)/shard_map/ppermute | solution.py:30
  12.6 0.0 collective-permute-start.6
  12.6 1.4 %prompt_probs.1 = (f32[4,256,512]{2,1,0:T(8,128)S(1)}, bf16[4,256,512]{2,1,0:T(8,128)(2,1)S(1)}, bf16[4,256,128]{2,1,0:T(8,128)(2,1)S(1)}, f32[3,64,512]{2,1,0:T(8,128)S(1)}) custom-call(bf16[4,512,256]{2,1,0:T(8,128)(2,1)S(1)} %get-tuple-element.55.refs_0_.qp_x, bf16[4,512,128]{2,1,0:T(8,128)(2,1)S(1)} %get-tuple-element.56.refs_1_.gp_m, ...), custom_call_target="tpu_custom_call" | custom-call | flops 2000000000 | bytes 1048576 | tf_op jit(solution)/shard_map/prompt_probs/pallas_call | solution.py:545
  14.0 0.0 collective-permute-done.4.refs_9_
  14.0 0.0 collective-permute-done.5.refs_10_
  14.0 0.0 collective-permute-done.6.refs_11_
  14.0 3.4 %responses.1 = (bf16[4,192,1024]{2,1,0:T(8,128)(2,1)S(1)}, bf16[4,192,1024]{2,1,0:T(8,128)(2,1)S(1)}, bf16[4,192,128]{2,1,0:T(8,128)(2,1)S(1)}, bf16[4,192,128]{...) custom-call(bf16[4,1024,256]{2,1,0:T(8,128)(2,1)S(1)} %get-tuple-ele, ...), custom_call_target="tpu_custom_call" | custom-call | flops 3000000000 | bytes 1048576 | tf_op jit(solution)/shard_map/responses/pallas_call | solution.py:563
  17.4 0.6 %collective-permute-start.8 = (bf16[3,2,64,512]{3,2,1,0:T(8,128)(2,1)S(1)}, bf16[3,2,64,512]{3,2,1,0:T(8,128)(2,1)S(1)}, u32[]{:S(2)}, u32[]{:S(2)}) collective-permute-start(bf16[3,2,64,512]{3,2,1,0:T(8,128)(2,1)S(1)} %get-tuple-element.95), channel_id=1, source_target_pairs={{0,4},{4,0},{8,12},{12,8},{16,20},{20,16},{24,28},{28,24},{1,5},{5... | collective-permute-start | bytes 1179656 | tf_op jit(solution)/shard_map/ppermute | solution.py:30
  18.0 1.1 %prompt_grads.1 = (bf16[4,256,512]{2,1,0:T(8,128)(2,1)S(1)}, bf16[4,256,128]{2,1,0:T(8,128)(2,1)S(1)}, f32[2,64,512]{2,1,0:T(8,128)S(1)}, f32[2,64,512]{2,1,0:T(8,128)S(1)}, f32[2,64,512]{2,1,0:T(8,128)S(1)}) custom-call(bf16[4,512,256]{2,1,0:T(8,128)(2,1)S(1)} %get-tuple-element.55.refs_0_.qp_x, bf16[4,512,256]{2,1,0:T(8,128)(2,1)S(1)} %get-tuple-element.68.refs_1_, ...), custom_call_target="tpu_custom_call" | custom-call | flops 2000000000 | bytes 1048576 | tf_op jit(solution)/shard_map/prompt_grads/pallas_call | solution.py:583
  19.1 0.7 %first_piece.1 = (f32[2,64,512]{2,1,0:T(8,128)S(1)}, bf16[2,64,512]{2,1,0:T(8,128)(2,1)S(1)}) custom-call(bf16[4,256,512]{2,1,0:T(8,128)(2,1)S(1)} %get-tuple-element.67.probs_p, bf16[4,256,512]{2,1,0:T(8,128)(2,1)S(1)} %get-tuple-element.75.dscore_p, bf16[4,512,256]{2,1,0:T(8,128)(2,1)S(1)} %get-tuple-element.55.refs_0_.qp_x, ...), custom_call_target="tpu_custom_call" | custom-call | flops 1000000000 | bytes 1048576 | tf_op jit(solution)/shard_map/first_piece/pallas_call | solution.py:597
  19.8 0.1 collective-permute-start.7
  19.9 0.0 collective-permute-done.8
  19.9 0.1 fusion.2
  20.0 2.2 %collective-permute-start.9 = (bf16[2,64,512]{2,1,0:T(8,128)(2,1)S(1)}, bf16[2,64,512]{2,1,0:T(8,128)(2,1)S(1)}, u32[]{:S(2)}, u32[]{:S(2)}) collective-permute-start(bf16[2,64,512]{2,1,0:T(8,128)(2,1)S(1)} %get-tuple-element.100), channel_id=1, source_target_pairs={{0,3},{1,2},{2,1},{3,0},{4,7},{5,6},{6,5},{7,4},{8,11},{9,10},{10,... | collective-permute-start | bytes 393224 | tf_op jit(solution)/shard_map/ppermute | solution.py:30
  22.3 0.7 %collective-permute-start.11 = (bf16[2,64,512]{2,1,0:T(8,128)(2,1)S(1)}, bf16[2,64,512]{2,1,0:T(8,128)(2,1)S(1)}, u32[]{:S(2)}, u32[]{:S(2)}) collective-permute-start(bf16[2,64,512]{2,1,0:T(8,128)(2,1)S(1)} %get-tuple-element.101), channel_id=1, source_target_pairs={{0,1},{1,0},{2,3},{3,2},{4,5},{5,4},{6,7},{7,6},{8,9},{9,8},{10,11... | collective-permute-start | bytes 393224 | tf_op jit(solution)/shard_map/ppermute | solution.py:30
  23.0 0.6 %collective-permute-start.10 = (bf16[2,64,512]{2,1,0:T(8,128)(2,1)S(1)}, bf16[2,64,512]{2,1,0:T(8,128)(2,1)S(1)}, u32[]{:S(2)}, u32[]{:S(2)}) collective-permute-start(bf16[2,64,512]{2,1,0:T(8,128)(2,1)S(1)} %get-tuple-element.102), channel_id=1, source_target_pairs={{0,2},{1,3},{2,0},{3,1},{4,6},{5,7},{6,4},{7,5},{8,10},{9,11},{10,... | collective-permute-start | bytes 393224 | tf_op jit(solution)/shard_map/ppermute | solution.py:30
  23.6 4.6 %finish.1 = (bf16[64,4096]{1,0:T(8,128)(2,1)}, bf16[64,4096]{1,0:T(8,128)(2,1)}, bf16[128,4096]{1,0:T(8,128)(2,1)}, bf16[128,4096]{1,0:T(8,128)(2,1)}, bf16[128,...) custom-call(f32[8,512]{1,0:T(8,128)S(1)} %get-tuple-element.54.keep_p, bf16[4,256,512]{2,1,0:T(8,128)(2,1)S(1)} %get-tuple-element.67.probs_p, ...), custom_call_target="tpu_custom_call" | custom-call | flops 8000000000 | bytes 1048576 | tf_op jit(solution)/shard_map/finish/pallas_call | solution.py:612
  28.2 0.0 collective-permute-done.7
  28.2 0.0 collective-permute-done.9
  28.2 1.5 %collective-permute-done.11 = bf16[2,64,512]{2,1,0:T(8,128)(2,1)S(1)} collective-permute-done((bf16[2,64,512]{2,1,0:T(8,128)(2,1)S(1)}, bf16[2,64,512]{2,1,0:T(8,128)(2,1)S(1)}, u32[]{:S(2)}, u32[]{:S(2)}) %collective-permute-start.11) | collective-permute-done | bytes 131104 | tf_op jit(solution)/shard_map/ppermute | solution.py:30
  29.7 0.0 collective-permute-done.10
  29.7 0.1 add_convert_fusion
  29.8 0.7 %fusion.3 = (bf16[1,64,512]{2,1,0:T(8,128)(2,1)}, bf16[1,64,512]{2,1,0:T(8,128)(2,1)}) fusion(bf16[2,64,512]{2,1,0:T(8,128)(2,1)S(1)} %add_convert_fusion), kind=kLoop, calls=%fused_computation.11 | loop fusion | bytes 262144 | tf_op jit(solution)/shard_map/slice | solution.py:450
Async XLA Ops:
  1.5 9.6 %collective-permute-start.3 = (bf16[64,1024]{1,0:T(8,128)(2,1)S(1)}, bf16[64,1024]{1,0:T(8,128)(2,1)S(1)}, u32[]{:S(2)}, u32[]{:S(2)}) collective-permute-start(bf16[64,1024]{1,0:T(8,128)(2,1)S(1)} %pad_maximum_fusion.refs_7_.refs_3_.refs_5_), channel_id=1, source_target_pairs={{0,3},{1,2},{2,1},{3,0},{4,7},{5,6},{6,5},{7,4},{8,11},{9,10},{10,... | collective-permute-start | bytes 393224 | tf_op jit(solution)/shard_map/ppermute | solution.py:30
  5.5 6.3 %collective-permute-start.2 = (bf16[64,1024]{1,0:T(8,128)(2,1)S(1)}, bf16[64,1024]{1,0:T(8,128)(2,1)S(1)}, u32[]{:S(2)}, u32[]{:S(2)}) collective-permute-start(bf16[64,1024]{1,0:T(8,128)(2,1)S(1)} %pad_maximum_fusion.refs_7_.refs_3_.refs_5_), channel_id=1, source_target_pairs={{0,2},{1,3},{2,0},{3,1},{4,6},{5,7},{6,4},{7,5},{8,10},{9,11},{10,... | collective-permute-start | bytes 393224 | tf_op jit(solution)/shard_map/ppermute | solution.py:30
  6.0 3.2 %collective-permute-start.1 = (bf16[64,1024]{1,0:T(8,128)(2,1)S(1)}, bf16[64,1024]{1,0:T(8,128)(2,1)S(1)}, u32[]{:S(2)}, u32[]{:S(2)}) collective-permute-start(bf16[64,1024]{1,0:T(8,128)(2,1)S(1)} %pad_maximum_fusion.refs_7_.refs_3_.refs_5_), channel_id=1, source_target_pairs={{0,4},{4,0},{8,12},{12,8},{16,20},{20,16},{24,28},{28,24},{1,5},{5... | collective-permute-start | bytes 393224 | tf_op jit(solution)/shard_map/ppermute | solution.py:30
  6.0 6.1 %collective-permute-start = (bf16[64,1024]{1,0:T(8,128)(2,1)S(1)}, bf16[64,1024]{1,0:T(8,128)(2,1)S(1)}, u32[]{:S(2)}, u32[]{:S(2)}) collective-permute-start(bf16[64,1024]{1,0:T(8,128)(2,1)S(1)} %pad_maximum_fusion.refs_7_.refs_3_.refs_5_), channel_id=1, source_target_pairs={{0,1},{1,0},{2,3},{3,2},{4,5},{5,4},{6,7},{7,6},{8,9},{9,8},{10,11... | collective-permute-start | bytes 393224 | tf_op jit(solution)/shard_map/ppermute | solution.py:30
  6.1 3.1 %copy-start = (bf16[1,128,512]{2,1,0:T(8,128)(2,1)S(1)}, bf16[1,128,512]{2,1,0:T(8,128)(2,1)}, u32[]{:S(2)}) copy-start(bf16[1,128,512]{2,1,0:T(8,128)(2,1)} %param.19) | copy-start | bytes 393220
  6.1 3.1 %copy-start.1 = (bf16[1,128,512]{2,1,0:T(8,128)(2,1)S(1)}, bf16[1,128,512]{2,1,0:T(8,128)(2,1)}, u32[]{:S(2)}) copy-start(bf16[1,128,512]{2,1,0:T(8,128)(2,1)} %param.20) | copy-start | bytes 393220
  12.1 1.9 %collective-permute-start.4 = (bf16[64,1024]{1,0:T(8,128)(2,1)S(1)}, bf16[64,1024]{1,0:T(8,128)(2,1)S(1)}, u32[]{:S(2)}, u32[]{:S(2)}) collective-permute-start(bf16[64,1024]{1,0:T(8,128)(2,1)S(1)} %collective-permute-done.refs_4_.refs_6_), channel_id=1, source_target_pairs={{0,4},{4,0},{8,12},{12,8},{16,20},{20,16},{24,28},{28,24},{1,5},{5... | collective-permute-start | bytes 393224 | tf_op jit(solution)/shard_map/ppermute | solution.py:30
  12.1 1.9 %collective-permute-start.5 = (bf16[64,1024]{1,0:T(8,128)(2,1)S(1)}, bf16[64,1024]{1,0:T(8,128)(2,1)S(1)}, u32[]{:S(2)}, u32[]{:S(2)}) collective-permute-start(bf16[64,1024]{1,0:T(8,128)(2,1)S(1)} %collective-permute-done.2.refs_5_.refs_7_), channel_id=1, source_target_pairs={{0,4},{4,0},{8,12},{12,8},{16,20},{20,16},{24,28},{28,24},{1,5},{5... | collective-permute-start | bytes 393224 | tf_op jit(solution)/shard_map/ppermute | solution.py:30
  12.6 1.4 %collective-permute-start.6 = (bf16[64,1024]{1,0:T(8,128)(2,1)S(1)}, bf16[64,1024]{1,0:T(8,128)(2,1)S(1)}, u32[]{:S(2)}, u32[]{:S(2)}) collective-permute-start(bf16[64,1024]{1,0:T(8,128)(2,1)S(1)} %collective-permute-done.3.refs_6_.refs_8_), channel_id=1, source_target_pairs={{0,4},{4,0},{8,12},{12,8},{16,20},{20,16},{24,28},{28,24},{1,5},{5... | collective-permute-start | bytes 393224 | tf_op jit(solution)/shard_map/ppermute | solution.py:30
  17.4 2.5 %collective-permute-start.8 = (bf16[3,2,64,512]{3,2,1,0:T(8,128)(2,1)S(1)}, bf16[3,2,64,512]{3,2,1,0:T(8,128)(2,1)S(1)}, u32[]{:S(2)}, u32[]{:S(2)}) collective-permute-start(bf16[3,2,64,512]{3,2,1,0:T(8,128)(2,1)S(1)} %get-tuple-element.95), channel_id=1, source_target_pairs={{0,4},{4,0},{8,12},{12,8},{16,20},{20,16},{24,28},{28,24},{1,5},{5... | collective-permute-start | bytes 1179656 | tf_op jit(solution)/shard_map/ppermute | solution.py:30
  19.8 8.4 %collective-permute-start.7 = (bf16[2,64,512]{2,1,0:T(8,128)(2,1)S(1)}, bf16[2,64,512]{2,1,0:T(8,128)(2,1)S(1)}, u32[]{:S(2)}, u32[]{:S(2)}) collective-permute-start(bf16[2,64,512]{2,1,0:T(8,128)(2,1)S(1)} %get-tuple-element.93), channel_id=1, source_target_pairs={{0,4},{4,0},{8,12},{12,8},{16,20},{20,16},{24,28},{28,24},{1,5},{5... | collective-permute-start | bytes 393224 | tf_op jit(solution)/shard_map/ppermute | solution.py:30
  20.0 8.2 %collective-permute-start.9 = (bf16[2,64,512]{2,1,0:T(8,128)(2,1)S(1)}, bf16[2,64,512]{2,1,0:T(8,128)(2,1)S(1)}, u32[]{:S(2)}, u32[]{:S(2)}) collective-permute-start(bf16[2,64,512]{2,1,0:T(8,128)(2,1)S(1)} %get-tuple-element.100), channel_id=1, source_target_pairs={{0,3},{1,2},{2,1},{3,0},{4,7},{5,6},{6,5},{7,4},{8,11},{9,10},{10,... | collective-permute-start | bytes 393224 | tf_op jit(solution)/shard_map/ppermute | solution.py:30
  22.3 7.4 %collective-permute-start.11 = (bf16[2,64,512]{2,1,0:T(8,128)(2,1)S(1)}, bf16[2,64,512]{2,1,0:T(8,128)(2,1)S(1)}, u32[]{:S(2)}, u32[]{:S(2)}) collective-permute-start(bf16[2,64,512]{2,1,0:T(8,128)(2,1)S(1)} %get-tuple-element.101), channel_id=1, source_target_pairs={{0,1},{1,0},{2,3},{3,2},{4,5},{5,4},{6,7},{7,6},{8,9},{9,8},{10,11... | collective-permute-start | bytes 393224 | tf_op jit(solution)/shard_map/ppermute | solution.py:30
  23.0 6.7 %collective-permute-start.10 = (bf16[2,64,512]{2,1,0:T(8,128)(2,1)S(1)}, bf16[2,64,512]{2,1,0:T(8,128)(2,1)S(1)}, u32[]{:S(2)}, u32[]{:S(2)}) collective-permute-start(bf16[2,64,512]{2,1,0:T(8,128)(2,1)S(1)} %get-tuple-element.102), channel_id=1, source_target_pairs={{0,2},{1,3},{2,0},{3,1},{4,6},{5,7},{6,4},{7,5},{8,10},{9,11},{10,... | collective-permute-start | bytes 393224 | tf_op jit(solution)/shard_map/ppermute | solution.py:30

commit v6 on v5

--- a/solution.py
+++ b/solution.py
@@ -274,9 +274,7 @@
     in_turn(first, second, third)
 
 
-def first_piece_kernel(
-    probs_p, dscore_p, qp_x, gp_m, raised_a, dprob_a, own_t, qr_x, gr_m, chosen, near, far
-):
+def first_piece_kernel(raised_a, dprob_a, own_t, qr_x, gr_m, chosen, near, far):
     piece = near.shape[1]
     slots = raised_a.shape[1] - piece
     is_own = chosen[0:1, :]
@@ -284,15 +282,15 @@
         probs = raised_a[c, slots:] * own_t[c, 0:1]
         dscore = (probs * (dprob_a[c, slots:] - own_t[c, 1:2])).astype(BF16)
         grads = dot(dscore, qr_x[c, :, :DH]), dot(probs.astype(BF16), gr_m[c])
-        own = dot(dscore_p[c, :piece], qp_x[c, :, :DH]), dot(probs_p[c, :piece], gp_m[c])
         for i in range(2):
-            near[i, :, lanes(c)] = own[i] + grads[i] * is_own
+            near[i, :, lanes(c)] = grads[i] * is_own
             far[i, :, lanes(c)] = (grads[i] * (1.0 - is_own)).astype(BF16)
 
 
 def finish_kernel(
     keep_p, probs_p, dscore_p, keys_p, values_p, keep_r, probs_c, dscore_c, keys_a, values_a,
-    keys_b, values_b, raised_a, dprob_a, own_t, k_r, v_r, q_x, g_m, out_p, dq_p, out_r, dq_r, dk_r, dv_r,
+    keys_b, values_b, raised_a, dprob_a, own_t, k_r, v_r, q_x, g_m, qp_x, gp_m,
+    out_p, dq_p, out_r, dq_r, dk_r, dv_r, near,
 ):
     c = pl.program_id(0)
     own_factor, delta = own_t[c, 0:1], own_t[c, 1:2]
@@ -313,6 +311,9 @@
     both = dot(left, right, TN)
     out_r[...] = across(both[:DH] * keep_r[0:1])
     dq_r[...] = across(both[DH:])
+    piece = near.shape[1]
+    near[0] = dot(dscore_p[c, :piece], qp_x[c, :, :DH])
+    near[1] = dot(probs_p[c, :piece], gp_m[c])
     right = jnp.concatenate([probs_p[c], dscore_p[c]], axis=0)
     both = dot(beside(values_p[c], keys_p[c]), right, TN)
     out_p[...] = across(both[:DH] * keep_p[0:1])
@@ -594,37 +595,39 @@
 
     parts = sent(near, back)
 
-    near, far = pl.pallas_call(
+    near_r, far = pl.pallas_call(
         first_piece_kernel,
-        in_specs=[vmem] * 10,
+        in_specs=[vmem] * 6,
         out_specs=[vmem] * 2,
         out_shape=[inside(2, rows, width, dtype=F32), inside(2, rows, width)],
         compiler_params=options(8),
         cost_estimate=cost(10**9),
         name="first_piece",
-    )(probs_p, dscore_p, qp_x, gp_m, raised_a, dprob_a, own_t, qr_x, gr_m, chosen)
+    )(raised_a, dprob_a, own_t, qr_x, gr_m, chosen)
     back = swapped(far, "grp", 1)
 
     def block(height, extent):
         return pl.BlockSpec((height, extent), lambda c: (0, c))
 
     wide_p, wide_r, own_block = block(rows, PER * DH), block(slots, PER * DH), block(slots, DH)
-    out_p, dq_p, out_r, dq_r, dk_r, dv_r = pl.pallas_call(
+    own_piece = pl.BlockSpec((2, rows, DH), lambda c: (0, 0, c))
+    out_p, dq_p, out_r, dq_r, dk_r, dv_r, near = pl.pallas_call(
         finish_kernel,
         grid=(KVH,),
-        in_specs=[vmem] * 15 + [own_block] * 2 + [vmem] * 2,
-        out_specs=[wide_p, wide_p, wide_r, wide_r, own_block, own_block],
+        in_specs=[vmem] * 15 + [own_block] * 2 + [vmem] * 4,
+        out_specs=[wide_p, wide_p, wide_r, wide_r, own_block, own_block, own_piece],
         out_shape=[jax.ShapeDtypeStruct((rows, HQ * DH), BF16)] * 2
         + [jax.ShapeDtypeStruct((slots, HQ * DH), BF16)] * 2
-        + [jax.ShapeDtypeStruct((slots, width), BF16)] * 2,
+        + [jax.ShapeDtypeStruct((slots, width), BF16)] * 2
+        + [inside(2, rows, width, dtype=F32)],
         compiler_params=options(20),
         cost_estimate=cost(8 * 10**9),
         name="finish",
     )(
         keep_p, probs_p, dscore_p, keys_p, values_p, keep_r, probs_c, dscore_c, keys_a, values_a,
-        keys_b, values_b, raised_a, dprob_a, own_t, k_resp[0], v_resp[0], qr_x, gr_m,
-    )
-    return collected(out_p, dq_p, out_r, dq_r, dk_r, dv_r, summed(near, back, parts))
+        keys_b, values_b, raised_a, dprob_a, own_t, k_resp[0], v_resp[0], qr_x, gr_m, qp_x, gp_m,
+    )
+    return collected(out_p, dq_p, out_r, dq_r, dk_r, dv_r, summed(near + near_r, back, parts))
 
 
 def solution(mesh):

time: 30.6 us -> 30.4 us (level)
  waiting for transfers between devices: 2.47 us -> 2.1 us
    ppermute x12, waiting for transfers between devices: 2.47 us -> 2.1 us  [swapped(): return lax.ppermute(block, axis, [(i, i ^ distance) for i in range(count)])]
    pallas_call x1, Pallas kernels: 4.61 us -> 4.95 us  [shards(): pl.pallas_call(finish_kernel, grid=(KVH,), in_specs=[vmem] * 15 + [own_bl...]
  transfers between devices with their start and end apart: 12 -> 12, of which waited for: 3 -> 3; matrix products, arithmetic and copies ran while one was open for 0% -> 0% of each run, Pallas kernels for 42% -> 43%
where the time goes in v6:
time: 30.4 us; the launch traced here: 30.2 us
  Pallas kernels  16.2 us (53%)
  starting transfers between devices  9.33 us (31%)
  waiting for transfers between devices  2.1 us (7%)
  other arithmetic  1.13 us (4%)
  between operations  0.76 us (2%)
  local copies, waits for them, and re-layouts  0.67 us (2%)
    ppermute x12, starting transfers between devices, swapped(): return lax.ppermute(block, axis, [(i, i ^ distance) for i in range(count)])  9.33 us
    pallas_call x1, Pallas kernels, shards(): pl.pallas_call(finish_kernel, grid=(KVH,), in_specs=[vmem] * 15 + [own_bl...  4.95 us
    pallas_call x1, Pallas kernels, shards(): pl.pallas_call(lambda *refs: response_kernel(late, *refs), in_specs=[vmem...  3.39 us
    pallas_call x1, Pallas kernels, shards(): pl.pallas_call(lambda *refs: prepare_kernel(count, *refs), in_specs=[hbm]...  3.03 us
    ppermute x12, waiting for transfers between devices, swapped(): return lax.ppermute(block, axis, [(i, i ^ distance) for i in range(count)])  2.1 us
    pallas_call x1, Pallas kernels, shards(): pl.pallas_call(lambda *refs: early_kernel(here, *refs), in_specs=[vmem] *...  1.93 us
    pallas_call x1, Pallas kernels, shards(): pl.pallas_call(lambda *refs: prompt_probs_kernel(count, *refs), in_specs=...  1.38 us
    pallas_call x1, Pallas kernels, shards(): pl.pallas_call(lambda *refs: prompt_grads_kernel(count, *refs), in_specs=...  1.05 us
  transfers between devices with their start and end apart: 12, of which 3 were waited for; matrix products, arithmetic and copies ran while one was open for 0% of the time, Pallas kernels for 43%

profile of v6, /device:TPU:0, one launch (start us, length us, event | category | flops | bytes accessed | tf_op | source)
XLA Modules:
  0.0 30.2 jit_solution(2213252900228634461)
XLA Ops:
  0.6 0.9 %pad_maximum_fusion.refs_7_.refs_3_.refs_5_ = bf16[64,1024]{1,0:T(8,128)(2,1)S(1)} fusion(bf16[64,512]{1,0:T(8,128)(2,1)} %bitcast.35, bf16[64,512]{1,0:T(8,128)(2,1)} %bitcast.36), kind=kLoop, calls=%fused_computation.10 | loop fusion | flops 262144 | bytes 262144 | tf_op jit(solution)/shard_map/concatenate | solution.py:488
  1.5 4.0 %collective-permute-start.3 = (bf16[64,1024]{1,0:T(8,128)(2,1)S(1)}, bf16[64,1024]{1,0:T(8,128)(2,1)S(1)}, u32[]{:S(2)}, u32[]{:S(2)}) collective-permute-start(bf16[64,1024]{1,0:T(8,128)(2,1)S(1)} %pad_maximum_fusion.refs_7_.refs_3_.refs_5_), channel_id=1, source_target_pairs={{0,3},{1,2},{2,1},{3,0},{4,7},{5,6},{6,5},{7,4},{8,11},{9,10},{10,... | collective-permute-start | bytes 393224 | tf_op jit(solution)/shard_map/ppermute | solution.py:30
  5.5 0.5 %collective-permute-start.2 = (bf16[64,1024]{1,0:T(8,128)(2,1)S(1)}, bf16[64,1024]{1,0:T(8,128)(2,1)S(1)}, u32[]{:S(2)}, u32[]{:S(2)}) collective-permute-start(bf16[64,1024]{1,0:T(8,128)(2,1)S(1)} %pad_maximum_fusion.refs_7_.refs_3_.refs_5_), channel_id=1, source_target_pairs={{0,2},{1,3},{2,0},{3,1},{4,6},{5,7},{6,4},{7,5},{8,10},{9,11},{10,... | collective-permute-start | bytes 393224 | tf_op jit(solution)/shard_map/ppermute | solution.py:30
  6.0 0.0 collective-permute-start.1
  6.0 0.1 collective-permute-start
  6.1 0.0 copy-start
  6.1 0.0 copy-start.1
  6.1 3.0 %prepare.1 = (bf16[4,512,256]{2,1,0:T(8,128)(2,1)S(1)}, bf16[4,512,256]{2,1,0:T(8,128)(2,1)S(1)}, bf16[4,512,128]{2,1,0:T(8,128)(2,1)S(1)}, bf16[4,1024,256]{2,1...) custom-call(s32[8]{0:T(128)} %refs_0_.1, ...), custom_call_target="tpu_custom_call" | custom-call | flops 4000000000 | bytes 1048576 | tf_op jit(solution)/shard_map/prepare/pallas_call | solution.py:500
  9.2 0.0 collective-permute-done.1.refs_8_
  9.2 0.0 copy-done
  9.2 0.0 copy-done.1
  9.2 1.9 %early.1 = (bf16[4,64,128]{2,1,0:T(8,128)(2,1)S(1)}, bf16[4,64,128]{2,1,0:T(8,128)(2,1)S(1)}, f32[4,192,1024]{2,1,0:T(8,128)S(1)}, f32[4,192,1024]{2,1,0:T(8,128)S(1)}, f32[4,8,1024]{2,1,0:T(8,128)S(1)}) custom-call(bf16[4,1024,256]{2,1,0:T(8,128)(2,1)S(1)} %get-tuple-element.59.refs_0_.q_x.qr_x, bf16[4,1024,256]{2,1,0:T(8,128)(2,1)S(1)} %get-tuple-element.60.refs_1_, ...), custom_call_target="tpu_custom_call" | custom-call | flops 3000000000 | bytes 1048576 | tf_op jit(solution)/shard_map/early/pallas_call | solution.py:531
  11.1 0.0 collective-permute-done.3.refs_6_.refs_8_
  11.1 0.6 %collective-permute-done.2.refs_5_.refs_7_ = bf16[64,1024]{1,0:T(8,128)(2,1)S(1)} collective-permute-done((bf16[64,1024]{1,0:T(8,128)(2,1)S(1)}, bf16[64,1024]{1,0:T(8,128)(2,1)S(1)}, u32[]{:S(2)}, u32[]{:S(2)}) %collective-permute-start.2) | collective-permute-done | bytes 131104 | tf_op jit(solution)/shard_map/ppermute | solution.py:30
  11.8 0.3 collective-permute-done.refs_4_.refs_6_
  12.1 0.0 collective-permute-start.4
  12.1 0.5 %collective-permute-start.5 = (bf16[64,1024]{1,0:T(8,128)(2,1)S(1)}, bf16[64,1024]{1,0:T(8,128)(2,1)S(1)}, u32[]{:S(2)}, u32[]{:S(2)}) collective-permute-start(bf16[64,1024]{1,0:T(8,128)(2,1)S(1)} %collective-permute-done.2.refs_5_.refs_7_), channel_id=1, source_target_pairs={{0,4},{4,0},{8,12},{12,8},{16,20},{20,16},{24,28},{28,24},{1,5},{5... | collective-permute-start | bytes 393224 | tf_op jit(solution)/shard_map/ppermute | solution.py:30
  12.6 0.0 collective-permute-start.6
  12.6 1.4 %prompt_probs.1 = (f32[4,256,512]{2,1,0:T(8,128)S(1)}, bf16[4,256,512]{2,1,0:T(8,128)(2,1)S(1)}, bf16[4,256,128]{2,1,0:T(8,128)(2,1)S(1)}, f32[3,64,512]{2,1,0:T(8,128)S(1)}) custom-call(bf16[4,512,256]{2,1,0:T(8,128)(2,1)S(1)} %get-tuple-element.56.refs_0_.qp_x, bf16[4,512,128]{2,1,0:T(8,128)(2,1)S(1)} %get-tuple-element.57.refs_1_.gp_m, ...), custom_call_target="tpu_custom_call" | custom-call | flops 2000000000 | bytes 1048576 | tf_op jit(solution)/shard_map/prompt_probs/pallas_call | solution.py:546
  14.0 0.0 collective-permute-done.4.refs_9_
  14.0 0.0 collective-permute-done.5.refs_10_
  14.0 0.0 collective-permute-done.6.refs_11_
  14.0 3.4 %responses.1 = (bf16[4,192,1024]{2,1,0:T(8,128)(2,1)S(1)}, bf16[4,192,1024]{2,1,0:T(8,128)(2,1)S(1)}, bf16[4,192,128]{2,1,0:T(8,128)(2,1)S(1)}, bf16[4,192,128]{...) custom-call(bf16[4,1024,256]{2,1,0:T(8,128)(2,1)S(1)} %get-tuple-ele, ...), custom_call_target="tpu_custom_call" | custom-call | flops 3000000000 | bytes 1048576 | tf_op jit(solution)/shard_map/responses/pallas_call | solution.py:564
  17.4 0.6 %collective-permute-start.8 = (bf16[3,2,64,512]{3,2,1,0:T(8,128)(2,1)S(1)}, bf16[3,2,64,512]{3,2,1,0:T(8,128)(2,1)S(1)}, u32[]{:S(2)}, u32[]{:S(2)}) collective-permute-start(bf16[3,2,64,512]{3,2,1,0:T(8,128)(2,1)S(1)} %get-tuple-element.97), channel_id=1, source_target_pairs={{0,4},{4,0},{8,12},{12,8},{16,20},{20,16},{24,28},{28,24},{1,5},{5... | collective-permute-start | bytes 1179656 | tf_op jit(solution)/shard_map/ppermute | solution.py:30
  18.0 0.5 %first_piece.1 = (f32[2,64,512]{2,1,0:T(8,128)S(1)}, bf16[2,64,512]{2,1,0:T(8,128)(2,1)S(1)}) custom-call(f32[4,192,1024]{2,1,0:T(8,128)S(1)} %get-tuple-element.86.raised_a, f32[4,192,1024]{2,1,0:T(8,128)S(1)} %get-tuple-element.87.dprob_a, f32[4,8,1024]{2,1,0:T(8,128)S(1)} %get-tuple-element.88.own_t, ...), custom_call_target="tpu_custom_call" | custom-call | flops 1000000000 | bytes 1048576 | tf_op jit(solution)/shard_map/first_piece/pallas_call | solution.py:598
  18.5 0.1 collective-permute-start.7
  18.6 1.1 %prompt_grads.1 = (bf16[4,256,512]{2,1,0:T(8,128)(2,1)S(1)}, bf16[4,256,128]{2,1,0:T(8,128)(2,1)S(1)}, f32[2,64,512]{2,1,0:T(8,128)S(1)}, f32[2,64,512]{2,1,0:T(8,128)S(1)}, f32[2,64,512]{2,1,0:T(8,128)S(1)}) custom-call(bf16[4,512,256]{2,1,0:T(8,128)(2,1)S(1)} %get-tuple-element.56.refs_0_.qp_x, bf16[4,512,256]{2,1,0:T(8,128)(2,1)S(1)} %get-tuple-element.69.refs_1_, ...), custom_call_target="tpu_custom_call" | custom-call | flops 2000000000 | bytes 1048576 | tf_op jit(solution)/shard_map/prompt_grads/pallas_call | solution.py:584
  19.6 0.0 collective-permute-done.8
  19.7 0.1 fusion.2
  19.8 2.3 %collective-permute-start.9 = (bf16[2,64,512]{2,1,0:T(8,128)(2,1)S(1)}, bf16[2,64,512]{2,1,0:T(8,128)(2,1)S(1)}, u32[]{:S(2)}, u32[]{:S(2)}) collective-permute-start(bf16[2,64,512]{2,1,0:T(8,128)(2,1)S(1)} %get-tuple-element.102), channel_id=1, source_target_pairs={{0,3},{1,2},{2,1},{3,0},{4,7},{5,6},{6,5},{7,4},{8,11},{9,10},{10,... | collective-permute-start | bytes 393224 | tf_op jit(solution)/shard_map/ppermute | solution.py:30
  22.1 0.7 %collective-permute-start.11 = (bf16[2,64,512]{2,1,0:T(8,128)(2,1)S(1)}, bf16[2,64,512]{2,1,0:T(8,128)(2,1)S(1)}, u32[]{:S(2)}, u32[]{:S(2)}) collective-permute-start(bf16[2,64,512]{2,1,0:T(8,128)(2,1)S(1)} %get-tuple-element.103), channel_id=1, source_target_pairs={{0,1},{1,0},{2,3},{3,2},{4,5},{5,4},{6,7},{7,6},{8,9},{9,8},{10,11... | collective-permute-start | bytes 393224 | tf_op jit(solution)/shard_map/ppermute | solution.py:30
  22.7 0.6 %collective-permute-start.10 = (bf16[2,64,512]{2,1,0:T(8,128)(2,1)S(1)}, bf16[2,64,512]{2,1,0:T(8,128)(2,1)S(1)}, u32[]{:S(2)}, u32[]{:S(2)}) collective-permute-start(bf16[2,64,512]{2,1,0:T(8,128)(2,1)S(1)} %get-tuple-element.104), channel_id=1, source_target_pairs={{0,2},{1,3},{2,0},{3,1},{4,6},{5,7},{6,4},{7,5},{8,10},{9,11},{10,... | collective-permute-start | bytes 393224 | tf_op jit(solution)/shard_map/ppermute | solution.py:30
  23.3 4.9 %finish.1 = (bf16[64,4096]{1,0:T(8,128)(2,1)}, bf16[64,4096]{1,0:T(8,128)(2,1)}, bf16[128,4096]{1,0:T(8,128)(2,1)}, bf16[128,4096]{1,0:T(8,128)(2,1)}, bf16[128,...) custom-call(f32[8,512]{1,0:T(8,128)S(1)} %get-tuple-element.55.keep_p, ...), custom_call_target="tpu_custom_call" | custom-call | flops 8000000000 | bytes 1048576 | tf_op jit(solution)/shard_map/finish/pallas_call | solution.py:614
  28.3 0.0 collective-permute-done.7
  28.3 0.0 collective-permute-done.9
  28.3 1.1 %collective-permute-done.11 = bf16[2,64,512]{2,1,0:T(8,128)(2,1)S(1)} collective-permute-done((bf16[2,64,512]{2,1,0:T(8,128)(2,1)S(1)}, bf16[2,64,512]{2,1,0:T(8,128)(2,1)S(1)}, u32[]{:S(2)}, u32[]{:S(2)}) %collective-permute-start.11) | collective-permute-done | bytes 131104 | tf_op jit(solution)/shard_map/ppermute | solution.py:30
  29.4 0.0 collective-permute-done.10
  29.5 0.1 add_convert_fusion
  29.6 0.7 %fusion.3 = (bf16[1,64,512]{2,1,0:T(8,128)(2,1)}, bf16[1,64,512]{2,1,0:T(8,128)(2,1)}) fusion(bf16[2,64,512]{2,1,0:T(8,128)(2,1)S(1)} %add_convert_fusion), kind=kLoop, calls=%fused_computation.11 | loop fusion | bytes 262144 | tf_op jit(solution)/shard_map/slice | solution.py:451
Async XLA Ops:
  1.5 9.6 %collective-permute-start.3 = (bf16[64,1024]{1,0:T(8,128)(2,1)S(1)}, bf16[64,1024]{1,0:T(8,128)(2,1)S(1)}, u32[]{:S(2)}, u32[]{:S(2)}) collective-permute-start(bf16[64,1024]{1,0:T(8,128)(2,1)S(1)} %pad_maximum_fusion.refs_7_.refs_3_.refs_5_), channel_id=1, source_target_pairs={{0,3},{1,2},{2,1},{3,0},{4,7},{5,6},{6,5},{7,4},{8,11},{9,10},{10,... | collective-permute-start | bytes 393224 | tf_op jit(solution)/shard_map/ppermute | solution.py:30
  5.5 6.3 %collective-permute-start.2 = (bf16[64,1024]{1,0:T(8,128)(2,1)S(1)}, bf16[64,1024]{1,0:T(8,128)(2,1)S(1)}, u32[]{:S(2)}, u32[]{:S(2)}) collective-permute-start(bf16[64,1024]{1,0:T(8,128)(2,1)S(1)} %pad_maximum_fusion.refs_7_.refs_3_.refs_5_), channel_id=1, source_target_pairs={{0,2},{1,3},{2,0},{3,1},{4,6},{5,7},{6,4},{7,5},{8,10},{9,11},{10,... | collective-permute-start | bytes 393224 | tf_op jit(solution)/shard_map/ppermute | solution.py:30
  6.0 3.2 %collective-permute-start.1 = (bf16[64,1024]{1,0:T(8,128)(2,1)S(1)}, bf16[64,1024]{1,0:T(8,128)(2,1)S(1)}, u32[]{:S(2)}, u32[]{:S(2)}) collective-permute-start(bf16[64,1024]{1,0:T(8,128)(2,1)S(1)} %pad_maximum_fusion.refs_7_.refs_3_.refs_5_), channel_id=1, source_target_pairs={{0,4},{4,0},{8,12},{12,8},{16,20},{20,16},{24,28},{28,24},{1,5},{5... | collective-permute-start | bytes 393224 | tf_op jit(solution)/shard_map/ppermute | solution.py:30
  6.0 6.1 %collective-permute-start = (bf16[64,1024]{1,0:T(8,128)(2,1)S(1)}, bf16[64,1024]{1,0:T(8,128)(2,1)S(1)}, u32[]{:S(2)}, u32[]{:S(2)}) collective-permute-start(bf16[64,1024]{1,0:T(8,128)(2,1)S(1)} %pad_maximum_fusion.refs_7_.refs_3_.refs_5_), channel_id=1, source_target_pairs={{0,1},{1,0},{2,3},{3,2},{4,5},{5,4},{6,7},{7,6},{8,9},{9,8},{10,11... | collective-permute-start | bytes 393224 | tf_op jit(solution)/shard_map/ppermute | solution.py:30
  6.1 3.1 %copy-start = (bf16[1,128,512]{2,1,0:T(8,128)(2,1)S(1)}, bf16[1,128,512]{2,1,0:T(8,128)(2,1)}, u32[]{:S(2)}) copy-start(bf16[1,128,512]{2,1,0:T(8,128)(2,1)} %param.19) | copy-start | bytes 393220
  6.1 3.1 %copy-start.1 = (bf16[1,128,512]{2,1,0:T(8,128)(2,1)S(1)}, bf16[1,128,512]{2,1,0:T(8,128)(2,1)}, u32[]{:S(2)}) copy-start(bf16[1,128,512]{2,1,0:T(8,128)(2,1)} %param.20) | copy-start | bytes 393220
  12.1 1.9 %collective-permute-start.4 = (bf16[64,1024]{1,0:T(8,128)(2,1)S(1)}, bf16[64,1024]{1,0:T(8,128)(2,1)S(1)}, u32[]{:S(2)}, u32[]{:S(2)}) collective-permute-start(bf16[64,1024]{1,0:T(8,128)(2,1)S(1)} %collective-permute-done.refs_4_.refs_6_), channel_id=1, source_target_pairs={{0,4},{4,0},{8,12},{12,8},{16,20},{20,16},{24,28},{28,24},{1,5},{5... | collective-permute-start | bytes 393224 | tf_op jit(solution)/shard_map/ppermute | solution.py:30
  12.1 1.9 %collective-permute-start.5 = (bf16[64,1024]{1,0:T(8,128)(2,1)S(1)}, bf16[64,1024]{1,0:T(8,128)(2,1)S(1)}, u32[]{:S(2)}, u32[]{:S(2)}) collective-permute-start(bf16[64,1024]{1,0:T(8,128)(2,1)S(1)} %collective-permute-done.2.refs_5_.refs_7_), channel_id=1, source_target_pairs={{0,4},{4,0},{8,12},{12,8},{16,20},{20,16},{24,28},{28,24},{1,5},{5... | collective-permute-start | bytes 393224 | tf_op jit(solution)/shard_map/ppermute | solution.py:30
  12.6 1.4 %collective-permute-start.6 = (bf16[64,1024]{1,0:T(8,128)(2,1)S(1)}, bf16[64,1024]{1,0:T(8,128)(2,1)S(1)}, u32[]{:S(2)}, u32[]{:S(2)}) collective-permute-start(bf16[64,1024]{1,0:T(8,128)(2,1)S(1)} %collective-permute-done.3.refs_6_.refs_8_), channel_id=1, source_target_pairs={{0,4},{4,0},{8,12},{12,8},{16,20},{20,16},{24,28},{28,24},{1,5},{5... | collective-permute-start | bytes 393224 | tf_op jit(solution)/shard_map/ppermute | solution.py:30
  17.4 2.2 %collective-permute-start.8 = (bf16[3,2,64,512]{3,2,1,0:T(8,128)(2,1)S(1)}, bf16[3,2,64,512]{3,2,1,0:T(8,128)(2,1)S(1)}, u32[]{:S(2)}, u32[]{:S(2)}) collective-permute-start(bf16[3,2,64,512]{3,2,1,0:T(8,128)(2,1)S(1)} %get-tuple-element.97), channel_id=1, source_target_pairs={{0,4},{4,0},{8,12},{12,8},{16,20},{20,16},{24,28},{28,24},{1,5},{5... | collective-permute-start | bytes 1179656 | tf_op jit(solution)/shard_map/ppermute | solution.py:30
  18.5 9.8 %collective-permute-start.7 = (bf16[2,64,512]{2,1,0:T(8,128)(2,1)S(1)}, bf16[2,64,512]{2,1,0:T(8,128)(2,1)S(1)}, u32[]{:S(2)}, u32[]{:S(2)}) collective-permute-start(bf16[2,64,512]{2,1,0:T(8,128)(2,1)S(1)} %get-tuple-element.95), channel_id=1, source_target_pairs={{0,4},{4,0},{8,12},{12,8},{16,20},{20,16},{24,28},{28,24},{1,5},{5... | collective-permute-start | bytes 393224 | tf_op jit(solution)/shard_map/ppermute | solution.py:30
  19.8 8.5 %collective-permute-start.9 = (bf16[2,64,512]{2,1,0:T(8,128)(2,1)S(1)}, bf16[2,64,512]{2,1,0:T(8,128)(2,1)S(1)}, u32[]{:S(2)}, u32[]{:S(2)}) collective-permute-start(bf16[2,64,512]{2,1,0:T(8,128)(2,1)S(1)} %get-tuple-element.102), channel_id=1, source_target_pairs={{0,3},{1,2},{2,1},{3,0},{4,7},{5,6},{6,5},{7,4},{8,11},{9,10},{10,... | collective-permute-start | bytes 393224 | tf_op jit(solution)/shard_map/ppermute | solution.py:30
  22.1 7.4 %collective-permute-start.11 = (bf16[2,64,512]{2,1,0:T(8,128)(2,1)S(1)}, bf16[2,64,512]{2,1,0:T(8,128)(2,1)S(1)}, u32[]{:S(2)}, u32[]{:S(2)}) collective-permute-start(bf16[2,64,512]{2,1,0:T(8,128)(2,1)S(1)} %get-tuple-element.103), channel_id=1, source_target_pairs={{0,1},{1,0},{2,3},{3,2},{4,5},{5,4},{6,7},{7,6},{8,9},{9,8},{10,11... | collective-permute-start | bytes 393224 | tf_op jit(solution)/shard_map/ppermute | solution.py:30
  22.7 6.7 %collective-permute-start.10 = (bf16[2,64,512]{2,1,0:T(8,128)(2,1)S(1)}, bf16[2,64,512]{2,1,0:T(8,128)(2,1)S(1)}, u32[]{:S(2)}, u32[]{:S(2)}) collective-permute-start(bf16[2,64,512]{2,1,0:T(8,128)(2,1)S(1)} %get-tuple-element.104), channel_id=1, source_target_pairs={{0,2},{1,3},{2,0},{3,1},{4,6},{5,7},{6,4},{7,5},{8,10},{9,11},{10,... | collective-permute-start | bytes 393224 | tf_op jit(solution)/shard_map/ppermute | solution.py:30

commit v7 on v6

--- a/solution.py
+++ b/solution.py
@@ -439,11 +439,14 @@
 
 
 def summed(near, back, parts):
-    total = near + back.astype(F32)
     order = ORDER if len(parts) == len(ORDER) else range(1, len(parts) + 1)
-    for d in order:
-        total = total + parts[d - 1].astype(F32)
-    return total.astype(BF16)
+    totals = []
+    for i in range(2):
+        total = near[i] + back[i].astype(F32)
+        for d in order:
+            total = total + parts[d - 1][i].astype(F32)
+        totals.append(total.astype(BF16))
+    return totals
 
 
 def collected(out_p, dq_p, out_r, dq_r, dk_r, dv_r, total):

time: 30.4 us -> 30.4 us (level)
  other arithmetic: 1.13 us -> 1.79 us
  local copies, waits for them, and re-layouts: 0.67 us -> 0.01 us
    slice x1 -> x0, local copies, waits for them, and re-layouts: 0.66 us -> none  [collected(): total[1]]
    convert_element_type x1, other arithmetic: 0.11 us -> 0.74 us  [summed(): totals.append(total.astype(BF16))]
  transfers between devices with their start and end apart: 12 -> 12, of which waited for: 3 -> 3; matrix products, arithmetic and copies ran while one was open for 0% -> 1% of each run, Pallas kernels for 43% -> 43%
where the time goes in v7:
time: 30.4 us; the launch traced here: 30.2 us
  Pallas kernels  16.2 us (53%)
  starting transfers between devices  9.33 us (31%)
  waiting for transfers between devices  2.05 us (7%)
  other arithmetic  1.79 us (6%)
  between operations  0.77 us (3%)
    ppermute x12, starting transfers between devices, swapped(): return lax.ppermute(block, axis, [(i, i ^ distance) for i in range(count)])  9.33 us
    pallas_call x1, Pallas kernels, shards(): pl.pallas_call(finish_kernel, grid=(KVH,), in_specs=[vmem] * 15 + [own_bl...  4.95 us
    pallas_call x1, Pallas kernels, shards(): pl.pallas_call(lambda *refs: response_kernel(late, *refs), in_specs=[vmem...  3.39 us
    pallas_call x1, Pallas kernels, shards(): pl.pallas_call(lambda *refs: prepare_kernel(count, *refs), in_specs=[hbm]...  3.03 us
    ppermute x12, waiting for transfers between devices, swapped(): return lax.ppermute(block, axis, [(i, i ^ distance) for i in range(count)])  2.05 us
    pallas_call x1, Pallas kernels, shards(): pl.pallas_call(lambda *refs: early_kernel(here, *refs), in_specs=[vmem] *...  1.93 us
    pallas_call x1, Pallas kernels, shards(): pl.pallas_call(lambda *refs: prompt_probs_kernel(count, *refs), in_specs=...  1.38 us
    pallas_call x1, Pallas kernels, shards(): pl.pallas_call(lambda *refs: prompt_grads_kernel(count, *refs), in_specs=...  1.05 us
  transfers between devices with their start and end apart: 12, of which 3 were waited for; matrix products, arithmetic and copies ran while one was open for 1% of the time, Pallas kernels for 43%

profile of v7, /device:TPU:0, one launch (start us, length us, event | category | flops | bytes accessed | tf_op | source)
XLA Modules:
  0.0 30.2 jit_solution(1735442507119160084)
XLA Ops:
  0.6 0.9 %pad_maximum_fusion.refs_7_.refs_3_.refs_5_ = bf16[64,1024]{1,0:T(8,128)(2,1)S(1)} fusion(bf16[64,512]{1,0:T(8,128)(2,1)} %bitcast.35, bf16[64,512]{1,0:T(8,128)(2,1)} %bitcast.36), kind=kLoop, calls=%fused_computation.19 | loop fusion | flops 262144 | bytes 262144 | tf_op jit(solution)/shard_map/concatenate | solution.py:491
  1.5 4.0 %collective-permute-start.3 = (bf16[64,1024]{1,0:T(8,128)(2,1)S(1)}, bf16[64,1024]{1,0:T(8,128)(2,1)S(1)}, u32[]{:S(2)}, u32[]{:S(2)}) collective-permute-start(bf16[64,1024]{1,0:T(8,128)(2,1)S(1)} %pad_maximum_fusion.refs_7_.refs_3_.refs_5_), channel_id=1, source_target_pairs={{0,3},{1,2},{2,1},{3,0},{4,7},{5,6},{6,5},{7,4},{8,11},{9,10},{10,... | collective-permute-start | bytes 393224 | tf_op jit(solution)/shard_map/ppermute | solution.py:30
  5.5 0.5 %collective-permute-start.2 = (bf16[64,1024]{1,0:T(8,128)(2,1)S(1)}, bf16[64,1024]{1,0:T(8,128)(2,1)S(1)}, u32[]{:S(2)}, u32[]{:S(2)}) collective-permute-start(bf16[64,1024]{1,0:T(8,128)(2,1)S(1)} %pad_maximum_fusion.refs_7_.refs_3_.refs_5_), channel_id=1, source_target_pairs={{0,2},{1,3},{2,0},{3,1},{4,6},{5,7},{6,4},{7,5},{8,10},{9,11},{10,... | collective-permute-start | bytes 393224 | tf_op jit(solution)/shard_map/ppermute | solution.py:30
  6.0 0.0 collective-permute-start.1
  6.0 0.1 collective-permute-start
  6.1 0.0 copy-start
  6.1 0.0 copy-start.1
  6.1 3.0 %prepare.1 = (bf16[4,512,256]{2,1,0:T(8,128)(2,1)S(1)}, bf16[4,512,256]{2,1,0:T(8,128)(2,1)S(1)}, bf16[4,512,128]{2,1,0:T(8,128)(2,1)S(1)}, bf16[4,1024,256]{2,1...) custom-call(s32[8]{0:T(128)} %refs_0_.1, ...), custom_call_target="tpu_custom_call" | custom-call | flops 4000000000 | bytes 1048576 | tf_op jit(solution)/shard_map/prepare/pallas_call | solution.py:503
  9.2 0.0 collective-permute-done.1.refs_8_
  9.2 0.0 copy-done
  9.2 0.0 copy-done.1
  9.2 1.9 %early.1 = (bf16[4,64,128]{2,1,0:T(8,128)(2,1)S(1)}, bf16[4,64,128]{2,1,0:T(8,128)(2,1)S(1)}, f32[4,192,1024]{2,1,0:T(8,128)S(1)}, f32[4,192,1024]{2,1,0:T(8,128)S(1)}, f32[4,8,1024]{2,1,0:T(8,128)S(1)}) custom-call(bf16[4,1024,256]{2,1,0:T(8,128)(2,1)S(1)} %get-tuple-element.59.refs_0_.q_x.qr_x, bf16[4,1024,256]{2,1,0:T(8,128)(2,1)S(1)} %get-tuple-element.60.refs_1_, ...), custom_call_target="tpu_custom_call" | custom-call | flops 3000000000 | bytes 1048576 | tf_op jit(solution)/shard_map/early/pallas_call | solution.py:534
  11.1 0.0 collective-permute-done.3.refs_6_.refs_8_
  11.1 0.6 %collective-permute-done.2.refs_5_.refs_7_ = bf16[64,1024]{1,0:T(8,128)(2,1)S(1)} collective-permute-done((bf16[64,1024]{1,0:T(8,128)(2,1)S(1)}, bf16[64,1024]{1,0:T(8,128)(2,1)S(1)}, u32[]{:S(2)}, u32[]{:S(2)}) %collective-permute-start.2) | collective-permute-done | bytes 131104 | tf_op jit(solution)/shard_map/ppermute | solution.py:30
  11.8 0.3 collective-permute-done.refs_4_.refs_6_
  12.1 0.0 collective-permute-start.4
  12.1 0.5 %collective-permute-start.5 = (bf16[64,1024]{1,0:T(8,128)(2,1)S(1)}, bf16[64,1024]{1,0:T(8,128)(2,1)S(1)}, u32[]{:S(2)}, u32[]{:S(2)}) collective-permute-start(bf16[64,1024]{1,0:T(8,128)(2,1)S(1)} %collective-permute-done.2.refs_5_.refs_7_), channel_id=1, source_target_pairs={{0,4},{4,0},{8,12},{12,8},{16,20},{20,16},{24,28},{28,24},{1,5},{5... | collective-permute-start | bytes 393224 | tf_op jit(solution)/shard_map/ppermute | solution.py:30
  12.6 0.0 collective-permute-start.6
  12.6 1.4 %prompt_probs.1 = (f32[4,256,512]{2,1,0:T(8,128)S(1)}, bf16[4,256,512]{2,1,0:T(8,128)(2,1)S(1)}, bf16[4,256,128]{2,1,0:T(8,128)(2,1)S(1)}, f32[3,64,512]{2,1,0:T(8,128)S(1)}) custom-call(bf16[4,512,256]{2,1,0:T(8,128)(2,1)S(1)} %get-tuple-element.56.refs_0_.qp_x, bf16[4,512,128]{2,1,0:T(8,128)(2,1)S(1)} %get-tuple-element.57.refs_1_.gp_m, ...), custom_call_target="tpu_custom_call" | custom-call | flops 2000000000 | bytes 1048576 | tf_op jit(solution)/shard_map/prompt_probs/pallas_call | solution.py:549
  14.0 0.0 collective-permute-done.4.refs_9_
  14.0 0.0 collective-permute-done.5.refs_10_
  14.0 0.0 collective-permute-done.6.refs_11_
  14.0 3.4 %responses.1 = (bf16[4,192,1024]{2,1,0:T(8,128)(2,1)S(1)}, bf16[4,192,1024]{2,1,0:T(8,128)(2,1)S(1)}, bf16[4,192,128]{2,1,0:T(8,128)(2,1)S(1)}, bf16[4,192,128]{...) custom-call(bf16[4,1024,256]{2,1,0:T(8,128)(2,1)S(1)} %get-tuple-ele, ...), custom_call_target="tpu_custom_call" | custom-call | flops 3000000000 | bytes 1048576 | tf_op jit(solution)/shard_map/responses/pallas_call | solution.py:567
  17.4 0.6 %collective-permute-start.8 = (bf16[3,2,64,512]{3,2,1,0:T(8,128)(2,1)S(1)}, bf16[3,2,64,512]{3,2,1,0:T(8,128)(2,1)S(1)}, u32[]{:S(2)}, u32[]{:S(2)}) collective-permute-start(bf16[3,2,64,512]{3,2,1,0:T(8,128)(2,1)S(1)} %get-tuple-element.97), channel_id=1, source_target_pairs={{0,4},{4,0},{8,12},{12,8},{16,20},{20,16},{24,28},{28,24},{1,5},{5... | collective-permute-start | bytes 1179656 | tf_op jit(solution)/shard_map/ppermute | solution.py:30
  18.0 0.5 %first_piece.1 = (f32[2,64,512]{2,1,0:T(8,128)S(1)}, bf16[2,64,512]{2,1,0:T(8,128)(2,1)S(1)}) custom-call(f32[4,192,1024]{2,1,0:T(8,128)S(1)} %get-tuple-element.86.raised_a, f32[4,192,1024]{2,1,0:T(8,128)S(1)} %get-tuple-element.87.dprob_a, f32[4,8,1024]{2,1,0:T(8,128)S(1)} %get-tuple-element.88.own_t, ...), custom_call_target="tpu_custom_call" | custom-call | flops 1000000000 | bytes 1048576 | tf_op jit(solution)/shard_map/first_piece/pallas_call | solution.py:601
  18.5 0.1 collective-permute-start.7
  18.6 1.1 %prompt_grads.1 = (bf16[4,256,512]{2,1,0:T(8,128)(2,1)S(1)}, bf16[4,256,128]{2,1,0:T(8,128)(2,1)S(1)}, f32[2,64,512]{2,1,0:T(8,128)S(1)}, f32[2,64,512]{2,1,0:T(8,128)S(1)}, f32[2,64,512]{2,1,0:T(8,128)S(1)}) custom-call(bf16[4,512,256]{2,1,0:T(8,128)(2,1)S(1)} %get-tuple-element.56.refs_0_.qp_x, bf16[4,512,256]{2,1,0:T(8,128)(2,1)S(1)} %get-tuple-element.69.refs_1_, ...), custom_call_target="tpu_custom_call" | custom-call | flops 2000000000 | bytes 1048576 | tf_op jit(solution)/shard_map/prompt_grads/pallas_call | solution.py:587
  19.6 0.0 collective-permute-done.8
  19.7 0.1 fusion.2
  19.8 2.3 %collective-permute-start.9 = (bf16[2,64,512]{2,1,0:T(8,128)(2,1)S(1)}, bf16[2,64,512]{2,1,0:T(8,128)(2,1)S(1)}, u32[]{:S(2)}, u32[]{:S(2)}) collective-permute-start(bf16[2,64,512]{2,1,0:T(8,128)(2,1)S(1)} %get-tuple-element.104), channel_id=1, source_target_pairs={{0,3},{1,2},{2,1},{3,0},{4,7},{5,6},{6,5},{7,4},{8,11},{9,10},{10,... | collective-permute-start | bytes 393224 | tf_op jit(solution)/shard_map/ppermute | solution.py:30
  22.1 0.7 %collective-permute-start.11 = (bf16[2,64,512]{2,1,0:T(8,128)(2,1)S(1)}, bf16[2,64,512]{2,1,0:T(8,128)(2,1)S(1)}, u32[]{:S(2)}, u32[]{:S(2)}) collective-permute-start(bf16[2,64,512]{2,1,0:T(8,128)(2,1)S(1)} %get-tuple-element.105), channel_id=1, source_target_pairs={{0,1},{1,0},{2,3},{3,2},{4,5},{5,4},{6,7},{7,6},{8,9},{9,8},{10,11... | collective-permute-start | bytes 393224 | tf_op jit(solution)/shard_map/ppermute | solution.py:30
  22.7 0.6 %collective-permute-start.10 = (bf16[2,64,512]{2,1,0:T(8,128)(2,1)S(1)}, bf16[2,64,512]{2,1,0:T(8,128)(2,1)S(1)}, u32[]{:S(2)}, u32[]{:S(2)}) collective-permute-start(bf16[2,64,512]{2,1,0:T(8,128)(2,1)S(1)} %get-tuple-element.106), channel_id=1, source_target_pairs={{0,2},{1,3},{2,0},{3,1},{4,6},{5,7},{6,4},{7,5},{8,10},{9,11},{10,... | collective-permute-start | bytes 393224 | tf_op jit(solution)/shard_map/ppermute | solution.py:30
  23.3 4.9 %finish.1 = (bf16[64,4096]{1,0:T(8,128)(2,1)}, bf16[64,4096]{1,0:T(8,128)(2,1)}, bf16[128,4096]{1,0:T(8,128)(2,1)}, bf16[128,4096]{1,0:T(8,128)(2,1)}, bf16[128,...) custom-call(f32[8,512]{1,0:T(8,128)S(1)} %get-tuple-element.55.keep_p, ...), custom_call_target="tpu_custom_call" | custom-call | flops 8000000000 | bytes 1048576 | tf_op jit(solution)/shard_map/finish/pallas_call | solution.py:617
  28.3 0.0 collective-permute-done.7
  28.4 0.0 collective-permute-done.9
  28.4 1.1 %collective-permute-done.11 = bf16[2,64,512]{2,1,0:T(8,128)(2,1)S(1)} collective-permute-done((bf16[2,64,512]{2,1,0:T(8,128)(2,1)S(1)}, bf16[2,64,512]{2,1,0:T(8,128)(2,1)S(1)}, u32[]{:S(2)}, u32[]{:S(2)}) %collective-permute-start.11) | collective-permute-done | bytes 131104 | tf_op jit(solution)/shard_map/ppermute | solution.py:30
  29.4 0.0 collective-permute-done.10
  29.5 0.7 %fusion.6 = (bf16[1,64,512]{2,1,0:T(8,128)(2,1)}, bf16[1,64,512]{2,1,0:T(8,128)(2,1)}) fusion(f32[2,64,512]{2,1,0:T(8,128)S(1)} %add.44, bf16[2,64,512]{2,1,0:T(8,128)(2,1)S(1)} %collective-permute-done.11, bf16[2,64,512]{2,1,0:T(8,128)(2,1)S(1)} %collective-permute-done.10, bf16[2,64,512]{2,1,0:T(8,128)(2,1)S(1)} %collective-permute-done.9, ...), kind=kLoop, calls=%fused_computation.10 | loop fusion | flops 589824 | bytes 917504 | tf_op jit(solution)/shard_map/convert_element_type | solution.py:448
  (1 shorter events, 0.0 us)
Async XLA Ops:
  1.5 9.6 %collective-permute-start.3 = (bf16[64,1024]{1,0:T(8,128)(2,1)S(1)}, bf16[64,1024]{1,0:T(8,128)(2,1)S(1)}, u32[]{:S(2)}, u32[]{:S(2)}) collective-permute-start(bf16[64,1024]{1,0:T(8,128)(2,1)S(1)} %pad_maximum_fusion.refs_7_.refs_3_.refs_5_), channel_id=1, source_target_pairs={{0,3},{1,2},{2,1},{3,0},{4,7},{5,6},{6,5},{7,4},{8,11},{9,10},{10,... | collective-permute-start | bytes 393224 | tf_op jit(solution)/shard_map/ppermute | solution.py:30
  5.5 6.3 %collective-permute-start.2 = (bf16[64,1024]{1,0:T(8,128)(2,1)S(1)}, bf16[64,1024]{1,0:T(8,128)(2,1)S(1)}, u32[]{:S(2)}, u32[]{:S(2)}) collective-permute-start(bf16[64,1024]{1,0:T(8,128)(2,1)S(1)} %pad_maximum_fusion.refs_7_.refs_3_.refs_5_), channel_id=1, source_target_pairs={{0,2},{1,3},{2,0},{3,1},{4,6},{5,7},{6,4},{7,5},{8,10},{9,11},{10,... | collective-permute-start | bytes 393224 | tf_op jit(solution)/shard_map/ppermute | solution.py:30
  6.0 3.2 %collective-permute-start.1 = (bf16[64,1024]{1,0:T(8,128)(2,1)S(1)}, bf16[64,1024]{1,0:T(8,128)(2,1)S(1)}, u32[]{:S(2)}, u32[]{:S(2)}) collective-permute-start(bf16[64,1024]{1,0:T(8,128)(2,1)S(1)} %pad_maximum_fusion.refs_7_.refs_3_.refs_5_), channel_id=1, source_target_pairs={{0,4},{4,0},{8,12},{12,8},{16,20},{20,16},{24,28},{28,24},{1,5},{5... | collective-permute-start | bytes 393224 | tf_op jit(solution)/shard_map/ppermute | solution.py:30
  6.0 6.1 %collective-permute-start = (bf16[64,1024]{1,0:T(8,128)(2,1)S(1)}, bf16[64,1024]{1,0:T(8,128)(2,1)S(1)}, u32[]{:S(2)}, u32[]{:S(2)}) collective-permute-start(bf16[64,1024]{1,0:T(8,128)(2,1)S(1)} %pad_maximum_fusion.refs_7_.refs_3_.refs_5_), channel_id=1, source_target_pairs={{0,1},{1,0},{2,3},{3,2},{4,5},{5,4},{6,7},{7,6},{8,9},{9,8},{10,11... | collective-permute-start | bytes 393224 | tf_op jit(solution)/shard_map/ppermute | solution.py:30
  6.1 3.1 %copy-start = (bf16[1,128,512]{2,1,0:T(8,128)(2,1)S(1)}, bf16[1,128,512]{2,1,0:T(8,128)(2,1)}, u32[]{:S(2)}) copy-start(bf16[1,128,512]{2,1,0:T(8,128)(2,1)} %param.19) | copy-start | bytes 393220
  6.1 3.1 %copy-start.1 = (bf16[1,128,512]{2,1,0:T(8,128)(2,1)S(1)}, bf16[1,128,512]{2,1,0:T(8,128)(2,1)}, u32[]{:S(2)}) copy-start(bf16[1,128,512]{2,1,0:T(8,128)(2,1)} %param.20) | copy-start | bytes 393220
  12.1 1.9 %collective-permute-start.4 = (bf16[64,1024]{1,0:T(8,128)(2,1)S(1)}, bf16[64,1024]{1,0:T(8,128)(2,1)S(1)}, u32[]{:S(2)}, u32[]{:S(2)}) collective-permute-start(bf16[64,1024]{1,0:T(8,128)(2,1)S(1)} %collective-permute-done.refs_4_.refs_6_), channel_id=1, source_target_pairs={{0,4},{4,0},{8,12},{12,8},{16,20},{20,16},{24,28},{28,24},{1,5},{5... | collective-permute-start | bytes 393224 | tf_op jit(solution)/shard_map/ppermute | solution.py:30
  12.1 1.9 %collective-permute-start.5 = (bf16[64,1024]{1,0:T(8,128)(2,1)S(1)}, bf16[64,1024]{1,0:T(8,128)(2,1)S(1)}, u32[]{:S(2)}, u32[]{:S(2)}) collective-permute-start(bf16[64,1024]{1,0:T(8,128)(2,1)S(1)} %collective-permute-done.2.refs_5_.refs_7_), channel_id=1, source_target_pairs={{0,4},{4,0},{8,12},{12,8},{16,20},{20,16},{24,28},{28,24},{1,5},{5... | collective-permute-start | bytes 393224 | tf_op jit(solution)/shard_map/ppermute | solution.py:30
  12.6 1.4 %collective-permute-start.6 = (bf16[64,1024]{1,0:T(8,128)(2,1)S(1)}, bf16[64,1024]{1,0:T(8,128)(2,1)S(1)}, u32[]{:S(2)}, u32[]{:S(2)}) collective-permute-start(bf16[64,1024]{1,0:T(8,128)(2,1)S(1)} %collective-permute-done.3.refs_6_.refs_8_), channel_id=1, source_target_pairs={{0,4},{4,0},{8,12},{12,8},{16,20},{20,16},{24,28},{28,24},{1,5},{5... | collective-permute-start | bytes 393224 | tf_op jit(solution)/shard_map/ppermute | solution.py:30
  17.4 2.2 %collective-permute-start.8 = (bf16[3,2,64,512]{3,2,1,0:T(8,128)(2,1)S(1)}, bf16[3,2,64,512]{3,2,1,0:T(8,128)(2,1)S(1)}, u32[]{:S(2)}, u32[]{:S(2)}) collective-permute-start(bf16[3,2,64,512]{3,2,1,0:T(8,128)(2,1)S(1)} %get-tuple-element.97), channel_id=1, source_target_pairs={{0,4},{4,0},{8,12},{12,8},{16,20},{20,16},{24,28},{28,24},{1,5},{5... | collective-permute-start | bytes 1179656 | tf_op jit(solution)/shard_map/ppermute | solution.py:30
  18.5 9.8 %collective-permute-start.7 = (bf16[2,64,512]{2,1,0:T(8,128)(2,1)S(1)}, bf16[2,64,512]{2,1,0:T(8,128)(2,1)S(1)}, u32[]{:S(2)}, u32[]{:S(2)}) collective-permute-start(bf16[2,64,512]{2,1,0:T(8,128)(2,1)S(1)} %get-tuple-element.95), channel_id=1, source_target_pairs={{0,4},{4,0},{8,12},{12,8},{16,20},{20,16},{24,28},{28,24},{1,5},{5... | collective-permute-start | bytes 393224 | tf_op jit(solution)/shard_map/ppermute | solution.py:30
  19.8 8.6 %collective-permute-start.9 = (bf16[2,64,512]{2,1,0:T(8,128)(2,1)S(1)}, bf16[2,64,512]{2,1,0:T(8,128)(2,1)S(1)}, u32[]{:S(2)}, u32[]{:S(2)}) collective-permute-start(bf16[2,64,512]{2,1,0:T(8,128)(2,1)S(1)} %get-tuple-element.104), channel_id=1, source_target_pairs={{0,3},{1,2},{2,1},{3,0},{4,7},{5,6},{6,5},{7,4},{8,11},{9,10},{10,... | collective-permute-start | bytes 393224 | tf_op jit(solution)/shard_map/ppermute | solution.py:30
  22.1 7.4 %collective-permute-start.11 = (bf16[2,64,512]{2,1,0:T(8,128)(2,1)S(1)}, bf16[2,64,512]{2,1,0:T(8,128)(2,1)S(1)}, u32[]{:S(2)}, u32[]{:S(2)}) collective-permute-start(bf16[2,64,512]{2,1,0:T(8,128)(2,1)S(1)} %get-tuple-element.105), channel_id=1, source_target_pairs={{0,1},{1,0},{2,3},{3,2},{4,5},{5,4},{6,7},{7,6},{8,9},{9,8},{10,11... | collective-permute-start | bytes 393224 | tf_op jit(solution)/shard_map/ppermute | solution.py:30
  22.7 6.7 %collective-permute-start.10 = (bf16[2,64,512]{2,1,0:T(8,128)(2,1)S(1)}, bf16[2,64,512]{2,1,0:T(8,128)(2,1)S(1)}, u32[]{:S(2)}, u32[]{:S(2)}) collective-permute-start(bf16[2,64,512]{2,1,0:T(8,128)(2,1)S(1)} %get-tuple-element.106), channel_id=1, source_target_pairs={{0,2},{1,3},{2,0},{3,1},{4,6},{5,7},{6,4},{7,5},{8,10},{9,11},{10,... | collective-permute-start | bytes 393224 | tf_op jit(solution)/shard_map/ppermute | solution.py:30
